TPU v7x, 128 devices: a whole 4x4x4 slice. The times are simulated.
128 devices in a mesh: cfg: 2 (over y_lo), seq: 8 (over z, y_hi), head: 8 (over x, core).
Axes of the slice: x: 4, y: 4 (y_hi: 2, y_lo: 2; y = y_hi * 2 + y_lo), z: 4, core: 2. Of those that a mesh axis runs over, the one named last changes fastest.
Arguments:
- queries: bfloat16 [2, 6144, 5120], P('cfg', 'seq', 'head'), may hold values from -8 to 8
- keys: bfloat16 [2, 6144, 5120], P('cfg', 'seq', 'head'), may hold values from -8 to 8
- values: bfloat16 [2, 6144, 5120], P('cfg', 'seq', 'head'), may hold values from -6 to 6
- hidden_in: bfloat16 [2, 6144, 5120], P('cfg', 'seq'), may hold values from -8 to 8
- out_weight: bfloat16 [5120, 5120], P('head'), may hold values from -0.125 to 0.125
- gate: float32 [5120], replicated, may hold values from 0.1 to 1.9
- mod_scale: float32 [5120], replicated, may hold values from 0.1 to 1.9
- mod_shift: float32 [5120], replicated, may hold values from -4 to 4
- head_weight: bfloat16 [5120, 64], replicated, may hold values from -0.015625 to 0.015625
- latent: float32 [6144, 64], P('seq', 'cfg'), may hold values from -6 to 6
- history: float32 [3, 6144, 64], P(None, 'seq', 'cfg'), may hold values from -16 to 16
- step_index: int32 [1], replicated, may hold values from 3 to 49
Outputs:
- guided: float32 [6144, 64], P('seq', 'cfg')
- latent_next: float32 [6144, 64], P('seq', 'cfg')
All inputs are finite; a program needn't handle non-finite values.
Results may differ from a plain program's by a relative error of at most 0.0029.
Values may be sent and summed in bfloat16 or wider, within the bound.
No kernel may reach another device: no remote copies, remote signals or barrier semaphores. Data moves between devices by JAX's collectives and lax.ppermute only.
A program may use at most 256 MiB of HBM per device.

v0:
```python
import math

import jax
import jax.numpy as jnp
from jax import lax
from jax.sharding import PartitionSpec as P

HSIZE = 128
STEPS = 50


guide_scale = 5.0
flow_shift = 5.0
epsilon = 1e-06


def swapped(value, axis, stride):
    mask = 2**stride
    pairs = [(source, source ^ mask) for source in range(lax.axis_size(axis))]
    return lax.ppermute(value, axis, pairs)


def sigma_slope(step_number):
    moment = 1.0 - step_number.astype(jnp.float32) / STEPS
    return flow_shift / (1.0 + (flow_shift - 1.0) * moment) ** 2


def split_heads(matrix):
    return matrix.reshape(matrix.shape[0], matrix.shape[1] // HSIZE, HSIZE).transpose(1, 0, 2)


def per_device(
    queries,
    keys,
    values,
    hidden_in,
    out_weight,
    gate,
    mod_scale,
    mod_shift,
    head_weight,
    latent,
    history,
    step_index,
):
    query_rows = queries[0]
    local_tokens = query_rows.shape[0]
    local_width = query_rows.shape[1]
    query_heads = split_heads(query_rows)
    head_count = query_heads.shape[0]
    inverse_root = 1.0 / math.sqrt(HSIZE)
    running_max = jnp.full((head_count, local_tokens), -1e30, jnp.float32)
    key_heads = split_heads(lax.all_gather(keys[0], "seq", axis=0, tiled=True))
    value_heads = split_heads(lax.all_gather(values[0], "seq", axis=0, tiled=True))
    scores = (
        jnp.einsum("hqd,hkd->hqk", query_heads, key_heads, preferred_element_type=jnp.float32)
        * inverse_root
    )
    new_max = jnp.maximum(running_max, jnp.max(scores, axis=2))
    weights = jnp.exp(scores - new_max[:, :, None])
    totals = jnp.sum(weights, axis=2)
    accumulated = jnp.einsum(
        "hqk,hkd->hqd",
        weights.astype(jnp.bfloat16),
        value_heads,
        preferred_element_type=jnp.float32,
    )
    final_max, totals, accumulated = (new_max, totals, accumulated)
    attended = (
        (accumulated / totals[:, :, None])
        .astype(jnp.bfloat16)
        .transpose(1, 0, 2)
        .reshape(local_tokens, local_width)
    )
    full_width = hidden_in.shape[2]
    projected_local = jnp.dot(attended, out_weight, preferred_element_type=jnp.float32)
    mixed = lax.psum_scatter(projected_local, "head", scatter_dimension=1, tiled=True)
    column_share = mixed.shape[1]
    column_start = lax.axis_index("head") * column_share
    residual = (
        lax.dynamic_slice_in_dim(hidden_in[0], column_start, column_share, 1).astype(jnp.float32)
        + lax.dynamic_slice_in_dim(gate, column_start, column_share, 0) * mixed
    )
    scale_part = lax.dynamic_slice_in_dim(mod_scale, column_start, column_share, 0)
    shift_part = lax.dynamic_slice_in_dim(mod_shift, column_start, column_share, 0)
    weight_part = lax.dynamic_slice_in_dim(head_weight, column_start, column_share, 0).astype(
        jnp.float32
    )
    sum_plain, sum_square = lax.psum(
        (jnp.sum(residual, axis=1), jnp.sum(residual * residual, axis=1)), "head"
    )
    center = sum_plain / full_width
    inverse = lax.rsqrt(sum_square / full_width - center * center + epsilon)
    normed = (residual - center[:, None]) * inverse[:, None] * scale_part + shift_part
    velocity = lax.psum(jnp.dot(normed, weight_part, precision=lax.Precision.HIGHEST), "head")
    channel_share = velocity.shape[1] // lax.axis_size("cfg")
    branch_index = lax.axis_index("cfg")
    outgoing = lax.dynamic_slice_in_dim(
        velocity, (1 - branch_index) * channel_share, channel_share, 1
    )
    partner_velocity = swapped(outgoing, "cfg", 0)
    own_velocity = lax.dynamic_slice_in_dim(
        velocity, branch_index * channel_share, channel_share, 1
    )
    holds_conditioned = branch_index == 0
    conditioned = jnp.where(holds_conditioned, own_velocity, partner_velocity)
    unconditioned = jnp.where(holds_conditioned, partner_velocity, own_velocity)
    guided = unconditioned + guide_scale * (conditioned - unconditioned)
    current_step = step_index[0]
    slopes = [sigma_slope(current_step - behind) for behind in range(4)]
    combined = (
        55.0 * slopes[0] * guided
        - 59.0 * slopes[1] * history[0]
        + 37.0 * slopes[2] * history[1]
        - 9.0 * slopes[3] * history[2]
    ) / 24.0
    advanced = latent - combined / STEPS
    return (guided, advanced)


def solution(mesh):
    placed = (
        P("cfg", "seq", "head"),
        P("cfg", "seq", "head"),
        P("cfg", "seq", "head"),
        P("cfg", "seq", None),
        P("head", None),
        P(),
        P(),
        P(),
        P(),
        P("seq", "cfg"),
        P(None, "seq", "cfg"),
        P(),
    )
    return jax.shard_map(
        per_device,
        mesh=mesh,
        in_specs=placed,
        out_specs=(P("seq", "cfg"), P("seq", "cfg")),
        check_vma=False,
    )
```

profile of v0, /device:TPU:0, one launch (start us, length us, event | category | flops | bytes accessed | tf_op | source)
XLA Modules:
  0.0 451.4 jit_solution(4356036031524588647)
XLA Ops:
  7.2 2.4 copy.17
  9.7 0.7 all-gather.7.cloned.1.call-update
  10.5 1.6 copy.16
  12.1 102.9 %all-gather.5.cloned.1.call-done = bf16[1,6144,640]{1,2,0:T(8,128)(2,1)} async-done(((bf16[1,768,640]{1,2,0:T(8,128)(2,1)}), bf16[1,6144,640]{1,2,0:T(8,128)(2,1)}) %all-gather.5.cloned.1.call-update) | async-done | bytes 7864336 | tf_op jit(solution)/shard_map/all_gather | solution.py:53
  115.0 10.7 %copy.18 = bf16[6144,5,128]{2,0,1:T(8,128)(2,1)} copy(bf16[6144,5,128]{0,2,1:T(8,128)(2,1)} %bitcast.52) | data formatting | bytes 15728640 | tf_op jit(solution)/shard_map/reshape | solution.py:29
  125.7 36.1 %multiply_reduce_fusion = (f32[5,768]{1,0:T(8,128)S(1)}, f32[5,768,6144]{2,1,0:T(8,128)}) fusion(bf16[5,768,128]{1,2,0:T(8,128)(2,1)S(1)} %bitcast.53, bf16[6144,5,128]{2,0,1:T(8,128)(2,1)} %copy.18), kind=kOutput, calls=%fused_computation.1 | convolution fusion | flops 6086979584 | bytes 103234560 | tf_op jit(solution)/shard_map/hqd,hkd->hqk/dot_general | solution.py:56
  161.8 29.3 %fusion = f32[5,768]{1,0:T(8,128)S(1)} fusion(f32[5,768,6144]{2,1,0:T(8,128)} %get-tuple-element.11, f32[5,768]{1,0:T(8,128)S(1)} %broadcast_maximum_fusion), kind=kLoop, calls=%fused_computation.2 | loop fusion | flops 70775040 | bytes 94402560 | tf_op jit(solution)/shard_map/reduce_sum | solution.py:61
  191.1 26.5 %all-gather.7.cloned.1.call-done = bf16[1,6144,640]{2,1,0:T(8,128)(2,1)} async-done(((bf16[1,768,640]{2,1,0:T(8,128)(2,1)}), bf16[1,6144,640]{2,1,0:T(8,128)(2,1)}) %all-gather.7.cloned.1.call-update) | async-done | bytes 7864336 | tf_op jit(solution)/shard_map/all_gather | solution.py:54
  217.6 10.6 %copy.20 = bf16[1,6144,640]{1,2,0:T(8,128)(2,1)} copy(bf16[1,6144,640]{2,1,0:T(8,128)(2,1)} %all-gather.7.cloned.1.call-done) | data formatting | bytes 15728640 | tf_op jit(solution)/shard_map/all_gather | solution.py:54
  228.2 34.2 %fusion.6 = bf16[768,5,128]{0,2,1:T(8,128)(2,1)S(1)} fusion(bf16[5,6144,128]{1,2,0:T(8,128)(2,1)} %bitcast.50, f32[5,768,6144]{2,1,0:T(8,128)} %get-tuple-element.11, f32[5,768]{1,0:T(8,128)S(1)} %broadcast_maximum_fusion, f32[768,5]{0,1:T(8,128)S(1)} %bitcast.54), kind=kOutput, calls=%fused_computation.9 | convolution fusion | flops 6111559680 | bytes 103249920 | tf_op jit(solution)/shard_map/hqk,hkd->hqd/dot_general | solution.py:62
  262.4 12.0 %fusion.24 = f32[768,5120]{1,0:T(8,128)} fusion(bf16[768,640]{0,1:T(8,128)(2,1)S(1)} %bitcast.51, bf16[640,5120]{1,0:T(8,128)(2,1)} %param.16), kind=kOutput, calls=%fused_computation.34 | convolution fusion | flops 5033164800 | bytes 23265280 | tf_op jit(solution)/shard_map/dot_general | solution.py:76
  274.5 0.0 all-reduce.3.cloned.1.call-start
  274.6 0.8 dynamic_slice.22
  275.4 0.8 dynamic_slice.23
  276.1 0.8 dynamic_slice.24
  276.9 82.8 %reduce-scatter.2.cloned.1.call-done = f32[768,640]{1,0:T(8,128)} async-done(((f32[768,5120]{1,0:T(8,128)}), f32[768,640]{1,0:T(8,128)}) %reduce-scatter.2.cloned.1.call-update) | async-done | bytes 1966096 | tf_op jit(solution)/shard_map/reduce_scatter | solution.py:77
  359.7 2.3 fusion.18
  362.0 12.9 %all-reduce = (f32[768]{0:T(1024)S(1)}, f32[768]{0:T(1024)S(1)}) all-reduce(f32[768]{0:T(1024)S(1)} %get-tuple-element.3, f32[768]{0:T(1024)S(1)} %get-tuple-element.2), channel_id=1, replica_groups=mesh['cfg'=2,'seq'=8,'head'=8] {'head'}, use_global_device_ids=true, to_apply=%region_6.0 | all-reduce | flops 1536 | bytes 12288 | tf_op jit(solution)/shard_map/psum | solution.py:89
  374.9 4.1 fusion.7
  379.0 58.7 %all-reduce.3.cloned.1.call-done = f32[768,64]{0,1:T(8,128)} async-done(((f32[768,64]{0,1:T(8,128)}), f32[768,64]{0,1:T(8,128)}) %all-reduce.3.cloned.1.call-update) | async-done | bytes 196624 | tf_op jit(solution)/shard_map/psum | solution.py:95
  437.7 0.9 constant_dynamic-slice_fusion
  438.6 1.5 collective-permute-start
  441.0 2.3 collective-permute-done
  443.3 1.6 fusion.20
  (14 shorter events, 0.2 us)
Async XLA Ops:
  7.2 367.7 %copy-start = (bf16[5120,64]{0,1:T(8,128)(2,1)S(1)}, bf16[5120,64]{0,1:T(8,128)(2,1)}, u32[]{:S(2)}) copy-start(bf16[5120,64]{0,1:T(8,128)(2,1)} %param.20) | copy-start | bytes 1966084
  7.2 107.8 %all-gather.5.cloned.1.call-start = ((), (), s32[]{:S(2)}) async-start(), calls=%async_computation.3 | async-start | bytes 8847360 | tf_op jit(solution)/shard_map/all_gather | solution.py:53
  9.7 207.9 %all-gather.7.cloned.1.call-start = ((), (), s32[]{:S(2)}) async-start(), calls=%async_computation.4 | async-start | bytes 8847360 | tf_op jit(solution)/shard_map/all_gather | solution.py:54
  10.4 349.2 %reduce-scatter.2.cloned.1.call-start = ((), (), s32[]{:S(2)}) async-start(), calls=%async_computation.1 | async-start | bytes 17694720 | tf_op jit(solution)/shard_map/reduce_scatter | solution.py:77
  274.5 168.8 %copy-start.1 = (f32[3,768,32]{1,2,0:T(8,128)S(1)}, f32[3,768,32]{1,2,0:T(8,128)}, u32[]{:S(2)}) copy-start(f32[3,768,32]{1,2,0:T(8,128)} %param.22) | copy-start | bytes 884740
  274.5 168.8 %copy-start.2 = (f32[768,32]{0,1:T(8,128)S(1)}, f32[768,32]{0,1:T(8,128)}, u32[]{:S(2)}) copy-start(f32[768,32]{0,1:T(8,128)} %param.21) | copy-start | bytes 294916
  274.5 163.2 %all-reduce.3.cloned.1.call-start = ((), (), s32[]{:S(2)}) async-start(), calls=%async_computation.2 | async-start | bytes 393216 | tf_op jit(solution)/shard_map/psum | solution.py:95
  438.6 4.6 %collective-permute-start = (f32[768,32]{0,1:T(8,128)S(1)}, f32[768,32]{0,1:T(8,128)S(1)}, u32[]{:S(2)}, u32[]{:S(2)}) collective-permute-start(f32[768,32]{0,1:T(8,128)S(1)} %constant_dynamic-slice_fusion), channel_id=1, source_target_pairs={{0,64},{64,0},{1,65},{65,1},{2,66},{66,2},{3,67},{67,3},{4,68},{68... | collective-permute-start | bytes 294920 | tf_op jit(solution)/shard_map/ppermute | solution.py:20
Sparse Core Ops, SparseCore 0:
  10.4 104.5 all-gather.4
  117.3 100.2 all-gather.6
  274.6 85.0 reduce-scatter.1
  379.1 58.5 all-reduce.2
where the time goes:
time: 452 us; the launch traced here: 451 us
  waiting for transfers between devices  274 us (61%)
  matrix products  86.4 us (19%)
  other arithmetic  33.2 us (7%)
  local copies, waits for them, and re-layouts  28.6 us (6%)
  between operations  14.7 us (3%)
  blocking collectives  12.9 us (3%)
    all_gather x1, waiting for transfers between devices, per_device(): key_heads = split_heads(lax.all_gather(keys[0], 'seq', axis=0, tiled=True))  103 us
    reduce_scatter x1, waiting for transfers between devices, per_device(): lax.psum_scatter(projected_local, 'head', scatter_dimension=1, tiled=True)  82.8 us
    psum x1, waiting for transfers between devices, per_device(): lax.psum(jnp.dot(normed, weight_part, precision=lax.Precision.HIGHEST), '...  58.7 us
    dot_general x1, matrix products, per_device(): jnp.einsum('hqd,hkd->hqk', query_heads, key_heads, preferred_element_type...  36.1 us
    dot_general x1, matrix products, per_device(): jnp.einsum('hqk,hkd->hqd', weights.astype(jnp.bfloat16), value_heads, pre...  34.2 us
    reduce_sum x1, other arithmetic, per_device(): totals = jnp.sum(weights, axis=2)  29.3 us
    all_gather x1, waiting for transfers between devices, per_device(): lax.all_gather(values[0], 'seq', axis=0, tiled=True)  26.5 us
    psum x1, blocking collectives, per_device(): lax.psum((jnp.sum(residual, axis=1), jnp.sum(residual * residual, axis=1)...  12.9 us
  transfers between devices with their start and end apart: 5, of which 5 were waited for; matrix products, arithmetic and copies ran while one was open for 18% of the time, Pallas kernels for 0%

commit v1 on v0

v1 whole, which is shorter than its diff:
```python
import functools
import math

import jax
import jax.numpy as jnp
from jax import lax
from jax.experimental import pallas as pl
from jax.experimental.pallas import tpu as pltpu
from jax.sharding import PartitionSpec as P

HSIZE = 128
STEPS = 50

guide_scale = 5.0
flow_shift = 5.0
epsilon = 1e-06

Z, YH, X, CORE = 4, 2, 4, 2
SEQ, HEAD = Z * YH, X * CORE

z_groups = [[z * YH + y for z in range(Z)] for y in range(YH)]
y_swap = [(s, s ^ 1) for s in range(SEQ)]
core_swap = [(h, h ^ 1) for h in range(HEAD)]
cfg_swap = [(0, 1), (1, 0)]
transposition = [(s * HEAD + h, h * HEAD + s) for s in range(SEQ) for h in range(HEAD)]


def x_shift(step):
    return [(x * CORE + c, (x + step) % X * CORE + c) for x in range(X) for c in range(CORE)]


def sigma_slope(step_number):
    moment = 1.0 - step_number.astype(jnp.float32) / STEPS
    return flow_shift / (1.0 + (flow_shift - 1.0) * moment) ** 2


def attend_body(query_ref, *refs, parts, part, chunk):
    key_refs, value_refs = refs[:parts], refs[parts : 2 * parts]
    out_ref, keys_t, values_one = refs[2 * parts :]
    tokens = parts * part

    @pl.when(pl.program_id(0) == 0)
    def _():
        step = 384
        for index in range(parts):
            for at in range(0, part, step):
                block = key_refs[index][at : at + step, :].astype(jnp.float32)
                block = block.T.astype(jnp.bfloat16)
                start = index * part + at
                keys_t[:HSIZE, start : start + step] = block
                keys_t[HSIZE:, start : start + step] = block
            rows = slice(index * part, (index + 1) * part)
            values_one[rows, :HSIZE] = value_refs[index][...]
            values_one[rows, HSIZE:] = jnp.ones((part, HSIZE), jnp.bfloat16)

    scaled = query_ref[...].astype(jnp.float32) * (math.log2(math.e) / math.sqrt(HSIZE))
    upper = scaled.astype(jnp.bfloat16)
    lower = (scaled - upper.astype(jnp.float32)).astype(jnp.bfloat16)
    queries = jnp.concatenate([upper, lower], axis=1)

    def score(at):
        return jnp.dot(queries, keys_t[:, at : at + chunk], preferred_element_type=jnp.float32)

    peak, total = None, None
    scores = score(0)
    for at in range(0, tokens, chunk):
        following = score(at + chunk) if at + chunk < tokens else None
        new_peak = jnp.max(scores, axis=1, keepdims=True)
        if peak is not None:
            new_peak = jnp.maximum(peak, new_peak)
        weights = jnp.exp2(scores - new_peak).astype(jnp.bfloat16)
        summed = jnp.dot(
            weights, values_one[at : at + chunk, :], preferred_element_type=jnp.float32
        )
        total = summed if peak is None else total * jnp.exp2(peak - new_peak) + summed
        peak, scores = new_peak, following
    out_ref[...] = (total[:, :HSIZE] / total[:, HSIZE:]).astype(jnp.bfloat16)


def attend(queries, keys, values, rows, chunk):
    parts, part = len(keys), keys[0].shape[0]
    tokens = parts * part
    whole = pl.BlockSpec((part, HSIZE), lambda i: (0, 0))
    tile = pl.BlockSpec((rows, HSIZE), lambda i: (i, 0))
    return pl.pallas_call(
        functools.partial(attend_body, parts=parts, part=part, chunk=chunk),
        grid=(queries.shape[0] // rows,),
        in_specs=[tile] + [whole] * (2 * parts),
        out_specs=tile,
        out_shape=jax.ShapeDtypeStruct(queries.shape, jnp.bfloat16),
        scratch_shapes=[
            pltpu.VMEM((2 * HSIZE, tokens), jnp.bfloat16),
            pltpu.VMEM((tokens, 2 * HSIZE), jnp.bfloat16),
        ],
        compiler_params=pltpu.CompilerParams(vmem_limit_bytes=52 * 2**20),
        cost_estimate=pl.CostEstimate(
            flops=8 * queries.shape[0] * tokens * HSIZE,
            bytes_accessed=4 * HSIZE * (queries.shape[0] + tokens),
            transcendentals=queries.shape[0] * tokens,
        ),
    )(queries, *keys, *values)


def per_device(
    queries,
    keys,
    values,
    hidden_in,
    out_weight,
    gate,
    mod_scale,
    mod_shift,
    head_weight,
    latent,
    history,
    step_index,
):
    queries, keys, values, hidden = queries[0], keys[0], values[0], hidden_in[0]
    local_tokens, local_width = queries.shape
    full_width = hidden.shape[1]
    spread = Z * HSIZE
    core = lax.axis_index("head") % CORE
    column = lax.axis_index("head") // CORE
    branch = lax.axis_index("cfg")

    last = jnp.stack([keys[:, spread:], values[:, spread:], queries[:, spread:]])
    last = lax.ppermute(last, ("seq", "head"), transposition)
    last_gathered = lax.all_gather(last[:2], "head", axis=1, tiled=True)

    half = full_width // CORE
    own_weight = lax.dynamic_slice_in_dim(out_weight, core * half, half, 1)
    other_weight = lax.ppermute(
        lax.dynamic_slice_in_dim(out_weight, (1 - core) * half, half, 1), "head", core_swap
    )

    def deal(value):
        return lax.all_to_all(
            value[:, :spread], "seq", 1, 0, tiled=True, axis_index_groups=z_groups
        )

    own_keys = deal(keys)
    partner_keys = lax.ppermute(own_keys, "seq", y_swap)
    own_values = deal(values)
    partner_values = lax.ppermute(own_values, "seq", y_swap)
    dealt_queries = deal(queries)
    dealt = attend(
        dealt_queries, [own_keys, partner_keys], [own_values, partner_values], 768, 3072
    )
    last_out = attend(last[2], [last_gathered[0]], [last_gathered[1]], 768, 3072)
    returned = lax.all_to_all(dealt, "seq", 0, 1, tiled=True, axis_index_groups=z_groups)
    last_out = lax.ppermute(last_out, ("seq", "head"), transposition)
    attended = jnp.concatenate([returned, last_out], axis=1)

    other_attended = lax.ppermute(attended, "head", core_swap)
    partial = jnp.dot(attended, own_weight, preferred_element_type=jnp.float32) + jnp.dot(
        other_attended, other_weight, preferred_element_type=jnp.float32
    )

    share = local_tokens // X

    def quarter(step):
        return lax.dynamic_slice_in_dim(partial, (column + step) % X * share, share, 0)

    summed = quarter(0)
    for step in (1, 3, 2):
        arrived = lax.ppermute(quarter(step).astype(jnp.bfloat16), "head", x_shift(step))
        summed = summed + arrived.astype(jnp.float32)

    my_hidden = lax.dynamic_slice(hidden, (column * share, core * half), (share, half))

    def my_half(vector):
        return lax.dynamic_slice_in_dim(vector, core * half, half, 0)

    residual = my_hidden.astype(jnp.float32) + my_half(gate) * summed
    scaled_weight = my_half(head_weight).astype(jnp.float32)
    scale_part, shift_part = my_half(mod_scale), my_half(mod_shift)
    sums = jnp.stack([jnp.sum(residual, axis=1), jnp.sum(residual * residual, axis=1)], axis=1)
    other_sums = lax.ppermute(sums, "head", core_swap)
    sums = (sums + other_sums) / full_width
    center = sums[:, :1]
    inverse = lax.rsqrt(sums[:, 1:] - center * center + epsilon)
    normed = (residual - center) * inverse * scale_part + shift_part
    velocity = jnp.dot(normed, scaled_weight, precision=lax.Precision.HIGHEST)
    velocity = velocity + lax.ppermute(velocity, "head", core_swap)

    channels = velocity.shape[1] // 2
    outgoing = lax.dynamic_slice_in_dim(velocity, (1 - branch) * channels, channels, 1)
    partner_velocity = lax.ppermute(outgoing, "cfg", cfg_swap)
    own_velocity = lax.dynamic_slice_in_dim(velocity, branch * channels, channels, 1)
    conditioned = jnp.where(branch == 0, own_velocity, partner_velocity)
    unconditioned = jnp.where(branch == 0, partner_velocity, own_velocity)
    guided = unconditioned + guide_scale * (conditioned - unconditioned)
    x_groups = [[x * CORE + c for x in range(X)] for c in range(CORE)]
    guided = lax.all_to_all(
        jnp.broadcast_to(guided[None], (X, share, channels)),
        "head",
        0,
        0,
        tiled=True,
        axis_index_groups=x_groups,
    ).reshape(local_tokens, channels)

    current_step = step_index[0]
    slopes = [sigma_slope(current_step - behind) for behind in range(4)]
    combined = (
        55.0 * slopes[0] * guided
        - 59.0 * slopes[1] * history[0]
        + 37.0 * slopes[2] * history[1]
        - 9.0 * slopes[3] * history[2]
    ) / 24.0
    advanced = latent - combined / STEPS
    return (guided, advanced)


def solution(mesh):
    placed = (
        P("cfg", "seq", "head"),
        P("cfg", "seq", "head"),
        P("cfg", "seq", "head"),
        P("cfg", "seq", None),
        P("head", None),
        P(),
        P(),
        P(),
        P(),
        P("seq", "cfg"),
        P(None, "seq", "cfg"),
        P(),
    )
    return jax.shard_map(
        per_device,
        mesh=mesh,
        in_specs=placed,
        out_specs=(P("seq", "cfg"), P("seq", "cfg")),
        check_vma=False,
    )
```

time: 452 us -> 264 us (0.58)
  waiting for transfers between devices: 274 us -> 93.9 us
  starting transfers between devices: 1.64 us -> 82.5 us
  matrix products: 86.4 us -> 11.9 us
  Pallas kernels: 0 us -> 30.5 us
  other arithmetic: 33.2 us -> 5.34 us
  blocking collectives: 12.9 us -> 0 us
  local copies, waits for them, and re-layouts: 28.6 us -> 22.6 us
    all_gather x2 -> x1, waiting for transfers between devices: 129 us -> 0.01 us  [per_device(): last_gathered = lax.all_gather(last[:2], 'head', axis=1, tiled=True)]
    reduce_scatter x1 -> x0, waiting for transfers between devices: 82.8 us -> none  [per_device(): lax.psum_scatter(projected_local, 'head', scatter_dimension=1, tiled=True)]
    dot_general x4 -> x3, matrix products: 86.4 us -> 11.9 us  [the longest x1 5.2 us: per_device(): jnp.dot(attended, own_weight, preferred_element_type=jnp.float32)]
    all_to_all x0 -> x5, starting transfers between devices: none -> 59.4 us  [the longest x3 51.7 us: deal(): lax.all_to_all(value[:, :spread], 'seq', 1, 0, tiled=True, axis_index_gro...]
    psum x1 -> x0, waiting for transfers between devices: 58.7 us -> none  [per_device(): lax.psum(jnp.dot(normed, weight_part, precision=lax.Precision.HIGHEST), '...]
    ppermute x1 -> x12, waiting for transfers between devices: 2.29 us -> 58.4 us  [the longest x3 43.1 us: per_device(): lax.ppermute(quarter(step).astype(jnp.bfloat16), 'head', x_shift(step))]
    all_to_all x0 -> x5, waiting for transfers between devices: none -> 35.4 us  [the longest x3 30.3 us: deal(): lax.all_to_all(value[:, :spread], 'seq', 1, 0, tiled=True, axis_index_gro...]
    pallas_call x0 -> x2, Pallas kernels: none -> 30.5 us  [attend(): pl.pallas_call(functools.partial(attend_body, parts=parts, part=part, chu...]
  transfers between devices with their start and end apart: 5 -> 18, of which waited for: 5 -> 12; matrix products, arithmetic and copies ran while one was open for 18% -> 5% of each run, Pallas kernels for 0% -> 12%
where the time goes in v1:
time: 264 us; the launch traced here: 262 us
  waiting for transfers between devices  93.9 us (36%)
  starting transfers between devices  82.5 us (31%)
  Pallas kernels  30.5 us (12%)
  local copies, waits for them, and re-layouts  22.6 us (9%)
  between operations  15.2 us (6%)
  matrix products  11.9 us (5%)
  other arithmetic  5.34 us (2%)
    all_to_all x3, starting transfers between devices, deal(): lax.all_to_all(value[:, :spread], 'seq', 1, 0, tiled=True, axis_index_gro...  51.7 us
    ppermute x3, waiting for transfers between devices, per_device(): lax.ppermute(quarter(step).astype(jnp.bfloat16), 'head', x_shift(step))  43.1 us
    pallas_call x2, Pallas kernels, attend(): pl.pallas_call(functools.partial(attend_body, parts=parts, part=part, chu...  30.5 us
    all_to_all x3, waiting for transfers between devices, deal(): lax.all_to_all(value[:, :spread], 'seq', 1, 0, tiled=True, axis_index_gro...  30.3 us
    ppermute x3, starting transfers between devices, per_device(): lax.ppermute(quarter(step).astype(jnp.bfloat16), 'head', x_shift(step))  11.9 us
    ppermute x1, waiting for transfers between devices, per_device(): partner_values = lax.ppermute(own_values, 'seq', y_swap)  9.04 us
    ppermute x1, starting transfers between devices, per_device(): other_attended = lax.ppermute(attended, 'head', core_swap)  6.01 us
  transfers between devices with their start and end apart: 18, of which 12 were waited for; matrix products, arithmetic and copies ran while one was open for 5% of the time, Pallas kernels for 12%

profile of v1, /device:TPU:0, one launch (start us, length us, event | category | flops | bytes accessed | tf_op | source)
XLA Modules:
  0.0 261.9 jit_solution(14185178726951453934)
XLA Ops:
  13.7 44.7 %all-to-all-start.1 = ((bf16[768,4,128]{2,0,1:T(8,128)(2,1)}), bf16[768,4,128]{2,0,1:T(8,128)(2,1)S(1)}, u32[]{:S(2)}, u32[]{:S(2)}) async-start(bf16[768,4,128]{2,0,1:T(8,128)(2,1)} %copy_bitcast_fusion.1), calls=%async_computation.1 | async-start | bytes 1572864 | tf_op jit(solution)/shard_map/all_to_all | solution.py:137
  59.4 12.2 %all-to-all-done.1 = bf16[768,4,128]{2,0,1:T(8,128)(2,1)S(1)} async-done(((bf16[768,4,128]{2,0,1:T(8,128)(2,1)}), bf16[768,4,128]{2,0,1:T(8,128)(2,1)S(1)}, u32[]{:S(2)}, u32[]{:S(2)}) %all-to-all-start.1) | async-done | bytes 786464 | tf_op jit(solution)/shard_map/all_to_all | solution.py:137
  71.5 3.5 %all-to-all-start.2 = ((bf16[768,4,128]{2,0,1:T(8,128)(2,1)}), bf16[768,4,128]{2,0,1:T(8,128)(2,1)S(1)}, u32[]{:S(2)}, u32[]{:S(2)}) async-start(bf16[768,4,128]{2,0,1:T(8,128)(2,1)} %copy_bitcast_fusion), calls=%async_computation.2 | async-start | bytes 1572864 | tf_op jit(solution)/shard_map/all_to_all | solution.py:137
  76.0 11.4 %all-to-all-done.2 = bf16[768,4,128]{2,0,1:T(8,128)(2,1)S(1)} async-done(((bf16[768,4,128]{2,0,1:T(8,128)(2,1)}), bf16[768,4,128]{2,0,1:T(8,128)(2,1)S(1)}, u32[]{:S(2)}, u32[]{:S(2)}) %all-to-all-start.2) | async-done | bytes 786464 | tf_op jit(solution)/shard_map/all_to_all | solution.py:137
  88.6 3.5 %all-to-all-start = ((bf16[768,4,128]{2,0,1:T(8,128)(2,1)}), bf16[768,4,128]{2,0,1:T(8,128)(2,1)S(1)}, u32[]{:S(2)}, u32[]{:S(2)}) async-start(bf16[768,4,128]{2,0,1:T(8,128)(2,1)} %copy_bitcast_fusion.2), calls=%async_computation | async-start | bytes 1572864 | tf_op jit(solution)/shard_map/all_to_all | solution.py:137
  92.1 3.9 %constant_dynamic-slice_fusion.1 = bf16[640,2560]{1,0:T(8,128)(2,1)} fusion(bf16[640,5120]{1,0:T(8,128)(2,1)} %param.16, s32[]{:T(128)S(6)} %select_n.76), kind=kLoop, calls=%fused_computation.39 | loop fusion | bytes 6553604 | tf_op jit(solution)/shard_map/dynamic_slice | solution.py:133
  96.9 6.8 %all-to-all-done = bf16[768,4,128]{2,0,1:T(8,128)(2,1)S(1)} async-done(((bf16[768,4,128]{2,0,1:T(8,128)(2,1)}), bf16[768,4,128]{2,0,1:T(8,128)(2,1)S(1)}, u32[]{:S(2)}, u32[]{:S(2)}) %all-to-all-start) | async-done | bytes 786464 | tf_op jit(solution)/shard_map/all_to_all | solution.py:137
  103.7 9.0 %collective-permute-done.1.refs_3_ = bf16[3072,128]{1,0:T(8,128)(2,1)} collective-permute-done((bf16[3072,128]{1,0:T(8,128)(2,1)S(1)}, bf16[3072,128]{1,0:T(8,128)(2,1)}, u32[]{:S(2)}, u32[]{:S(2)}) %collective-permute-start.1) | collective-permute-done | bytes 786464 | tf_op jit(solution)/shard_map/ppermute | solution.py:144
  112.7 23.3 %shard_map.131 = bf16[3072,128]{1,0:T(8,128)(2,1)S(1)} custom-call(bf16[3072,128]{1,0:T(8,128)(2,1)S(1)} %bitcast.73, bf16[3072,128]{1,0:T(8,128)(2,1)} %bitcast.84, bf16[3072,128]{1,0:T(8,128)(2,1)} %collective-permute-done.refs_1_, bf16[3072,128]{1,0:T(8,128)(2,1)} %bitcast.86, bf16[3072,128]{1,0:T(8,128)(2,1)} %collective-permute-done.1.refs_3_), custom_call_target="tpu_custom_call" | custom-call | flops 19327352832 | bytes 4718592 | tf_op jit(solution)/shard_map/pallas_call | solution.py:85
  137.2 4.4 %all-to-all-start.3 = ((bf16[4,768,128]{1,2,0:T(8,128)(2,1)}), bf16[4,768,128]{1,2,0:T(8,128)(2,1)S(1)}, u32[]{:S(2)}, u32[]{:S(2)}) async-start(bf16[4,768,128]{1,2,0:T(8,128)(2,1)} %copy.30), calls=%async_computation.3 | async-start | bytes 1572864 | tf_op jit(solution)/shard_map/all_to_all | solution.py:150
  141.6 3.2 %slice_bitcast_fusion = (bf16[6144,128]{1,0:T(8,128)(2,1)}, bf16[6144,128]{1,0:T(8,128)(2,1)S(1)}) fusion(bf16[2,6144,128]{2,1,0:T(8,128)(2,1)} %all-gather.2.cloned.1.call-done), kind=kLoop, calls=%fused_computation.12 | loop fusion | bytes 6291456 | tf_op jit(solution)/shard_map/squeeze | solution.py:149
  144.8 7.2 %shard_map.132 = bf16[768,128]{1,0:T(8,128)(2,1)S(1)} custom-call(bf16[768,128]{1,0:T(8,128)(2,1)S(1)} %slice_bitcast_fusion.5.query_ref, bf16[6144,128]{1,0:T(8,128)(2,1)S(1)} %get-tuple-element.9.refs_0_, bf16[6144,128]{1,0:T(8,128)(2,1)} %get-tuple-element.8.refs_1_), custom_call_target="tpu_custom_call" | custom-call | flops 4831838208 | bytes 3538944 | tf_op jit(solution)/shard_map/pallas_call | solution.py:85
  153.9 6.0 %collective-permute-start.4 = (bf16[768,640]{0,1:T(8,128)(2,1)}, bf16[768,640]{0,1:T(8,128)(2,1)S(1)}, u32[]{:S(2)}, u32[]{:S(2)}) collective-permute-start(bf16[768,640]{0,1:T(8,128)(2,1)} %pad_maximum_fusion), channel_id=1, source_target_pairs={{0,1},{1,0},{2,3},{3,2},{4,5},{5,4},{6,7},{7,6},{8,9},{9,8},{10,11... | collective-permute-start | bytes 2949128 | tf_op jit(solution)/shard_map/ppermute | solution.py:154
  162.3 5.2 %fusion.19 = f32[768,2560]{1,0:T(8,128)S(1)} fusion(bf16[768,640]{0,1:T(8,128)(2,1)S(1)} %collective-permute-done.4, bf16[640,2560]{1,0:T(8,128)(2,1)} %collective-permute-done.5), kind=kOutput, calls=%fused_computation.48 | convolution fusion | flops 2516582400 | bytes 12124160 | tf_op jit(solution)/shard_map/dot_general | solution.py:155
  167.5 5.2 %convolution_add_fusion = f32[768,2560]{1,0:T(8,128)S(1)} fusion(f32[768,2560]{1,0:T(8,128)S(1)} %fusion.19, bf16[640,5120]{1,0:T(8,128)(2,1)} %param.16, s32[]{:T(128)S(6)} %select_n.75, bf16[768,128]{0,1:T(8,128)(2,1)S(1)} %copy.31, bf16[768,512]{0,1:T(8,128)(2,1)S(1)} %bitcast.76), kind=kOutput, calls=%fused_computation | convolution fusion | flops 2520514560 | bytes 19988484 | tf_op jit(solution)/shard_map/dot_general | solution.py:155
  172.7 3.1 %copy-done.1 = f32[768,2560]{1,0:T(8,128)} copy-done((f32[768,2560]{1,0:T(8,128)}, f32[768,2560]{1,0:T(8,128)S(1)}, u32[]{:S(2)}) %copy-start.1) | copy-done | bytes 7864344
  177.0 6.9 %collective-permute-start.6 = (bf16[192,2560]{1,0:T(8,128)(2,1)}, bf16[192,2560]{1,0:T(8,128)(2,1)}, u32[]{:S(2)}, u32[]{:S(2)}) collective-permute-start(bf16[192,2560]{1,0:T(8,128)(2,1)} %get-tuple-element.5), channel_id=1, source_target_pairs={{0,2},{1,3},{2,4},{3,5},{4,6},{5,7},{6,0},{7,1},{8,10},{9,11},{10,... | collective-permute-start | bytes 2949128 | tf_op jit(solution)/shard_map/ppermute | solution.py:166
  183.9 3.6 %collective-permute-start.7 = (bf16[192,2560]{1,0:T(8,128)(2,1)S(1)}, bf16[192,2560]{1,0:T(8,128)(2,1)}, u32[]{:S(2)}, u32[]{:S(2)}) collective-permute-start(bf16[192,2560]{1,0:T(8,128)(2,1)S(1)} %get-tuple-element.7), channel_id=1, source_target_pairs={{0,6},{1,7},{2,0},{3,1},{4,2},{5,3},{6,4},{7,5},{8,14},{9,15},{10,... | collective-permute-start | bytes 2949128 | tf_op jit(solution)/shard_map/ppermute | solution.py:166
  189.0 20.8 %collective-permute-done.6 = bf16[192,2560]{1,0:T(8,128)(2,1)} collective-permute-done((bf16[192,2560]{1,0:T(8,128)(2,1)}, bf16[192,2560]{1,0:T(8,128)(2,1)}, u32[]{:S(2)}, u32[]{:S(2)}) %collective-permute-start.6) | collective-permute-done | bytes 983072 | tf_op jit(solution)/shard_map/ppermute | solution.py:166
  209.9 20.0 %collective-permute-done.7 = bf16[192,2560]{1,0:T(8,128)(2,1)} collective-permute-done((bf16[192,2560]{1,0:T(8,128)(2,1)S(1)}, bf16[192,2560]{1,0:T(8,128)(2,1)}, u32[]{:S(2)}, u32[]{:S(2)}) %collective-permute-start.7) | collective-permute-done | bytes 983072 | tf_op jit(solution)/shard_map/ppermute | solution.py:166
  232.1 3.5 %fusion.17 = (f32[192]{0:T(256)S(1)}, f32[192]{0:T(256)S(1)}, f32[192,2560]{1,0:T(8,128)S(1)}) fusion(bf16[192,2560]{1,0:T(8,128)(2,1)} %collective-permute-done.8, bf16[192,2560]{1,0:T(8,128)(2,1)} %collective-permute-done.7, bf16[192,2560]{1,0:T(8,128)(2,1)} %collective-permute-done.6, f32[768,2560]{1,0:T(8,128)} %copy-done.1, s32[]{:T(128)S(6)} %select_n.78, ...), kind=kLoop, calls=%fused_computation.46 | loop fusion | flops 5897856 | bytes 7876108 | tf_op jit(solution)/shard_map/reduce_sum | solution.py:177
  239.8 2.5 collective-permute-start.11
  244.8 3.3 %all-to-all-start.4 = ((f32[4,192,32]{1,2,0:T(8,128)}), f32[4,192,32]{1,2,0:T(8,128)S(1)}, u32[]{:S(2)}, u32[]{:S(2)}) async-start(f32[4,192,32]{1,2,0:T(8,128)} %broadcast_in_dim.2), calls=%async_computation.4 | async-start | bytes 262144 | tf_op jit(solution)/shard_map/all_to_all | solution.py:194
  249.0 5.1 %all-to-all-done.4 = f32[4,192,32]{1,2,0:T(8,128)S(1)} async-done(((f32[4,192,32]{1,2,0:T(8,128)}), f32[4,192,32]{1,2,0:T(8,128)S(1)}, u32[]{:S(2)}, u32[]{:S(2)}) %all-to-all-start.4) | async-done | bytes 98336 | tf_op jit(solution)/shard_map/all_to_all | solution.py:194
  (75 shorter events, 28.6 us)
Async XLA Ops:
  7.2 229.8 %copy-start = (bf16[5120,64]{0,1:T(8,128)(2,1)S(1)}, bf16[5120,64]{0,1:T(8,128)(2,1)}, u32[]{:S(2)}) copy-start(bf16[5120,64]{0,1:T(8,128)(2,1)} %param.20) | copy-start | bytes 1966084
  7.2 134.4 %all-gather.2.cloned.1.call-start = ((), (), s32[]{:S(2)}) async-start(), calls=%async_computation.5 | async-start | bytes 3538944 | tf_op jit(solution)/shard_map/all_gather | solution.py:128
  10.3 0.7 collective-permute-start.2
  12.6 45.8 %copy-start.3 = (bf16[1,768,640]{2,1,0:T(8,128)(2,1)S(1)}, bf16[1,768,640]{2,1,0:T(8,128)(2,1)}, u32[]{:S(2)}) copy-start(bf16[1,768,640]{2,1,0:T(8,128)(2,1)} %param.14) | copy-start | bytes 2949124
  13.7 57.9 %all-to-all-start.1 = ((bf16[768,4,128]{2,0,1:T(8,128)(2,1)}), bf16[768,4,128]{2,0,1:T(8,128)(2,1)S(1)}, u32[]{:S(2)}, u32[]{:S(2)}) async-start(bf16[768,4,128]{2,0,1:T(8,128)(2,1)} %copy_bitcast_fusion.1), calls=%async_computation.1 | async-start | bytes 1572864 | tf_op jit(solution)/shard_map/all_to_all | solution.py:137
  58.3 29.1 %copy-start.4 = (bf16[1,768,640]{2,1,0:T(8,128)(2,1)S(1)}, bf16[1,768,640]{2,1,0:T(8,128)(2,1)}, u32[]{:S(2)}) copy-start(bf16[1,768,640]{2,1,0:T(8,128)(2,1)} %param.12) | copy-start | bytes 2949124
  71.5 15.9 %all-to-all-start.2 = ((bf16[768,4,128]{2,0,1:T(8,128)(2,1)}), bf16[768,4,128]{2,0,1:T(8,128)(2,1)S(1)}, u32[]{:S(2)}, u32[]{:S(2)}) async-start(bf16[768,4,128]{2,0,1:T(8,128)(2,1)} %copy_bitcast_fusion), calls=%async_computation.2 | async-start | bytes 1572864 | tf_op jit(solution)/shard_map/all_to_all | solution.py:137
  75.0 28.6 %collective-permute-start = (bf16[3072,128]{1,0:T(8,128)(2,1)S(1)}, bf16[3072,128]{1,0:T(8,128)(2,1)}, u32[]{:S(2)}, u32[]{:S(2)}) collective-permute-start(bf16[3072,128]{1,0:T(8,128)(2,1)S(1)} %bitcast.83), channel_id=1, source_target_pairs={{0,8},{8,0},{16,24},{24,16},{32,40},{40,32},{48,56},{56,48},{1,9},... | collective-permute-start | bytes 2359304 | tf_op jit(solution)/shard_map/ppermute | solution.py:142
  87.4 25.3 %collective-permute-start.1 = (bf16[3072,128]{1,0:T(8,128)(2,1)S(1)}, bf16[3072,128]{1,0:T(8,128)(2,1)}, u32[]{:S(2)}, u32[]{:S(2)}) collective-permute-start(bf16[3072,128]{1,0:T(8,128)(2,1)S(1)} %bitcast.85), channel_id=1, source_target_pairs={{0,8},{8,0},{16,24},{24,16},{32,40},{40,32},{48,56},{56,48},{1,9},... | collective-permute-start | bytes 2359304 | tf_op jit(solution)/shard_map/ppermute | solution.py:144
  88.6 15.1 %all-to-all-start = ((bf16[768,4,128]{2,0,1:T(8,128)(2,1)}), bf16[768,4,128]{2,0,1:T(8,128)(2,1)S(1)}, u32[]{:S(2)}, u32[]{:S(2)}) async-start(bf16[768,4,128]{2,0,1:T(8,128)(2,1)} %copy_bitcast_fusion.2), calls=%async_computation | async-start | bytes 1572864 | tf_op jit(solution)/shard_map/all_to_all | solution.py:137
  96.0 63.9 %collective-permute-start.5 = (bf16[640,2560]{1,0:T(8,128)(2,1)}, bf16[640,2560]{1,0:T(8,128)(2,1)}, u32[]{:S(2)}, u32[]{:S(2)}) collective-permute-start(bf16[640,2560]{1,0:T(8,128)(2,1)} %constant_dynamic-slice_fusion.1), channel_id=1, source_target_pairs={{0,1},{1,0},{2,3},{3,2},{4,5},{5,4},{6,7},{7,6},{8,9},{9,8},{10,11... | collective-permute-start | bytes 9830408 | tf_op jit(solution)/shard_map/ppermute | solution.py:132
  137.2 15.7 %all-to-all-start.3 = ((bf16[4,768,128]{1,2,0:T(8,128)(2,1)}), bf16[4,768,128]{1,2,0:T(8,128)(2,1)S(1)}, u32[]{:S(2)}, u32[]{:S(2)}) async-start(bf16[4,768,128]{1,2,0:T(8,128)(2,1)} %copy.30), calls=%async_computation.3 | async-start | bytes 1572864 | tf_op jit(solution)/shard_map/all_to_all | solution.py:150
  152.0 0.7 collective-permute-start.3
  153.9 8.4 %collective-permute-start.4 = (bf16[768,640]{0,1:T(8,128)(2,1)}, bf16[768,640]{0,1:T(8,128)(2,1)S(1)}, u32[]{:S(2)}, u32[]{:S(2)}) collective-permute-start(bf16[768,640]{0,1:T(8,128)(2,1)} %pad_maximum_fusion), channel_id=1, source_target_pairs={{0,1},{1,0},{2,3},{3,2},{4,5},{5,4},{6,7},{7,6},{8,9},{9,8},{10,11... | collective-permute-start | bytes 2949128 | tf_op jit(solution)/shard_map/ppermute | solution.py:154
  177.0 32.8 %collective-permute-start.6 = (bf16[192,2560]{1,0:T(8,128)(2,1)}, bf16[192,2560]{1,0:T(8,128)(2,1)}, u32[]{:S(2)}, u32[]{:S(2)}) collective-permute-start(bf16[192,2560]{1,0:T(8,128)(2,1)} %get-tuple-element.5), channel_id=1, source_target_pairs={{0,2},{1,3},{2,4},{3,5},{4,6},{5,7},{6,0},{7,1},{8,10},{9,11},{10,... | collective-permute-start | bytes 2949128 | tf_op jit(solution)/shard_map/ppermute | solution.py:166
  183.9 46.0 %collective-permute-start.7 = (bf16[192,2560]{1,0:T(8,128)(2,1)S(1)}, bf16[192,2560]{1,0:T(8,128)(2,1)}, u32[]{:S(2)}, u32[]{:S(2)}) collective-permute-start(bf16[192,2560]{1,0:T(8,128)(2,1)S(1)} %get-tuple-element.7), channel_id=1, source_target_pairs={{0,6},{1,7},{2,0},{3,1},{4,2},{5,3},{6,4},{7,5},{8,14},{9,15},{10,... | collective-permute-start | bytes 2949128 | tf_op jit(solution)/shard_map/ppermute | solution.py:166
  187.5 44.6 %collective-permute-start.8 = (bf16[192,2560]{1,0:T(8,128)(2,1)S(1)}, bf16[192,2560]{1,0:T(8,128)(2,1)}, u32[]{:S(2)}, u32[]{:S(2)}) collective-permute-start(bf16[192,2560]{1,0:T(8,128)(2,1)S(1)} %get-tuple-element.6), channel_id=1, source_target_pairs={{0,4},{1,5},{2,6},{3,7},{4,0},{5,1},{6,2},{7,3},{8,12},{9,13},{10,... | collective-permute-start | bytes 2949128 | tf_op jit(solution)/shard_map/ppermute | solution.py:166
  189.0 46.7 %copy-start.12 = (f32[5120]{0:T(1024)S(1)}, f32[5120]{0:T(1024)}, u32[]{:S(2)}) copy-start(f32[5120]{0:T(1024)} %param.18) | copy-start | bytes 61444
  189.0 46.8 %copy-start.13 = (f32[5120]{0:T(1024)S(1)}, f32[5120]{0:T(1024)}, u32[]{:S(2)}) copy-start(f32[5120]{0:T(1024)} %param.19) | copy-start | bytes 61444
  235.6 18.7 %copy-start.10 = (f32[768,32]{0,1:T(8,128)S(1)}, f32[768,32]{0,1:T(8,128)}, u32[]{:S(2)}) copy-start(f32[768,32]{0,1:T(8,128)} %param.21) | copy-start | bytes 294916
  235.7 1.2 collective-permute-start.9
  238.4 1.3 collective-permute-start.10
  239.8 4.4 %collective-permute-start.11 = (f32[192,32]{0,1:T(8,128)S(1)}, f32[192,32]{0,1:T(8,128)S(1)}, u32[]{:S(2)}, u32[]{:S(2)}) collective-permute-start(f32[192,32]{0,1:T(8,128)S(1)} %constant_dynamic-slice_fusion), channel_id=1, source_target_pairs={{0,64},{64,0},{1,65},{65,1},{2,66},{66,2},{3,67},{67,3},{4,68},{68... | collective-permute-start | bytes 73736 | tf_op jit(solution)/shard_map/ppermute | solution.py:188
  244.8 9.3 %all-to-all-start.4 = ((f32[4,192,32]{1,2,0:T(8,128)}), f32[4,192,32]{1,2,0:T(8,128)S(1)}, u32[]{:S(2)}, u32[]{:S(2)}) async-start(f32[4,192,32]{1,2,0:T(8,128)} %broadcast_in_dim.2), calls=%async_computation.4 | async-start | bytes 262144 | tf_op jit(solution)/shard_map/all_to_all | solution.py:194
  (8 other events, 67.5 us)
Sparse Core Ops, SparseCore 0:
  12.7 69.6 all-gather.1

commit v2 on v1

v2 whole, which is shorter than its diff:
```python
import functools
import math

import jax
import jax.numpy as jnp
from jax import lax
from jax.experimental import pallas as pl
from jax.experimental.pallas import tpu as pltpu
from jax.sharding import PartitionSpec as P

HSIZE = 128
STEPS = 50

guide_scale = 5.0
flow_shift = 5.0
epsilon = 1e-06

Z, YH, X, CORE = 4, 2, 4, 2
SEQ, HEAD = Z * YH, X * CORE

z_groups = [[z * YH + y for z in range(Z)] for y in range(YH)]
y_swap = [(s, s ^ 1) for s in range(SEQ)]
core_swap = [(h, h ^ 1) for h in range(HEAD)]
cfg_swap = [(0, 1), (1, 0)]


def x_shift(step):
    return [(x * CORE + c, (x + step) % X * CORE + c) for x in range(X) for c in range(CORE)]


def sigma_slope(step_number):
    moment = 1.0 - step_number.astype(jnp.float32) / STEPS
    return flow_shift / (1.0 + (flow_shift - 1.0) * moment) ** 2


def attend_body(*refs, begun, ended, rows, subs, chunk):
    query_ref, key_ref, value_ref = refs[:3]
    refs = refs[3:]
    if begun:
        sum_in, stat_in = refs[:2]
        refs = refs[2:]
    if ended:
        out_ref = refs[0]
        refs = refs[1:]
    else:
        sum_out, stat_out = refs[:2]
        refs = refs[2:]
    keys_t, values_one = refs
    tokens = key_ref.shape[0]

    @pl.when(pl.program_id(0) == 0)
    def _():
        step = 384
        for at in range(0, tokens, step):
            block = key_ref[at : at + step, :].astype(jnp.float32).T.astype(jnp.bfloat16)
            keys_t[:HSIZE, at : at + step] = block
            keys_t[HSIZE:, at : at + step] = block
        values_one[:, :HSIZE] = value_ref[...]
        values_one[:, HSIZE:] = jnp.ones((tokens, HSIZE), jnp.bfloat16)

    work = [(sub, at) for sub in range(subs) for at in range(0, tokens, chunk)]

    def score(item):
        sub, at = item
        scaled = query_ref[sub * rows : (sub + 1) * rows, :].astype(jnp.float32)
        scaled = scaled * (math.log2(math.e) / math.sqrt(HSIZE))
        upper = scaled.astype(jnp.bfloat16)
        lower = (scaled - upper.astype(jnp.float32)).astype(jnp.bfloat16)
        return jnp.dot(
            jnp.concatenate([upper, lower], axis=1),
            keys_t[:, at : at + chunk],
            preferred_element_type=jnp.float32,
        )

    peak, total = None, None
    scores = score(work[0])
    for index, (sub, at) in enumerate(work):
        following = score(work[index + 1]) if index + 1 < len(work) else None
        new_peak = jnp.max(scores, axis=1, keepdims=True)
        if at > 0:
            new_peak = jnp.maximum(peak, new_peak)
        weights = jnp.exp2(scores - new_peak).astype(jnp.bfloat16)
        summed = jnp.dot(weights, values_one[at : at + chunk, :], preferred_element_type=jnp.float32)
        total = summed if at == 0 else total * jnp.exp2(peak - new_peak) + summed
        peak, scores = new_peak, following
        if at + chunk == tokens:
            span = slice(sub * rows, (sub + 1) * rows)
            top, low = total[:, :HSIZE], total[:, HSIZE:]
            if begun:
                peak_in, low_in = stat_in[span, :1], stat_in[span, 1:2]
                both = jnp.maximum(peak, peak_in)
                here, there = jnp.exp2(peak - both), jnp.exp2(peak_in - both)
                top = top * here + sum_in[span, :] * there
                low = low * here + low_in * there
                peak = both
            if ended:
                out_ref[span, :] = (top / low).astype(jnp.bfloat16)
            else:
                lane = lax.broadcasted_iota(jnp.int32, low.shape, 1)
                sum_out[span, :] = top
                stat_out[span, :] = jnp.where(lane == 0, peak, low)

def attend(queries, keys, values, state=None, last=True, rows=768, subs=1, chunk=1536):
    count, tokens = queries.shape[0], keys.shape[0]
    tile = pl.BlockSpec((rows * subs, HSIZE), lambda i: (i, 0))
    whole = pl.BlockSpec((tokens, HSIZE), lambda i: (0, 0))
    wide = jax.ShapeDtypeStruct((count, HSIZE), jnp.float32)
    return pl.pallas_call(
        functools.partial(attend_body, begun=state is not None, ended=last, rows=rows, subs=subs, chunk=chunk),
        grid=(count // (rows * subs),),
        in_specs=[tile, whole, whole] + ([] if state is None else [tile, tile]),
        out_specs=tile if last else [tile, tile],
        out_shape=jax.ShapeDtypeStruct((count, HSIZE), jnp.bfloat16) if last else [wide, wide],
        scratch_shapes=[
            pltpu.VMEM((2 * HSIZE, tokens), jnp.bfloat16),
            pltpu.VMEM((tokens, 2 * HSIZE), jnp.bfloat16),
        ],
        compiler_params=pltpu.CompilerParams(vmem_limit_bytes=56 * 2**20),
        cost_estimate=pl.CostEstimate(
            flops=8 * count * tokens * HSIZE,
            bytes_accessed=4 * HSIZE * (count + tokens),
            transcendentals=count * tokens,
        ),
    )(queries, keys, values, *(state or ()))


def per_device(
    queries,
    keys,
    values,
    hidden_in,
    out_weight,
    gate,
    mod_scale,
    mod_shift,
    head_weight,
    latent,
    history,
    step_index,
):
    queries, keys, values, hidden = queries[0], keys[0], values[0], hidden_in[0]
    local_tokens = queries.shape[0]
    full_width = hidden.shape[1]
    spread = Z * HSIZE
    half, share = full_width // CORE, local_tokens // X
    core = lax.axis_index("head") % CORE
    column = lax.axis_index("head") // CORE
    branch = lax.axis_index("cfg")

    fifth = lax.all_gather(
        jnp.stack([keys[:, spread:], values[:, spread:]]), "seq", axis=1, tiled=True
    )

    weight = lax.dynamic_slice_in_dim(out_weight, core * half, half, 1)
    other_weight = lax.dynamic_slice_in_dim(out_weight, (1 - core) * half, half, 1)
    weight = jnp.concatenate([weight, lax.ppermute(other_weight, "head", core_swap)])

    def deal(value):
        blocks = value[:, :spread].reshape(local_tokens, Z, HSIZE).transpose(1, 0, 2)
        return lax.all_to_all(
            blocks, "seq", 0, 0, tiled=True, axis_index_groups=z_groups
        ).reshape(Z * local_tokens, HSIZE)

    own_keys = deal(keys)
    partner_keys = lax.ppermute(own_keys, "seq", y_swap)
    values, own_keys = lax.optimization_barrier((values, own_keys))
    own_values = deal(values)
    partner_values = lax.ppermute(own_values, "seq", y_swap)
    dealt_queries, own_values = lax.optimization_barrier((queries, own_values))
    dealt_queries = deal(dealt_queries)
    dealt_queries, weight = lax.optimization_barrier((dealt_queries, weight))

    state = attend(dealt_queries, own_keys, own_values, None, False, 768, 2, 3072)
    dealt = attend(dealt_queries, partner_keys, partner_values, state, True, 768, 2, 3072)
    fifth_queries, dealt = lax.optimization_barrier((queries[:, spread:], dealt))
    dealt = lax.all_to_all(
        dealt.reshape(Z, local_tokens, HSIZE), "seq", 0, 0, tiled=True, axis_index_groups=z_groups
    )
    fifth_out = attend(fifth_queries, fifth[0], fifth[1], None, True, 768, 1, 3072)
    attended = jnp.concatenate(
        [dealt.transpose(1, 0, 2).reshape(local_tokens, spread), fifth_out], axis=1
    )
    attended = jnp.concatenate([attended, lax.ppermute(attended, "head", core_swap)], axis=1)

    def quarter(step):
        rows = lax.dynamic_slice_in_dim(attended, (column + step) % X * share, share, 0)
        return jnp.dot(rows, weight, preferred_element_type=jnp.float32)

    wire, middle = jnp.bfloat16, share // 2
    opposite = quarter(2).astype(wire)
    behind_far = lax.ppermute(opposite[:middle], "head", x_shift(1))
    ahead_far = lax.ppermute(opposite[middle:], "head", x_shift(3))
    forward, backward = quarter(1), quarter(3)
    forward = jnp.concatenate(
        [forward[:middle] + behind_far.astype(jnp.float32), forward[middle:]]
    ).astype(wire)
    backward = jnp.concatenate(
        [backward[:middle], backward[middle:] + ahead_far.astype(jnp.float32)]
    ).astype(wire)
    behind = lax.ppermute(forward, "head", x_shift(1))
    ahead = lax.ppermute(backward, "head", x_shift(3))
    summed = quarter(0) + behind.astype(jnp.float32) + ahead.astype(jnp.float32)

    my_hidden = lax.dynamic_slice(hidden, (column * share, core * half), (share, half))

    def my_half(vector):
        return lax.dynamic_slice_in_dim(vector, core * half, half, 0)

    residual = my_hidden.astype(jnp.float32) + my_half(gate) * summed
    weight_part = my_half(head_weight).astype(jnp.float32)
    scale_part, shift_part = my_half(mod_scale), my_half(mod_shift)
    projected = jnp.dot(residual * scale_part, weight_part, precision=lax.Precision.HIGHEST)
    levels = jnp.dot(
        jnp.stack([scale_part, shift_part]), weight_part, precision=lax.Precision.HIGHEST
    )
    levels = levels + lax.ppermute(levels, "head", core_swap)
    channels = projected.shape[1] // 2
    sums = jnp.stack([jnp.sum(residual, axis=1), jnp.sum(residual * residual, axis=1)], axis=1)
    parts = jnp.concatenate([projected, sums], axis=1)
    parts = parts + lax.ppermute(parts, "head", core_swap)
    center = parts[:, 2 * channels : 2 * channels + 1] / full_width
    inverse = lax.rsqrt(parts[:, 2 * channels + 1 :] / full_width - center * center + epsilon)
    velocity = (parts[:, : 2 * channels] - center * levels[:1]) * inverse + levels[1:]

    outgoing = lax.dynamic_slice_in_dim(velocity, (1 - branch) * channels, channels, 1)
    partner_velocity = lax.ppermute(outgoing, "cfg", cfg_swap)
    own_velocity = lax.dynamic_slice_in_dim(velocity, branch * channels, channels, 1)
    conditioned = jnp.where(branch == 0, own_velocity, partner_velocity)
    unconditioned = jnp.where(branch == 0, partner_velocity, own_velocity)
    guided = unconditioned + guide_scale * (conditioned - unconditioned)
    ring = [guided] + [lax.ppermute(guided, "head", x_shift(X - ahead)) for ahead in range(1, X)]
    guided = lax.dynamic_slice_in_dim(
        jnp.concatenate(ring + ring[:-1]), (X - column) % X * share, local_tokens, 0
    )

    current_step = step_index[0]
    slopes = [sigma_slope(current_step - behind) for behind in range(4)]
    combined = (
        55.0 * slopes[0] * guided
        - 59.0 * slopes[1] * history[0]
        + 37.0 * slopes[2] * history[1]
        - 9.0 * slopes[3] * history[2]
    ) / 24.0
    advanced = latent - combined / STEPS
    return (guided, advanced)


def solution(mesh):
    placed = (
        P("cfg", "seq", "head"),
        P("cfg", "seq", "head"),
        P("cfg", "seq", "head"),
        P("cfg", "seq", None),
        P("head", None),
        P(),
        P(),
        P(),
        P(),
        P("seq", "cfg"),
        P(None, "seq", "cfg"),
        P(),
    )
    return jax.shard_map(
        per_device,
        mesh=mesh,
        in_specs=placed,
        out_specs=(P("seq", "cfg"), P("seq", "cfg")),
        check_vma=False,
    )
```

time: 264 us -> 207 us (0.78)
  starting transfers between devices: 82.5 us -> 29.8 us
  waiting for transfers between devices: 93.9 us -> 60.2 us
  blocking collectives: 0 us -> 19.7 us
  other arithmetic: 5.34 us -> 11.6 us
  Pallas kernels: 30.5 us -> 36.3 us
  local copies, waits for them, and re-layouts: 22.6 us -> 18.2 us
  matrix products: 11.9 us -> 15 us
    all_to_all x5 -> x3, starting transfers between devices: 59.4 us -> 11.5 us  [the longest x2 6.99 us: deal(): lax.all_to_all(blocks, 'seq', 0, 0, tiled=True, axis_index_groups=z_groups)]
    all_to_all x5 -> x3, waiting for transfers between devices: 35.4 us -> 14.6 us  [the longest x2 14.6 us: deal(): lax.all_to_all(blocks, 'seq', 0, 0, tiled=True, axis_index_groups=z_groups)]
    all_to_all x0 -> x1, blocking collectives: none -> 19.7 us  [deal(): lax.all_to_all(blocks, 'seq', 0, 0, tiled=True, axis_index_groups=z_groups)]
    ppermute x9 -> x11, waiting for transfers between devices: 47.5 us -> 35.1 us  [the longest x1 18 us: per_device(): behind = lax.ppermute(forward, 'head', x_shift(1))]
    concatenate x1 -> x6, other arithmetic: 1.02 us -> 9.73 us  [the longest x1 6.11 us: per_device(): jnp.concatenate([weight, lax.ppermute(other_weight, 'head', core_swap)])]
    ppermute x9 -> x11, starting transfers between devices: 19.6 us -> 11.5 us  [the longest x3 4.71 us: per_device(): lax.ppermute(guided, 'head', x_shift(X - ahead))]
    pallas_call x2 -> x3, Pallas kernels: 30.5 us -> 36.3 us  [attend(): pl.pallas_call(functools.partial(attend_body, begun=state is not None, en...]
    all_to_all x5 -> x0, local copies, waits for them, and re-layouts: 4.49 us -> none  [the longest x3 3.22 us: deal(): lax.all_to_all(value[:, :spread], 'seq', 1, 0, tiled=True, axis_index_gro...]
  transfers between devices with their start and end apart: 18 -> 18, of which waited for: 12 -> 12; matrix products, arithmetic and copies ran while one was open for 5% -> 11% of each run, Pallas kernels for 12% -> 18%
where the time goes in v2:
time: 207 us; the launch traced here: 206 us
  waiting for transfers between devices  60.2 us (29%)
  Pallas kernels  36.3 us (18%)
  starting transfers between devices  29.8 us (14%)
  blocking collectives  19.7 us (10%)
  local copies, waits for them, and re-layouts  18.2 us (9%)
  between operations  15.3 us (7%)
  matrix products  15 us (7%)
  other arithmetic  11.6 us (6%)
    pallas_call x3, Pallas kernels, attend(): pl.pallas_call(functools.partial(attend_body, begun=state is not None, en...  36.3 us
    all_to_all x1, blocking collectives, deal(): lax.all_to_all(blocks, 'seq', 0, 0, tiled=True, axis_index_groups=z_groups)  19.7 us
    ppermute x1, waiting for transfers between devices, per_device(): behind = lax.ppermute(forward, 'head', x_shift(1))  18 us
    all_to_all x2, waiting for transfers between devices, deal(): lax.all_to_all(blocks, 'seq', 0, 0, tiled=True, axis_index_groups=z_groups)  14.6 us
    dot_general x4, matrix products, quarter(): return jnp.dot(rows, weight, preferred_element_type=jnp.float32)  13.4 us
    ppermute x1, waiting for transfers between devices, per_device(): partner_values = lax.ppermute(own_values, 'seq', y_swap)  8.15 us
    ppermute x1, waiting for transfers between devices, per_device(): behind_far = lax.ppermute(opposite[:middle], 'head', x_shift(1))  7.89 us
    all_to_all x2, starting transfers between devices, deal(): lax.all_to_all(blocks, 'seq', 0, 0, tiled=True, axis_index_groups=z_groups)  6.99 us
  transfers between devices with their start and end apart: 18, of which 12 were waited for; matrix products, arithmetic and copies ran while one was open for 11% of the time, Pallas kernels for 18%

profile of v2, /device:TPU:0, one launch (start us, length us, event | category | flops | bytes accessed | tf_op | source)
XLA Modules:
  0.0 206.2 jit_solution(14691424265319793720)
XLA Ops:
  7.3 6.2 %constant_dynamic-slice_fusion.3 = (bf16[640,2560]{1,0:T(8,128)(2,1)}, bf16[640,2560]{1,0:T(8,128)(2,1)}) fusion(bf16[640,5120]{1,0:T(8,128)(2,1)} %param.16, s32[]{:T(128)S(6)} %select_n.82, s32[]{:T(128)S(6)} %select_n.83), kind=kLoop, calls=%fused_computation.61 | loop fusion | bytes 13107208 | tf_op jit(solution)/shard_map/dynamic_slice | solution.py:154
  14.5 19.7 %all_to_all.20 = bf16[4,768,128]{2,1,0:T(8,128)(2,1)S(1)} all-to-all(bf16[4,768,128]{2,1,0:T(8,128)(2,1)S(1)} %bitcast_bitcast_fusion.2), channel_id=1, replica_groups={{0,16,32,48},{8,24,40,56},{1,17,33,49},{9,25,41,57},{2,18,34,50},{10,26..., dimensions={0} | all-to-all | bytes 1572864 | tf_op jit(solution)/shard_map/all_to_all | solution.py:160
  35.2 3.5 %all-to-all-start.1 = ((bf16[4,768,128]{2,1,0:T(8,128)(2,1)}), bf16[4,768,128]{2,1,0:T(8,128)(2,1)S(1)}, u32[]{:S(2)}, u32[]{:S(2)}) async-start(bf16[4,768,128]{2,1,0:T(8,128)(2,1)} %bitcast_bitcast_fusion.1), calls=%async_computation.1 | async-start | bytes 1572864 | tf_op jit(solution)/shard_map/all_to_all | solution.py:160
  39.4 3.4 %collective-permute-start.1 = (bf16[3072,128]{1,0:T(8,128)(2,1)S(1)}, bf16[3072,128]{1,0:T(8,128)(2,1)}, u32[]{:S(2)}, u32[]{:S(2)}) collective-permute-start(bf16[3072,128]{1,0:T(8,128)(2,1)S(1)} %bitcast.84), channel_id=1, source_target_pairs={{0,8},{8,0},{16,24},{24,16},{32,40},{40,32},{48,56},{56,48},{1,9},... | collective-permute-start | bytes 2359304 | tf_op jit(solution)/shard_map/ppermute | solution.py:165
  42.8 8.3 %all-to-all-done.1 = bf16[4,768,128]{2,1,0:T(8,128)(2,1)S(1)} async-done(((bf16[4,768,128]{2,1,0:T(8,128)(2,1)}), bf16[4,768,128]{2,1,0:T(8,128)(2,1)S(1)}, u32[]{:S(2)}, u32[]{:S(2)}) %all-to-all-start.1) | async-done | bytes 786464 | tf_op jit(solution)/shard_map/all_to_all | solution.py:160
  53.8 3.5 %all-to-all-start.2 = ((bf16[4,768,128]{2,1,0:T(8,128)(2,1)}), bf16[4,768,128]{2,1,0:T(8,128)(2,1)S(1)}, u32[]{:S(2)}, u32[]{:S(2)}) async-start(bf16[4,768,128]{2,1,0:T(8,128)(2,1)} %bitcast_bitcast_fusion), calls=%async_computation.2 | async-start | bytes 1572864 | tf_op jit(solution)/shard_map/all_to_all | solution.py:160
  57.3 6.1 %pad_maximum_fusion = bf16[1280,2560]{1,0:T(8,128)(2,1)} fusion(bf16[640,2560]{1,0:T(8,128)(2,1)} %collective-permute-done, bf16[640,2560]{1,0:T(8,128)(2,1)} %get-tuple-element.26), kind=kLoop, calls=%fused_computation | loop fusion | flops 13107200 | bytes 13107200 | tf_op jit(solution)/shard_map/concatenate | solution.py:156
  63.4 6.4 %all-to-all-done.2 = bf16[4,768,128]{2,1,0:T(8,128)(2,1)S(1)} async-done(((bf16[4,768,128]{2,1,0:T(8,128)(2,1)}), bf16[4,768,128]{2,1,0:T(8,128)(2,1)S(1)}, u32[]{:S(2)}, u32[]{:S(2)}) %all-to-all-start.2) | async-done | bytes 786464 | tf_op jit(solution)/shard_map/all_to_all | solution.py:160
  70.7 13.4 %shard_map.131 = (f32[3072,128]{1,0:T(8,128)}, f32[3072,128]{1,0:T(8,128)}) custom-call(bf16[3072,128]{1,0:T(8,128)(2,1)} %bitcast.86, bf16[3072,128]{1,0:T(8,128)(2,1)} %bitcast.85, bf16[3072,128]{1,0:T(8,128)(2,1)} %bitcast.83), custom_call_target="tpu_custom_call" | custom-call | flops 9663676416 | bytes 3145728 | tf_op jit(solution)/shard_map/pallas_call | solution.py:108
  84.1 8.1 %collective-permute-done.2.refs_2_ = bf16[3072,128]{1,0:T(8,128)(2,1)} collective-permute-done((bf16[3072,128]{1,0:T(8,128)(2,1)S(1)}, bf16[3072,128]{1,0:T(8,128)(2,1)}, u32[]{:S(2)}, u32[]{:S(2)}) %collective-permute-start.2) | collective-permute-done | bytes 786464 | tf_op jit(solution)/shard_map/ppermute | solution.py:168
  92.3 14.5 %shard_map.132 = bf16[3072,128]{1,0:T(8,128)(2,1)} custom-call(bf16[3072,128]{1,0:T(8,128)(2,1)} %bitcast.87, bf16[3072,128]{1,0:T(8,128)(2,1)} %collective-permute-done.1.refs_1_, bf16[3072,128]{1,0:T(8,128)(2,1)} %collective-permute-done.2.refs_2_, f32[3072,128]{1,0:T(8,128)} %get-tuple-element.17.refs_3_, f32[3072,128]{1,0:T(8,128)} %get-tuple-element.18.refs_4_), custom_call_target="tpu_custom_call" | custom-call | flops 9663676416 | bytes 3145728 | tf_op jit(solution)/shard_map/pallas_call | solution.py:108
  106.7 2.3 %copy.26 = bf16[4,768,128]{1,2,0:T(8,128)(2,1)} copy(bf16[4,768,128]{2,1,0:T(8,128)(2,1)} %bitcast.88) | data formatting | bytes 1572864 | tf_op jit(solution)/shard_map/reshape | solution.py:177
  109.0 4.5 %all-to-all-start.3 = ((bf16[4,768,128]{1,2,0:T(8,128)(2,1)}), bf16[4,768,128]{1,2,0:T(8,128)(2,1)S(1)}, u32[]{:S(2)}, u32[]{:S(2)}) async-start(bf16[4,768,128]{1,2,0:T(8,128)(2,1)} %copy.26), calls=%async_computation.3 | async-start | bytes 1572864 | tf_op jit(solution)/shard_map/all_to_all | solution.py:176
  113.5 3.8 %slice_bitcast_fusion = (bf16[6144,128]{1,0:T(8,128)(2,1)}, bf16[6144,128]{1,0:T(8,128)(2,1)}) fusion(bf16[2,6144,128]{2,1,0:T(8,128)(2,1)} %all-gather.2.cloned.1.call-done), kind=kLoop, calls=%fused_computation.10 | loop fusion | bytes 6291456 | tf_op jit(solution)/shard_map/squeeze | solution.py:179
  117.3 8.4 %shard_map.133 = bf16[768,128]{1,0:T(8,128)(2,1)} custom-call(bf16[768,128]{1,0:T(8,128)(2,1)} %slice.90.refs_0_, bf16[6144,128]{1,0:T(8,128)(2,1)} %get-tuple-element.29.refs_1_, bf16[6144,128]{1,0:T(8,128)(2,1)} %get-tuple-element.28.refs_2_), custom_call_target="tpu_custom_call" | custom-call | flops 4831838208 | bytes 3538944 | tf_op jit(solution)/shard_map/pallas_call | solution.py:108
  127.5 2.2 %collective-permute-done.3 = bf16[768,640]{0,1:T(8,128)(2,1)} collective-permute-done((bf16[768,640]{0,1:T(8,128)(2,1)S(1)}, bf16[768,640]{0,1:T(8,128)(2,1)}, u32[]{:S(2)}, u32[]{:S(2)}) %collective-permute-start.3) | collective-permute-done | bytes 983072 | tf_op jit(solution)/shard_map/ppermute | solution.py:183
  131.2 4.6 %convolution_convert_fusion = bf16[192,2560]{1,0:T(8,128)(2,1)S(1)} fusion(bf16[1280,2560]{1,0:T(8,128)(2,1)} %pad_maximum_fusion, bf16[768,1280]{0,1:T(8,128)(2,1)S(1)} %pad_maximum_fusion.1, s32[]{:T(128)S(6)} %select_n.89), kind=kOutput, calls=%fused_computation.5 | convolution fusion | flops 1258782720 | bytes 8192004 | tf_op jit(solution)/shard_map/dot_general | solution.py:187
  142.5 7.9 %collective-permute-done.4 = bf16[96,2560]{1,0:T(8,128)(2,1)S(1)} collective-permute-done((bf16[96,2560]{1,0:T(8,128)(2,1)S(1)}, bf16[96,2560]{1,0:T(8,128)(2,1)S(1)}, u32[]{:S(2)}, u32[]{:S(2)}) %collective-permute-start.4) | collective-permute-done | bytes 491552 | tf_op jit(solution)/shard_map/ppermute | solution.py:191
  153.2 3.0 %collective-permute-start.7 = (bf16[192,2560]{1,0:T(8,128)(2,1)}, bf16[192,2560]{1,0:T(8,128)(2,1)}, u32[]{:S(2)}, u32[]{:S(2)}) collective-permute-start(bf16[192,2560]{1,0:T(8,128)(2,1)} %pad_maximum_fusion.4), channel_id=1, source_target_pairs={{0,6},{1,7},{2,0},{3,1},{4,2},{5,3},{6,4},{7,5},{8,14},{9,15},{10,... | collective-permute-start | bytes 2949128 | tf_op jit(solution)/shard_map/ppermute | solution.py:201
  157.9 18.0 %collective-permute-done.5 = bf16[192,2560]{1,0:T(8,128)(2,1)} collective-permute-done((bf16[192,2560]{1,0:T(8,128)(2,1)}, bf16[192,2560]{1,0:T(8,128)(2,1)}, u32[]{:S(2)}, u32[]{:S(2)}) %collective-permute-start.5) | collective-permute-done | bytes 983072 | tf_op jit(solution)/shard_map/ppermute | solution.py:200
  176.7 5.7 %fusion.33 = (f32[192]{0:T(256)S(1)}, f32[192]{0:T(256)S(1)}, f32[192,2560]{1,0:T(8,128)S(1)}) fusion(bf16[192,2560]{1,0:T(8,128)(2,1)} %collective-permute-done.7, bf16[192,2560]{1,0:T(8,128)(2,1)} %collective-permute-done.5, bf16[1280,2560]{1,0:T(8,128)(2,1)} %pad_maximum_fusion, bf16[768,1280]{0,1:T(8,128)(2,1)S(1)} %pad_maximum_fusion.1, ...), kind=kOutput, calls=%fused_computation.71 | convolution fusion | flops 1263205888 | bytes 12137996 | tf_op jit(solution)/shard_map/dot_general | solution.py:187
  186.8 2.4 %collective-permute-done.10 = f32[192,32]{0,1:T(8,128)S(1)} collective-permute-done((f32[192,32]{0,1:T(8,128)S(1)}, f32[192,32]{0,1:T(8,128)S(1)}, u32[]{:S(2)}, u32[]{:S(2)}) %collective-permute-start.10) | collective-permute-done | bytes 24608 | tf_op jit(solution)/shard_map/ppermute | solution.py:226
  189.2 3.8 %collective-permute-start.11 = (f32[192,32]{0,1:T(8,128)S(1)}, f32[192,32]{0,1:T(8,128)S(1)}, u32[]{:S(2)}, u32[]{:S(2)}) collective-permute-start(f32[192,32]{0,1:T(8,128)S(1)} %multiply_add_fusion), channel_id=1, source_target_pairs={{0,6},{1,7},{2,0},{3,1},{4,2},{5,3},{6,4},{7,5},{8,14},{9,15},{10,... | collective-permute-start | bytes 73736 | tf_op jit(solution)/shard_map/ppermute | solution.py:231
  194.7 3.7 %collective-permute-done.12 = f32[192,32]{0,1:T(8,128)S(1)} collective-permute-done((f32[192,32]{0,1:T(8,128)S(1)}, f32[192,32]{0,1:T(8,128)S(1)}, u32[]{:S(2)}, u32[]{:S(2)}) %collective-permute-start.12) | collective-permute-done | bytes 24608 | tf_op jit(solution)/shard_map/ppermute | solution.py:231
  (90 shorter events, 27.7 us)
Async XLA Ops:
  7.2 149.2 %copy-start = (bf16[5120,64]{0,1:T(8,128)(2,1)S(1)}, bf16[5120,64]{0,1:T(8,128)(2,1)}, u32[]{:S(2)}) copy-start(bf16[5120,64]{0,1:T(8,128)(2,1)} %param.20) | copy-start | bytes 1966084
  7.2 106.3 %all-gather.2.cloned.1.call-start = ((), (), s32[]{:S(2)}) async-start(), calls=%async_computation.4 | async-start | bytes 3538944 | tf_op jit(solution)/shard_map/all_gather | solution.py:150
  13.4 43.8 %collective-permute-start = (bf16[640,2560]{1,0:T(8,128)(2,1)}, bf16[640,2560]{1,0:T(8,128)(2,1)}, u32[]{:S(2)}, u32[]{:S(2)}) collective-permute-start(bf16[640,2560]{1,0:T(8,128)(2,1)} %get-tuple-element.27), channel_id=1, source_target_pairs={{0,1},{1,0},{2,3},{3,2},{4,5},{5,4},{6,7},{7,6},{8,9},{9,8},{10,11... | collective-permute-start | bytes 9830408 | tf_op jit(solution)/shard_map/ppermute | solution.py:156
  34.1 19.6 %copy-start.6 = (bf16[4,768,128]{2,1,0:T(8,128)(2,1)}, bf16[4,768,128]{2,1,0:T(8,128)(2,1)S(1)}, u32[]{:S(2)}) copy-start(bf16[4,768,128]{2,1,0:T(8,128)(2,1)S(1)} %all_to_all.20) | copy-start | bytes 2359300
  35.2 15.9 %all-to-all-start.1 = ((bf16[4,768,128]{2,1,0:T(8,128)(2,1)}), bf16[4,768,128]{2,1,0:T(8,128)(2,1)S(1)}, u32[]{:S(2)}, u32[]{:S(2)}) async-start(bf16[4,768,128]{2,1,0:T(8,128)(2,1)} %bitcast_bitcast_fusion.1), calls=%async_computation.1 | async-start | bytes 1572864 | tf_op jit(solution)/shard_map/all_to_all | solution.py:160
  39.4 44.7 %collective-permute-start.1 = (bf16[3072,128]{1,0:T(8,128)(2,1)S(1)}, bf16[3072,128]{1,0:T(8,128)(2,1)}, u32[]{:S(2)}, u32[]{:S(2)}) collective-permute-start(bf16[3072,128]{1,0:T(8,128)(2,1)S(1)} %bitcast.84), channel_id=1, source_target_pairs={{0,8},{8,0},{16,24},{24,16},{32,40},{40,32},{48,56},{56,48},{1,9},... | collective-permute-start | bytes 2359304 | tf_op jit(solution)/shard_map/ppermute | solution.py:165
  51.0 12.4 %copy-start.5 = (bf16[4,768,128]{2,1,0:T(8,128)(2,1)}, bf16[4,768,128]{2,1,0:T(8,128)(2,1)S(1)}, u32[]{:S(2)}) copy-start(bf16[4,768,128]{2,1,0:T(8,128)(2,1)S(1)} %all-to-all-done.1) | copy-start | bytes 2359300
  51.0 41.2 %collective-permute-start.2 = (bf16[3072,128]{1,0:T(8,128)(2,1)S(1)}, bf16[3072,128]{1,0:T(8,128)(2,1)}, u32[]{:S(2)}, u32[]{:S(2)}) collective-permute-start(bf16[3072,128]{1,0:T(8,128)(2,1)S(1)} %bitcast.82), channel_id=1, source_target_pairs={{0,8},{8,0},{16,24},{24,16},{32,40},{40,32},{48,56},{56,48},{1,9},... | collective-permute-start | bytes 2359304 | tf_op jit(solution)/shard_map/ppermute | solution.py:168
  53.8 16.0 %all-to-all-start.2 = ((bf16[4,768,128]{2,1,0:T(8,128)(2,1)}), bf16[4,768,128]{2,1,0:T(8,128)(2,1)S(1)}, u32[]{:S(2)}, u32[]{:S(2)}) async-start(bf16[4,768,128]{2,1,0:T(8,128)(2,1)} %bitcast_bitcast_fusion), calls=%async_computation.2 | async-start | bytes 1572864 | tf_op jit(solution)/shard_map/all_to_all | solution.py:160
  109.0 17.7 %all-to-all-start.3 = ((bf16[4,768,128]{1,2,0:T(8,128)(2,1)}), bf16[4,768,128]{1,2,0:T(8,128)(2,1)S(1)}, u32[]{:S(2)}, u32[]{:S(2)}) async-start(bf16[4,768,128]{1,2,0:T(8,128)(2,1)} %copy.26), calls=%async_computation.3 | async-start | bytes 1572864 | tf_op jit(solution)/shard_map/all_to_all | solution.py:176
  126.9 2.8 %collective-permute-start.3 = (bf16[768,640]{0,1:T(8,128)(2,1)S(1)}, bf16[768,640]{0,1:T(8,128)(2,1)}, u32[]{:S(2)}, u32[]{:S(2)}) collective-permute-start(bf16[768,640]{0,1:T(8,128)(2,1)S(1)} %pad_maximum_fusion.2), channel_id=1, source_target_pairs={{0,1},{1,0},{2,3},{3,2},{4,5},{5,4},{6,7},{7,6},{8,9},{9,8},{10,11... | collective-permute-start | bytes 2949128 | tf_op jit(solution)/shard_map/ppermute | solution.py:183
  129.6 7.7 %slice-start = ((s8[6553600]{0:T(1024)(128)(4,1)}), s8[2359296]{0:T(1024)(128)(4,1)S(1)}, s32[]{:S(2)}) async-start(s8[6553600]{0:T(1024)(128)(4,1)} %bitcast.72), calls=%async_computation.5 | async-start | bytes 4718592
  135.8 14.5 %collective-permute-start.4 = (bf16[96,2560]{1,0:T(8,128)(2,1)S(1)}, bf16[96,2560]{1,0:T(8,128)(2,1)S(1)}, u32[]{:S(2)}, u32[]{:S(2)}) collective-permute-start(bf16[96,2560]{1,0:T(8,128)(2,1)S(1)} %get-tuple-element.30), channel_id=1, source_target_pairs={{0,2},{1,3},{2,4},{3,5},{4,6},{5,7},{6,0},{7,1},{8,10},{9,11},{10,... | collective-permute-start | bytes 1474568 | tf_op jit(solution)/shard_map/ppermute | solution.py:191
  139.0 13.0 %collective-permute-start.6 = (bf16[96,2560]{1,0:T(8,128)(2,1)S(1)}, bf16[96,2560]{1,0:T(8,128)(2,1)S(1)}, u32[]{:S(2)}, u32[]{:S(2)}) collective-permute-start(bf16[96,2560]{1,0:T(8,128)(2,1)S(1)} %get-tuple-element.31), channel_id=1, source_target_pairs={{0,6},{1,7},{2,0},{3,1},{4,2},{5,3},{6,4},{7,5},{8,14},{9,15},{10,... | collective-permute-start | bytes 1474568 | tf_op jit(solution)/shard_map/ppermute | solution.py:192
  151.5 24.5 %collective-permute-start.5 = (bf16[192,2560]{1,0:T(8,128)(2,1)}, bf16[192,2560]{1,0:T(8,128)(2,1)}, u32[]{:S(2)}, u32[]{:S(2)}) collective-permute-start(bf16[192,2560]{1,0:T(8,128)(2,1)} %pad_maximum_fusion.3), channel_id=1, source_target_pairs={{0,2},{1,3},{2,4},{3,5},{4,6},{5,7},{6,0},{7,1},{8,10},{9,11},{10,... | collective-permute-start | bytes 2949128 | tf_op jit(solution)/shard_map/ppermute | solution.py:200
  153.2 23.5 %collective-permute-start.7 = (bf16[192,2560]{1,0:T(8,128)(2,1)}, bf16[192,2560]{1,0:T(8,128)(2,1)}, u32[]{:S(2)}, u32[]{:S(2)}) collective-permute-start(bf16[192,2560]{1,0:T(8,128)(2,1)} %pad_maximum_fusion.4), channel_id=1, source_target_pairs={{0,6},{1,7},{2,0},{3,1},{4,2},{5,3},{6,4},{7,5},{8,14},{9,15},{10,... | collective-permute-start | bytes 2949128 | tf_op jit(solution)/shard_map/ppermute | solution.py:201
  156.8 1.2 collective-permute-start.9
  182.4 16.1 %copy-start.8 = (f32[3,768,32]{1,2,0:T(8,128)S(1)}, f32[3,768,32]{1,2,0:T(8,128)}, u32[]{:S(2)}) copy-start(f32[3,768,32]{1,2,0:T(8,128)} %param.22) | copy-start | bytes 884740
  182.4 16.1 %copy-start.9 = (f32[768,32]{0,1:T(8,128)S(1)}, f32[768,32]{0,1:T(8,128)}, u32[]{:S(2)}) copy-start(f32[768,32]{0,1:T(8,128)} %param.21) | copy-start | bytes 294916
  183.7 1.3 collective-permute-start.8
  185.2 4.0 %collective-permute-start.10 = (f32[192,32]{0,1:T(8,128)S(1)}, f32[192,32]{0,1:T(8,128)S(1)}, u32[]{:S(2)}, u32[]{:S(2)}) collective-permute-start(f32[192,32]{0,1:T(8,128)S(1)} %constant_dynamic-slice_fusion), channel_id=1, source_target_pairs={{0,64},{64,0},{1,65},{65,1},{2,66},{66,2},{3,67},{67,3},{4,68},{68... | collective-permute-start | bytes 73736 | tf_op jit(solution)/shard_map/ppermute | solution.py:226
  189.2 5.6 %collective-permute-start.11 = (f32[192,32]{0,1:T(8,128)S(1)}, f32[192,32]{0,1:T(8,128)S(1)}, u32[]{:S(2)}, u32[]{:S(2)}) collective-permute-start(f32[192,32]{0,1:T(8,128)S(1)} %multiply_add_fusion), channel_id=1, source_target_pairs={{0,6},{1,7},{2,0},{3,1},{4,2},{5,3},{6,4},{7,5},{8,14},{9,15},{10,... | collective-permute-start | bytes 73736 | tf_op jit(solution)/shard_map/ppermute | solution.py:231
  192.9 5.5 %collective-permute-start.12 = (f32[192,32]{0,1:T(8,128)S(1)}, f32[192,32]{0,1:T(8,128)S(1)}, u32[]{:S(2)}, u32[]{:S(2)}) collective-permute-start(f32[192,32]{0,1:T(8,128)S(1)} %multiply_add_fusion), channel_id=1, source_target_pairs={{0,4},{1,5},{2,6},{3,7},{4,0},{5,1},{6,2},{7,3},{8,12},{9,13},{10,... | collective-permute-start | bytes 73736 | tf_op jit(solution)/shard_map/ppermute | solution.py:231
  192.9 5.5 %collective-permute-start.13 = (f32[192,32]{0,1:T(8,128)S(1)}, f32[192,32]{0,1:T(8,128)S(1)}, u32[]{:S(2)}, u32[]{:S(2)}) collective-permute-start(f32[192,32]{0,1:T(8,128)S(1)} %multiply_add_fusion), channel_id=1, source_target_pairs={{0,2},{1,3},{2,4},{3,5},{4,6},{5,7},{6,0},{7,1},{8,10},{9,11},{10,... | collective-permute-start | bytes 73736 | tf_op jit(solution)/shard_map/ppermute | solution.py:231
  (9 other events, 39.6 us)
Sparse Core Ops, SparseCore 0:
  14.4 83.3 all-gather.1

commit v3 on v0

v3 whole, which is shorter than its diff:
```python
import functools
import math

import jax
import jax.numpy as jnp
from jax import lax
from jax.experimental import pallas as pl
from jax.experimental.pallas import tpu as pltpu
from jax.sharding import PartitionSpec as P

HSIZE = 128
STEPS = 50
SUMS = 8

guide_scale = 5.0
flow_shift = 5.0
epsilon = 1e-06

Z, YH, X, CORE = 4, 2, 4, 2
SEQ, HEAD = Z * YH, X * CORE

z_groups = [[z * YH + y for z in range(Z)] for y in range(YH)]
core_swap = [(h, h ^ 1) for h in range(HEAD)]
cfg_swap = [(0, 1), (1, 0)]
both_swap = [(n, n ^ (HEAD + 1)) for n in range(2 * HEAD)]


def traded(step, flip=0):
    return [
        (
            (z * YH + y) * HEAD + x * CORE + c,
            ((z + step) % Z * YH + c) * HEAD + x * CORE + (y + flip) % CORE,
        )
        for z in range(Z)
        for y in range(YH)
        for x in range(X)
        for c in range(CORE)
    ]


def x_shift(step):
    return [(x * CORE + c, (x + step) % X * CORE + c) for x in range(X) for c in range(CORE)]


def sigma_slope(step_number):
    moment = 1.0 - step_number.astype(jnp.float32) / STEPS
    return flow_shift / (1.0 + (flow_shift - 1.0) * moment) ** 2


def pack_body(place, *refs, heads):
    sources, outs = refs[:3], refs[3:]
    number = 0
    for out, count in zip(outs, heads):
        for head in range(count):

            @pl.when(pl.program_id(0) == number)
            def _(out=out, head=head):
                for kind, source in enumerate(sources):
                    out[3 * head + kind] = source[...]

            number += 1


def pack(place, sources, steps, heads):
    tokens = sources[0].shape[0]

    def column(i, place):
        step = sum(jnp.where(i == n, step, 0) for n, step in enumerate(steps))
        return 0, jnp.where(i < len(steps), (place[3] + step) % Z, Z)

    return pl.pallas_call(
        functools.partial(pack_body, heads=heads),
        grid_spec=pltpu.PrefetchScalarGridSpec(
            num_scalar_prefetch=1,
            grid=(sum(heads),),
            in_specs=[pl.BlockSpec((tokens, HSIZE), column)] * len(sources),
            out_specs=[
                pl.BlockSpec((3 * count, tokens, HSIZE), lambda i, place: (0, 0, 0))
                for count in heads
            ],
        ),
        out_shape=[
            jax.ShapeDtypeStruct((3 * count, tokens, HSIZE), jnp.bfloat16) for count in heads
        ],
        compiler_params=pltpu.CompilerParams(vmem_limit_bytes=56 * 2**20),
    )(place, *sources)


def attend_body(*refs, heads, parts, chunk):
    query_refs, refs = refs[:heads], refs[heads:]
    key_refs, value_refs, refs = refs[:parts], refs[parts : 2 * parts], refs[2 * parts :]
    out_refs, (query_ref, keys_t, values_one) = refs[:heads], refs[heads:]
    tokens = values_one.shape[0]

    for index in range(heads):

        @pl.when(pl.program_id(0) == index)
        def _(ref=query_refs[index]):
            query_ref[...] = ref[...]

    @pl.when(pl.program_id(0) == 0)
    def _():
        step, start = 384, 0
        for key_ref, value_ref in zip(key_refs, value_refs):
            length = key_ref.shape[0]
            for at in range(0, length, step):
                block = key_ref[at : at + step, :].astype(jnp.float32).T.astype(jnp.bfloat16)
                keys_t[:HSIZE, start + at : start + at + step] = block
                keys_t[HSIZE:, start + at : start + at + step] = block
            values_one[start : start + length, :HSIZE] = value_ref[...]
            start += length
        values_one[:, HSIZE:] = jnp.ones((tokens, HSIZE), jnp.bfloat16)

    scaled = query_ref[...].astype(jnp.float32) * (math.log2(math.e) / math.sqrt(HSIZE))
    upper = scaled.astype(jnp.bfloat16)
    lower = (scaled - upper.astype(jnp.float32)).astype(jnp.bfloat16)
    queries = jnp.concatenate([upper, lower], axis=1)

    def score(at):
        return jnp.dot(queries, keys_t[:, at : at + chunk], preferred_element_type=jnp.float32)

    peak, total = None, None
    scores = score(0)
    for at in range(0, tokens, chunk):
        following = score(at + chunk) if at + chunk < tokens else None
        new_peak = jnp.max(scores, axis=1, keepdims=True)
        if at > 0:
            new_peak = jnp.maximum(peak, new_peak)
        weights = jnp.exp2(scores - new_peak).astype(jnp.bfloat16)
        summed = jnp.dot(
            weights, values_one[at : at + chunk, :], preferred_element_type=jnp.float32
        )
        total = summed if at == 0 else total * jnp.exp2(peak - new_peak) + summed
        peak, scores = new_peak, following
    result = (total[:, :HSIZE] / total[:, HSIZE:]).astype(jnp.bfloat16)
    for index in range(heads):

        @pl.when(pl.program_id(0) == index)
        def _(ref=out_refs[index]):
            ref[...] = result


def attend(queries, keys, values, chunk=3072):
    rows = queries[0][0].shape[1]
    tokens = sum(part.shape[1] for part, _ in keys)
    operands = (*queries, *keys, *values)
    return pl.pallas_call(
        functools.partial(attend_body, heads=len(queries), parts=len(keys), chunk=chunk),
        grid=(len(queries),),
        in_specs=[
            pl.BlockSpec((pl.squeezed, array.shape[1], HSIZE), lambda i, index=index: (index, 0, 0))
            for array, index in operands
        ],
        out_specs=[pl.BlockSpec((rows, HSIZE), lambda i: (0, 0))] * len(queries),
        out_shape=[jax.ShapeDtypeStruct((rows, HSIZE), jnp.bfloat16)] * len(queries),
        scratch_shapes=[
            pltpu.VMEM((rows, HSIZE), jnp.bfloat16),
            pltpu.VMEM((2 * HSIZE, tokens), jnp.bfloat16),
            pltpu.VMEM((tokens, 2 * HSIZE), jnp.bfloat16),
        ],
        compiler_params=pltpu.CompilerParams(vmem_limit_bytes=56 * 2**20),
        cost_estimate=pl.CostEstimate(flops=1000, bytes_accessed=1000, transcendentals=0),
    )(*(array for array, _ in operands))


def project_body(place, *refs, steps):
    operands, own_weight, other_weight, outs = refs[: 2 * Z + 2], *refs[2 * Z + 2 :][:2], refs[2 * Z + 4 : -2]
    rows, weight = refs[-2:]
    share = rows.shape[0] // len(steps)
    depth = own_weight.shape[0]

    @pl.when(pl.program_id(0) == 0)
    def _():
        for index, step in enumerate(steps):
            start = pl.multiple_of((place[0] + step) % X * share, share)
            span = slice(index * share, (index + 1) * share)
            for number, ref in enumerate(operands):
                side, head = divmod(number, Z + 1)
                at = side * depth + (spread(place, head) if head < Z else Z * HSIZE)
                rows[span, pl.ds(at, HSIZE)] = ref[pl.ds(start, share), :]

    weight[:depth] = own_weight[...]
    weight[depth:] = other_weight[...]
    product = jnp.dot(rows[...], weight[...], preferred_element_type=jnp.float32)
    height = outs[0].shape[0]
    for index, out in enumerate(outs):
        out[...] = product[index * height : (index + 1) * height].astype(out.dtype)


def spread(place, step):
    return pl.multiple_of((place[3] + step) % Z * HSIZE, HSIZE)


def project(place, attended, own_weight, other_weight, steps, kinds, height, tile=1280):
    depth, half = other_weight.shape
    rows = attended[0].shape[0] // X * len(steps)
    tiles = half // tile
    return pl.pallas_call(
        functools.partial(project_body, steps=steps),
        grid_spec=pltpu.PrefetchScalarGridSpec(
            num_scalar_prefetch=1,
            grid=(tiles,),
            in_specs=[
                pl.BlockSpec(operand.shape, lambda i, place: (0, 0)) for operand in attended
            ]
            + [
                pl.BlockSpec((depth, tile), lambda i, place: (0, place[1] * tiles + i)),
                pl.BlockSpec((depth, tile), lambda i, place: (0, i)),
            ],
            out_specs=[pl.BlockSpec((height, tile), lambda i, place: (0, i))] * len(kinds),
            scratch_shapes=[
                pltpu.VMEM((rows, 2 * depth), jnp.bfloat16),
                pltpu.VMEM((2 * depth, tile), jnp.bfloat16),
            ],
        ),
        out_shape=[jax.ShapeDtypeStruct((height, half), kind) for kind in kinds],
        compiler_params=pltpu.CompilerParams(vmem_limit_bytes=56 * 2**20),
        cost_estimate=pl.CostEstimate(flops=1000, bytes_accessed=1000, transcendentals=0),
    )(place, *attended, own_weight, other_weight)


def finish_body(place, *refs):
    own, arrived, hidden, gate, scale, head_weight = refs[:2], refs[2:6], *refs[6:10]
    kept, given, total, turned = refs[10:]
    index = pl.program_id(0)
    summed = [
        own[n][...] + arrived[n][...].astype(jnp.float32) + arrived[2 + n][...].astype(jnp.float32)
        for n in range(2)
    ]
    residual = hidden[...].astype(jnp.float32) + gate[...] * jnp.concatenate(summed, axis=0)
    rest = residual * scale[...]
    projected = None
    for _ in range(3):
        part = rest.astype(jnp.bfloat16)
        rest = rest - part.astype(jnp.float32)
        product = jnp.dot(part, head_weight[...], preferred_element_type=jnp.float32)
        projected = product if projected is None else projected + product
    channels = projected.shape[1]
    plain = jnp.sum(residual, axis=1, keepdims=True)
    square = jnp.sum(residual * residual, axis=1, keepdims=True)
    lane = lax.broadcasted_iota(jnp.int32, (residual.shape[0], HSIZE - channels), 1)
    sums = jnp.where(lane == 0, plain, jnp.where(lane == 1, square, 0.0))
    parts = jnp.concatenate([projected, sums], axis=1)

    @pl.when(index == 0)
    def _():
        total[...] = parts

    @pl.when(index > 0)
    def _():
        total[...] += parts

    @pl.when(index == pl.num_programs(0) - 1)
    def _():
        turned[...] = total[...].T
        part = channels // 2
        for out, branch in ((kept, place[2]), (given, 1 - place[2])):
            out[:part] = turned[pl.ds(pl.multiple_of(branch * part, part), part), :]
            out[part:] = turned[channels : channels + out.shape[0] - part, :]


def finish(place, own, arrived, hidden, gate, scale, head_weight, tile=1280):
    middle, half = own[0].shape
    share, tiles = 2 * middle, half // tile
    height = head_weight.shape[1] // 2 + SUMS
    block = pl.BlockSpec((middle, tile), lambda i, place: (0, i))
    vector = pl.BlockSpec((1, tile), lambda i, place: (0, place[1] * tiles + i))
    return pl.pallas_call(
        finish_body,
        grid_spec=pltpu.PrefetchScalarGridSpec(
            num_scalar_prefetch=1,
            grid=(tiles,),
            in_specs=[block] * 6
            + [
                pl.BlockSpec((share, tile), lambda i, place: (place[0], place[1] * tiles + i)),
                vector,
                vector,
                pl.BlockSpec(
                    (tile, head_weight.shape[1]), lambda i, place: (place[1] * tiles + i, 0)
                ),
            ],
            out_specs=[pl.BlockSpec((height, share), lambda i, place: (0, 0))] * 2,
            scratch_shapes=[
                pltpu.VMEM((share, HSIZE), jnp.float32),
                pltpu.VMEM((HSIZE, share), jnp.float32),
            ],
        ),
        out_shape=[jax.ShapeDtypeStruct((height, share), jnp.float32)] * 2,
        compiler_params=pltpu.CompilerParams(vmem_limit_bytes=56 * 2**20),
        cost_estimate=pl.CostEstimate(
            flops=6 * share * half * HSIZE, bytes_accessed=12 * share * half, transcendentals=0
        ),
    )(place, *own, *arrived, hidden, gate[None], scale[None], head_weight)


def per_device(
    queries,
    keys,
    values,
    hidden_in,
    out_weight,
    gate,
    mod_scale,
    mod_shift,
    head_weight,
    latent,
    history,
    step_index,
):
    queries, keys, values, hidden = queries[0], keys[0], values[0], hidden_in[0]
    local_tokens = queries.shape[0]
    full_width = hidden.shape[1]
    half, share = full_width // CORE, local_tokens // X
    core = lax.axis_index("head") % CORE
    column = lax.axis_index("head") // CORE
    branch = lax.axis_index("cfg")

    z = lax.axis_index("seq") // YH
    place = jnp.stack([column, core, branch, z]).astype(jnp.int32)
    pair = "seq", "head"

    order = (1, 3, 2, 0)
    messages = pack(place, (queries, keys, values), order, (1, 1, 1, 2))
    messages, weight = lax.optimization_barrier((messages, out_weight))
    near = {
        step: lax.ppermute(message, pair, traded(step)) for step, message in zip(order, messages)
    }
    other_weight = lax.ppermute(
        lax.dynamic_slice_in_dim(weight, (1 - core) * half, half, 1), "head", core_swap
    )
    far = {step: lax.ppermute(near[step][:3], "head", core_swap) for step in order}
    near, far, other_weight = lax.optimization_barrier((near, far, other_weight))
    fifth_near = lax.all_gather(
        near[0][4:], "seq", axis=1, tiled=True, axis_index_groups=z_groups
    )
    dealt = attend(
        [(near[step], 0) for step in order],
        [(side[step], 1) for side in (near, far) for step in order],
        [(side[step], 2) for side in (near, far) for step in order],
    )
    fifth_near, dealt = lax.optimization_barrier((fifth_near, dealt))
    fifth_far = lax.ppermute(fifth_near, "head", core_swap)
    back = {
        step: lax.ppermute(result, pair, traded(-step)) for step, result in zip(order, dealt)
    }
    (fifth_out,) = attend(
        [(near[0], 3)],
        [(fifth_near, 0), (fifth_far, 0)],
        [(fifth_near, 1), (fifth_far, 1)],
    )
    back, fifth_out = lax.optimization_barrier((back, fifth_out))
    own_attended = [back[step] for step in range(Z)]
    attended = (
        *own_attended,
        lax.ppermute(fifth_out, pair, traded(0)),
        *(lax.ppermute(part, "head", core_swap) for part in own_attended),
        lax.ppermute(fifth_out, pair, traded(0, 1)),
    )

    wire, middle = jnp.bfloat16, share // 2
    weights = out_weight, other_weight
    opposite = project(place, attended, *weights, (2,), (wire,) * 2, middle)
    behind_far = lax.ppermute(opposite[0], "head", x_shift(1))
    ahead_far = lax.ppermute(opposite[1], "head", x_shift(3))
    attended, opposite = lax.optimization_barrier((attended, opposite))
    *rest, own_upper, own_lower = project(
        place, attended, *weights, (1, 3, 0), (jnp.float32, wire, wire) + (jnp.float32,) * 3, middle
    )
    forward, forward_lower, backward_upper, backward = rest
    behind_lower = lax.ppermute(forward_lower, "head", x_shift(1))
    ahead_upper = lax.ppermute(backward_upper, "head", x_shift(3))
    forward = (forward + behind_far.astype(jnp.float32)).astype(wire)
    backward = (backward + ahead_far.astype(jnp.float32)).astype(wire)
    behind_upper = lax.ppermute(forward, "head", x_shift(1))
    ahead_lower = lax.ppermute(backward, "head", x_shift(3))
    arrived = behind_upper, behind_lower, ahead_upper, ahead_lower

    kept, given = finish(
        place, (own_upper, own_lower), arrived, hidden, gate, mod_scale, head_weight
    )
    here = kept + lax.ppermute(kept, "head", core_swap)
    there = lax.ppermute(given, "cfg", cfg_swap) + lax.ppermute(
        given, ("cfg", "head"), both_swap
    )
    channels = head_weight.shape[1] // 2
    levels = jnp.dot(
        head_weight.astype(jnp.float32).T,
        jnp.stack([mod_scale, mod_shift], axis=1),
        precision=lax.Precision.HIGHEST,
    )
    levels = lax.dynamic_slice_in_dim(levels, branch * channels, channels, 0)

    def velocity(total):
        center = total[channels : channels + 1] / full_width
        inverse = lax.rsqrt(total[channels + 1 : channels + 2] / full_width - center * center + epsilon)
        return (total[:channels] - center * levels[:, :1]) * inverse + levels[:, 1:]

    conditioned = velocity(jnp.where(branch == 0, here, there))
    unconditioned = velocity(jnp.where(branch == 0, there, here))
    guided = unconditioned + guide_scale * (conditioned - unconditioned)
    ring = [guided] + [lax.ppermute(guided, "head", x_shift(X - ahead)) for ahead in range(1, X)]
    guided = lax.dynamic_slice_in_dim(
        jnp.concatenate(ring + ring[:-1], axis=1), (X - column) % X * share, local_tokens, 1
    ).T

    current_step = step_index[0]
    slopes = [sigma_slope(current_step - behind) for behind in range(4)]
    combined = (
        55.0 * slopes[0] * guided
        - 59.0 * slopes[1] * history[0]
        + 37.0 * slopes[2] * history[1]
        - 9.0 * slopes[3] * history[2]
    ) / 24.0
    advanced = latent - combined / STEPS
    return (guided, advanced)


def solution(mesh):
    placed = (
        P("cfg", "seq", "head"),
        P("cfg", "seq", "head"),
        P("cfg", "seq", "head"),
        P("cfg", "seq", None),
        P("head", None),
        P(),
        P(),
        P(),
        P(),
        P("seq", "cfg"),
        P(None, "seq", "cfg"),
        P(),
    )
    return jax.shard_map(
        per_device,
        mesh=mesh,
        in_specs=placed,
        out_specs=(P("seq", "cfg"), P("seq", "cfg")),
        check_vma=False,
    )
```

time: 452 us -> 194 us (0.43)
  waiting for transfers between devices: 274 us -> 36 us
  matrix products: 86.4 us -> 0.61 us
  starting transfers between devices: 1.64 us -> 67.9 us
  Pallas kernels: 0 us -> 59 us
  other arithmetic: 33.2 us -> 5.67 us
  local copies, waits for them, and re-layouts: 28.6 us -> 7.41 us
  blocking collectives: 12.9 us -> 0 us
    all_gather x2 -> x1, waiting for transfers between devices: 129 us -> 3.73 us  [per_device(): lax.all_gather(near[0][4:], 'seq', axis=1, tiled=True, axis_index_groups=...]
    dot_general x4 -> x1, matrix products: 86.4 us -> 0.61 us  [per_device(): jnp.dot(head_weight.astype(jnp.float32).T, jnp.stack([mod_scale, mod_shif...]
    reduce_scatter x1 -> x0, waiting for transfers between devices: 82.8 us -> none  [per_device(): lax.psum_scatter(projected_local, 'head', scatter_dimension=1, tiled=True)]
    ppermute x1 -> x32, starting transfers between devices: 1.49 us -> 67.9 us  [the longest x4 27.2 us: per_device(): lax.ppermute(near[step][:3], 'head', core_swap)]
    pallas_call x0 -> x6, Pallas kernels: none -> 59 us  [the longest x2 33.3 us: attend(): pl.pallas_call(functools.partial(attend_body, heads=len(queries), parts=l...]
    psum x1 -> x0, waiting for transfers between devices: 58.7 us -> none  [per_device(): lax.psum(jnp.dot(normed, weight_part, precision=lax.Precision.HIGHEST), '...]
    reduce_sum x2 -> x0, other arithmetic: 31.6 us -> none  [the longest x1 29.3 us: per_device(): totals = jnp.sum(weights, axis=2)]
    ppermute x1 -> x32, waiting for transfers between devices: 2.29 us -> 32.3 us  [the longest x1 6.29 us: per_device(): lax.ppermute(fifth_out, pair, traded(0, 1))]
  transfers between devices with their start and end apart: 5 -> 33, of which waited for: 5 -> 12; matrix products, arithmetic and copies ran while one was open for 18% -> 3% of each run, Pallas kernels for 0% -> 22%
where the time goes in v3:
time: 194 us; the launch traced here: 192 us
  starting transfers between devices  67.9 us (35%)
  Pallas kernels  59 us (30%)
  waiting for transfers between devices  36 us (19%)
  between operations  15.3 us (8%)
  local copies, waits for them, and re-layouts  7.41 us (4%)
  other arithmetic  5.67 us (3%)
    pallas_call x2, Pallas kernels, attend(): pl.pallas_call(functools.partial(attend_body, heads=len(queries), parts=l...  33.3 us
    ppermute x4, starting transfers between devices, per_device(): lax.ppermute(near[step][:3], 'head', core_swap)  27.2 us
    pallas_call x2, Pallas kernels, project(): pl.pallas_call(functools.partial(project_body, steps=steps), grid_spec=pl...  14.9 us
    ppermute x4, starting transfers between devices, per_device(): lax.ppermute(part, 'head', core_swap)  9.47 us
    ppermute x4, starting transfers between devices, per_device(): lax.ppermute(message, pair, traded(step))  7.4 us
    ppermute x1, waiting for transfers between devices, per_device(): lax.ppermute(fifth_out, pair, traded(0, 1))  6.29 us
    pallas_call x1, Pallas kernels, pack(): pl.pallas_call(functools.partial(pack_body, heads=heads), grid_spec=pltpu...  5.79 us
    ppermute x4, waiting for transfers between devices, per_device(): lax.ppermute(message, pair, traded(step))  5.39 us
  transfers between devices with their start and end apart: 33, of which 12 were waited for; matrix products, arithmetic and copies ran while one was open for 3% of the time, Pallas kernels for 22%

profile of v3, /device:TPU:0, one launch (start us, length us, event | category | flops | bytes accessed | tf_op | source)
XLA Modules:
  0.0 191.9 jit_solution(16164940860104878111)
XLA Ops:
  7.9 5.8 %shard_map.131 = (bf16[3,768,128]{2,1,0:T(8,128)(2,1)}, bf16[3,768,128]{2,1,0:T(8,128)(2,1)}, bf16[3,768,128]{2,1,0:T(8,128)(2,1)}, bf16[6,768,128]{2,1,0:T(8,128)(2,1)}) custom-call(s32[4]{0:T(128)} %pad_add_fusion.place, bf16[768,640]{1,0:T(8,128)(2,1)} %bitcast.45, bf16[768,640]{1,0:T(8,128)(2,1)} %bitcast.46, bf16[768,640]{1,0:T(8,128)(2,1)} %bitcast.47), custom_call_target="tpu_custom_call" | custom-call | tf_op jit(solution)/shard_map/pallas_call | solution.py:71
  13.7 2.3 %constant_dynamic-slice_fusion = bf16[640,2560]{1,0:T(8,128)(2,1)S(1)} fusion(bf16[640,5120]{1,0:T(8,128)(2,1)} %refs_10_.3, s32[]{:T(128)S(6)} %select_n.43), kind=kLoop, calls=%fused_computation.32 | loop fusion | bytes 6553604 | tf_op jit(solution)/shard_map/dynamic_slice | solution.py:329
  16.9 2.1 %collective-permute-start.1 = (bf16[3,768,128]{2,1,0:T(8,128)(2,1)S(1)}, bf16[3,768,128]{2,1,0:T(8,128)(2,1)S(1)}, u32[]{:S(2)}, u32[]{:S(2)}) collective-permute-start(bf16[3,768,128]{2,1,0:T(8,128)(2,1)S(1)} %copy-done.30), channel_id=1, source_target_pairs={{0,16},{1,24},{2,18},{3,26},{4,20},{5,28},{6,22},{7,30},{8,17},{9,... | collective-permute-start | bytes 1769480 | tf_op jit(solution)/shard_map/ppermute | solution.py:326
  18.9 3.6 %collective-permute-start.2 = (bf16[3,768,128]{2,1,0:T(8,128)(2,1)S(1)}, bf16[3,768,128]{2,1,0:T(8,128)(2,1)S(1)}, u32[]{:S(2)}, u32[]{:S(2)}) collective-permute-start(bf16[3,768,128]{2,1,0:T(8,128)(2,1)S(1)} %copy-done.29), channel_id=1, source_target_pairs={{0,32},{1,40},{2,34},{3,42},{4,36},{5,44},{6,38},{7,46},{8,33},{9,... | collective-permute-start | bytes 1769480 | tf_op jit(solution)/shard_map/ppermute | solution.py:326
  23.5 5.4 %collective-permute-done.1.refs_0_.refs_4_.refs_12_ = bf16[3,768,128]{2,1,0:T(8,128)(2,1)S(1)} collective-permute-done((bf16[3,768,128]{2,1,0:T(8,128)(2,1)S(1)}, bf16[3,768,128]{2,1,0:T(8,128)(2,1)S(1)}, u32[]{:S(2)}, u32[]{:S(2)}) %collective-permute-start.1) | collective-permute-done | bytes 589856 | tf_op jit(solution)/shard_map/ppermute | solution.py:326
  28.9 16.7 %collective-permute-start.5 = (bf16[3,768,128]{2,1,0:T(8,128)(2,1)S(1)}, bf16[3,768,128]{2,1,0:T(8,128)(2,1)S(1)}, u32[]{:S(2)}, u32[]{:S(2)}) collective-permute-start(bf16[3,768,128]{2,1,0:T(8,128)(2,1)S(1)} %collective-permute-done.1.refs_0_.refs_4_.refs_12_), channel_id=1, source_target_pairs={{0,1},{1,0},{2,3},{3,2},{4,5},{5,4},{6,7},{7,6},{8,9},{9,8},{10,11... | collective-permute-start | bytes 1769480 | tf_op jit(solution)/shard_map/ppermute | solution.py:331
  45.7 6.2 %collective-permute-start.6 = (bf16[3,768,128]{2,1,0:T(8,128)(2,1)S(1)}, bf16[3,768,128]{2,1,0:T(8,128)(2,1)S(1)}, u32[]{:S(2)}, u32[]{:S(2)}) collective-permute-start(bf16[3,768,128]{2,1,0:T(8,128)(2,1)S(1)} %collective-permute-done.2.refs_2_.refs_6_.refs_14_), channel_id=1, source_target_pairs={{0,1},{1,0},{2,3},{3,2},{4,5},{5,4},{6,7},{7,6},{8,9},{9,8},{10,11... | collective-permute-start | bytes 1769480 | tf_op jit(solution)/shard_map/ppermute | solution.py:331
  51.8 4.2 %collective-permute-start.7 = (bf16[3,768,128]{2,1,0:T(8,128)(2,1)S(1)}, bf16[3,768,128]{2,1,0:T(8,128)(2,1)S(1)}, u32[]{:S(2)}, u32[]{:S(2)}) collective-permute-start(bf16[3,768,128]{2,1,0:T(8,128)(2,1)S(1)} %collective-permute-done.3.refs_1_.refs_5_.refs_13_), channel_id=1, source_target_pairs={{0,1},{1,0},{2,3},{3,2},{4,5},{5,4},{6,7},{7,6},{8,9},{9,8},{10,11... | collective-permute-start | bytes 1769480 | tf_op jit(solution)/shard_map/ppermute | solution.py:331
  59.5 24.9 %shard_map.132 = (bf16[768,128]{1,0:T(8,128)(2,1)}, bf16[768,128]{1,0:T(8,128)(2,1)}, bf16[768,128]{1,0:T(8,128)(2,1)}, bf16[768,128]{1,0:T(8,128)(2,1)}) custom-call(bf16[3,768,128]{2,1,0:T(8,128)(2,1)} %copy-done.2, bf16[3,768,128]{2,1,0:T(8,128)(2,1)} %copy-done.4, bf16[3,768,128]{2,1,0:T(8,128)(2,1)} %copy-done.3, bf16[6,768,128]{2,1,0:T(8,128)(2,1)} %copy-done, ...), custom_call_target="tpu_custom_call" | custom-call | flops 1000 | bytes 1000 | tf_op jit(solution)/shard_map/pallas_call | solution.py:147
  84.4 3.7 %all-gather.2.cloned.1.call-done.refs_1_.refs_3_ = bf16[2,3072,128]{2,1,0:T(8,128)(2,1)} async-done(((bf16[2,768,128]{2,1,0:T(8,128)(2,1)}), bf16[2,3072,128]{2,1,0:T(8,128)(2,1)}) %all-gather.2.cloned.1.call-update) | async-done | bytes 1572880 | tf_op jit(solution)/shard_map/all_gather | solution.py:333
  94.1 8.4 %shard_map.133 = bf16[768,128]{1,0:T(8,128)(2,1)} custom-call(bf16[6,768,128]{2,1,0:T(8,128)(2,1)} %copy-done, bf16[2,3072,128]{2,1,0:T(8,128)(2,1)} %all-gather.2.cloned.1.call-done.refs_1_.refs_3_, bf16[2,3072,128]{2,1,0:T(8,128)(2,1)} %copy-done.1, bf16[2,3072,128]{2,1,0:T(8,128)(2,1)} %all-gather.2.cloned.1.call-done.refs_1_.refs_3_, ...), custom_call_target="tpu_custom_call" | custom-call | flops 1000 | bytes 1000 | tf_op jit(solution)/shard_map/pallas_call | solution.py:147
  104.2 8.9 %collective-permute-start.15 = (bf16[768,128]{1,0:T(8,128)(2,1)S(1)}, bf16[768,128]{1,0:T(8,128)(2,1)S(1)}, u32[]{:S(2)}, u32[]{:S(2)}) collective-permute-start(bf16[768,128]{1,0:T(8,128)(2,1)S(1)} %collective-permute-done.9.refs_0_), channel_id=1, source_target_pairs={{0,1},{1,0},{2,3},{3,2},{4,5},{5,4},{6,7},{7,6},{8,9},{9,8},{10,11... | collective-permute-start | bytes 589832 | tf_op jit(solution)/shard_map/ppermute | solution.py:356
  113.6 3.5 %collective-permute-start.19 = (bf16[768,128]{1,0:T(8,128)(2,1)}, bf16[768,128]{1,0:T(8,128)(2,1)S(1)}, u32[]{:S(2)}, u32[]{:S(2)}) collective-permute-start(bf16[768,128]{1,0:T(8,128)(2,1)} %shard_map.133), channel_id=1, source_target_pairs={{0,1},{1,9},{2,3},{3,11},{4,5},{5,13},{6,7},{7,15},{8,0},{9,8},{10... | collective-permute-start | bytes 589832 | tf_op jit(solution)/shard_map/ppermute | solution.py:357
  117.2 6.3 %collective-permute-done.19.refs_9_ = bf16[768,128]{1,0:T(8,128)(2,1)S(1)} collective-permute-done((bf16[768,128]{1,0:T(8,128)(2,1)}, bf16[768,128]{1,0:T(8,128)(2,1)S(1)}, u32[]{:S(2)}, u32[]{:S(2)}) %collective-permute-start.19) | collective-permute-done | bytes 196640 | tf_op jit(solution)/shard_map/ppermute | solution.py:357
  124.2 5.8 %shard_map.134 = (bf16[96,2560]{1,0:T(8,128)(2,1)}, bf16[96,2560]{1,0:T(8,128)(2,1)}) custom-call(s32[4]{0:T(128)} %pad_add_fusion.place, bf16[768,128]{1,0:T(8,128)(2,1)} %copy-done.12, bf16[768,128]{1,0:T(8,128)(2,1)} %copy-done.9, bf16[768,128]{1,0:T(8,128)(2,1)} %copy-done.10, bf16[768,128]{1,0:T(8,128)(2,1)} %copy-done.11, bf16[768,128]{1,0:T(8,128)(2,1)} %copy-done.13, ...), custom_call_target="tpu_custom_call" | custom-call | flops 1000 | bytes 1000 | tf_op jit(solution)/shard_map/pallas_call | solution.py:198
  130.1 2.7 %collective-permute-start.24 = (bf16[96,2560]{1,0:T(8,128)(2,1)}, bf16[96,2560]{1,0:T(8,128)(2,1)S(1)}, u32[]{:S(2)}, u32[]{:S(2)}) collective-permute-start(bf16[96,2560]{1,0:T(8,128)(2,1)} %get-tuple-element.87), channel_id=1, source_target_pairs={{0,6},{1,7},{2,0},{3,1},{4,2},{5,3},{6,4},{7,5},{8,14},{9,15},{10,... | collective-permute-start | bytes 1474568 | tf_op jit(solution)/shard_map/ppermute | solution.py:364
  132.8 9.0 %shard_map.135 = (f32[96,2560]{1,0:T(8,128)}, bf16[96,2560]{1,0:T(8,128)(2,1)}, bf16[96,2560]{1,0:T(8,128)(2,1)}, f32[96,2560]{1,0:T(8,128)}, f32[96,2560]{1,0:T(8,128)}, /*index=5*/f32[96,2560]{1,0:T(8,128)}) custom-call(s32[4]{0:T(128)} %pad_add_fusion.place, bf16[768,128]{1,0:T(8,128)(2,1)} %copy-done.12, bf16[768,128]{1,0:T(8,128)(2,1)} %copy-done.9, ...), custom_call_target="tpu_custom_call" | custom-call | flops 1000 | bytes 1000 | tf_op jit(solution)/shard_map/pallas_call | solution.py:198
  142.7 2.5 %collective-permute-start.23 = (bf16[96,2560]{1,0:T(8,128)(2,1)}, bf16[96,2560]{1,0:T(8,128)(2,1)S(1)}, u32[]{:S(2)}, u32[]{:S(2)}) collective-permute-start(bf16[96,2560]{1,0:T(8,128)(2,1)} %get-tuple-element.102), channel_id=1, source_target_pairs={{0,6},{1,7},{2,0},{3,1},{4,2},{5,3},{6,4},{7,5},{8,14},{9,15},{10,... | collective-permute-start | bytes 1474568 | tf_op jit(solution)/shard_map/ppermute | solution.py:371
  146.5 2.2 %collective-permute-start.25 = (bf16[96,2560]{1,0:T(8,128)(2,1)S(1)}, bf16[96,2560]{1,0:T(8,128)(2,1)S(1)}, u32[]{:S(2)}, u32[]{:S(2)}) collective-permute-start(bf16[96,2560]{1,0:T(8,128)(2,1)S(1)} %add_convert_fusion), channel_id=1, source_target_pairs={{0,6},{1,7},{2,0},{3,1},{4,2},{5,3},{6,4},{7,5},{8,14},{9,15},{10,... | collective-permute-start | bytes 1474568 | tf_op jit(solution)/shard_map/ppermute | solution.py:375
  153.0 4.5 %collective-permute-done.22.refs_3_ = bf16[96,2560]{1,0:T(8,128)(2,1)S(1)} collective-permute-done((bf16[96,2560]{1,0:T(8,128)(2,1)}, bf16[96,2560]{1,0:T(8,128)(2,1)S(1)}, u32[]{:S(2)}, u32[]{:S(2)}) %collective-permute-start.22) | collective-permute-done | bytes 491552 | tf_op jit(solution)/shard_map/ppermute | solution.py:370
  157.5 5.1 %collective-permute-done.25.refs_5_ = bf16[96,2560]{1,0:T(8,128)(2,1)S(1)} collective-permute-done((bf16[96,2560]{1,0:T(8,128)(2,1)S(1)}, bf16[96,2560]{1,0:T(8,128)(2,1)S(1)}, u32[]{:S(2)}, u32[]{:S(2)}) %collective-permute-start.25) | collective-permute-done | bytes 491552 | tf_op jit(solution)/shard_map/ppermute | solution.py:375
  165.4 5.0 %shard_map.136 = (f32[40,192]{1,0:T(8,128)}, f32[40,192]{1,0:T(8,128)}) custom-call(s32[4]{0:T(128)} %pad_add_fusion.place, f32[96,2560]{1,0:T(8,128)} %get-tuple-element.98.refs_0_, f32[96,2560]{1,0:T(8,128)} %get-tuple-element.99.refs_1_, bf16[96,2560]{1,0:T(8,128)(2,1)} %copy-done.22, bf16[96,2560]{1,0:T(8,128)(2,1)} %copy-done.19, ...), custom_call_target="tpu_custom_call" | custom-call | flops 377487360 | bytes 5898240 | tf_op jit(solution)/shard_map/pallas_call | solution.py:268
  172.7 2.1 %collective-permute-done.26 = f32[40,192]{1,0:T(8,128)S(1)} collective-permute-done((f32[40,192]{1,0:T(8,128)}, f32[40,192]{1,0:T(8,128)S(1)}, u32[]{:S(2)}, u32[]{:S(2)}) %collective-permute-start.26) | collective-permute-done | bytes 30752 | tf_op jit(solution)/shard_map/ppermute | solution.py:382
  180.7 3.4 %collective-permute-done.30 = f32[32,192]{1,0:T(8,128)S(1)} collective-permute-done((f32[32,192]{1,0:T(8,128)S(1)}, f32[32,192]{1,0:T(8,128)S(1)}, u32[]{:S(2)}, u32[]{:S(2)}) %collective-permute-start.30) | collective-permute-done | bytes 24608 | tf_op jit(solution)/shard_map/ppermute | solution.py:401
  (126 shorter events, 32.3 us)
Async XLA Ops:
  7.2 81.0 %all-gather.2.cloned.1.call-start = ((), (), s32[]{:S(2)}) async-start(), calls=%async_computation | async-start | bytes 1966080 | tf_op jit(solution)/shard_map/all_gather | solution.py:333
  16.0 42.6 %collective-permute-start.8 = (bf16[640,2560]{1,0:T(8,128)(2,1)S(1)}, bf16[640,2560]{1,0:T(8,128)(2,1)}, u32[]{:S(2)}, u32[]{:S(2)}) collective-permute-start(bf16[640,2560]{1,0:T(8,128)(2,1)S(1)} %constant_dynamic-slice_fusion), channel_id=1, source_target_pairs={{0,1},{1,0},{2,3},{3,2},{4,5},{5,4},{6,7},{7,6},{8,9},{9,8},{10,11... | collective-permute-start | bytes 9830408 | tf_op jit(solution)/shard_map/ppermute | solution.py:328
  16.1 39.9 %collective-permute-start = (bf16[6,768,128]{2,1,0:T(8,128)(2,1)S(1)}, bf16[6,768,128]{2,1,0:T(8,128)(2,1)S(1)}, u32[]{:S(2)}, u32[]{:S(2)}) collective-permute-start(bf16[6,768,128]{2,1,0:T(8,128)(2,1)S(1)} %copy-done.27), channel_id=1, source_target_pairs={{0,0},{1,8},{2,2},{3,10},{4,4},{5,12},{6,6},{7,14},{8,1},{9,9},{10... | collective-permute-start | bytes 3538952 | tf_op jit(solution)/shard_map/ppermute | solution.py:326
  16.9 12.1 %collective-permute-start.1 = (bf16[3,768,128]{2,1,0:T(8,128)(2,1)S(1)}, bf16[3,768,128]{2,1,0:T(8,128)(2,1)S(1)}, u32[]{:S(2)}, u32[]{:S(2)}) collective-permute-start(bf16[3,768,128]{2,1,0:T(8,128)(2,1)S(1)} %copy-done.30), channel_id=1, source_target_pairs={{0,16},{1,24},{2,18},{3,26},{4,20},{5,28},{6,22},{7,30},{8,17},{9,... | collective-permute-start | bytes 1769480 | tf_op jit(solution)/shard_map/ppermute | solution.py:326
  18.9 26.7 %collective-permute-start.2 = (bf16[3,768,128]{2,1,0:T(8,128)(2,1)S(1)}, bf16[3,768,128]{2,1,0:T(8,128)(2,1)S(1)}, u32[]{:S(2)}, u32[]{:S(2)}) collective-permute-start(bf16[3,768,128]{2,1,0:T(8,128)(2,1)S(1)} %copy-done.29), channel_id=1, source_target_pairs={{0,32},{1,40},{2,34},{3,42},{4,36},{5,44},{6,38},{7,46},{8,33},{9,... | collective-permute-start | bytes 1769480 | tf_op jit(solution)/shard_map/ppermute | solution.py:326
  22.5 29.3 %collective-permute-start.3 = (bf16[3,768,128]{2,1,0:T(8,128)(2,1)S(1)}, bf16[3,768,128]{2,1,0:T(8,128)(2,1)S(1)}, u32[]{:S(2)}, u32[]{:S(2)}) collective-permute-start(bf16[3,768,128]{2,1,0:T(8,128)(2,1)S(1)} %copy-done.28), channel_id=1, source_target_pairs={{0,48},{1,56},{2,50},{3,58},{4,52},{5,60},{6,54},{7,62},{8,49},{9,... | collective-permute-start | bytes 1769480 | tf_op jit(solution)/shard_map/ppermute | solution.py:326
  28.9 27.3 %collective-permute-start.5 = (bf16[3,768,128]{2,1,0:T(8,128)(2,1)S(1)}, bf16[3,768,128]{2,1,0:T(8,128)(2,1)S(1)}, u32[]{:S(2)}, u32[]{:S(2)}) collective-permute-start(bf16[3,768,128]{2,1,0:T(8,128)(2,1)S(1)} %collective-permute-done.1.refs_0_.refs_4_.refs_12_), channel_id=1, source_target_pairs={{0,1},{1,0},{2,3},{3,2},{4,5},{5,4},{6,7},{7,6},{8,9},{9,8},{10,11... | collective-permute-start | bytes 1769480 | tf_op jit(solution)/shard_map/ppermute | solution.py:331
  45.7 10.5 %collective-permute-start.6 = (bf16[3,768,128]{2,1,0:T(8,128)(2,1)S(1)}, bf16[3,768,128]{2,1,0:T(8,128)(2,1)S(1)}, u32[]{:S(2)}, u32[]{:S(2)}) collective-permute-start(bf16[3,768,128]{2,1,0:T(8,128)(2,1)S(1)} %collective-permute-done.2.refs_2_.refs_6_.refs_14_), channel_id=1, source_target_pairs={{0,1},{1,0},{2,3},{3,2},{4,5},{5,4},{6,7},{7,6},{8,9},{9,8},{10,11... | collective-permute-start | bytes 1769480 | tf_op jit(solution)/shard_map/ppermute | solution.py:331
  51.8 5.9 %collective-permute-start.7 = (bf16[3,768,128]{2,1,0:T(8,128)(2,1)S(1)}, bf16[3,768,128]{2,1,0:T(8,128)(2,1)S(1)}, u32[]{:S(2)}, u32[]{:S(2)}) collective-permute-start(bf16[3,768,128]{2,1,0:T(8,128)(2,1)S(1)} %collective-permute-done.3.refs_1_.refs_5_.refs_13_), channel_id=1, source_target_pairs={{0,1},{1,0},{2,3},{3,2},{4,5},{5,4},{6,7},{7,6},{8,9},{9,8},{10,11... | collective-permute-start | bytes 1769480 | tf_op jit(solution)/shard_map/ppermute | solution.py:331
  88.2 14.3 %collective-permute-start.10 = (bf16[768,128]{1,0:T(8,128)(2,1)}, bf16[768,128]{1,0:T(8,128)(2,1)S(1)}, u32[]{:S(2)}, u32[]{:S(2)}) collective-permute-start(bf16[768,128]{1,0:T(8,128)(2,1)} %get-tuple-element.76), channel_id=1, source_target_pairs={{0,48},{1,56},{2,50},{3,58},{4,52},{5,60},{6,54},{7,62},{8,49},{9,... | collective-permute-start | bytes 589832 | tf_op jit(solution)/shard_map/ppermute | solution.py:344
  89.8 12.7 %collective-permute-start.11 = (bf16[768,128]{1,0:T(8,128)(2,1)}, bf16[768,128]{1,0:T(8,128)(2,1)S(1)}, u32[]{:S(2)}, u32[]{:S(2)}) collective-permute-start(bf16[768,128]{1,0:T(8,128)(2,1)} %get-tuple-element.77), channel_id=1, source_target_pairs={{0,32},{1,40},{2,34},{3,42},{4,36},{5,44},{6,38},{7,46},{8,33},{9,... | collective-permute-start | bytes 589832 | tf_op jit(solution)/shard_map/ppermute | solution.py:344
  90.7 11.9 %collective-permute-start.12 = (bf16[768,128]{1,0:T(8,128)(2,1)}, bf16[768,128]{1,0:T(8,128)(2,1)S(1)}, u32[]{:S(2)}, u32[]{:S(2)}) collective-permute-start(bf16[768,128]{1,0:T(8,128)(2,1)} %get-tuple-element.78), channel_id=1, source_target_pairs={{0,16},{1,24},{2,18},{3,26},{4,20},{5,28},{6,22},{7,30},{8,17},{9,... | collective-permute-start | bytes 589832 | tf_op jit(solution)/shard_map/ppermute | solution.py:344
  91.4 11.2 %collective-permute-start.9 = (bf16[768,128]{1,0:T(8,128)(2,1)}, bf16[768,128]{1,0:T(8,128)(2,1)S(1)}, u32[]{:S(2)}, u32[]{:S(2)}) collective-permute-start(bf16[768,128]{1,0:T(8,128)(2,1)} %get-tuple-element.75), channel_id=1, source_target_pairs={{0,0},{1,8},{2,2},{3,10},{4,4},{5,12},{6,6},{7,14},{8,1},{9,9},{10... | collective-permute-start | bytes 589832 | tf_op jit(solution)/shard_map/ppermute | solution.py:344
  102.6 11.1 %collective-permute-start.14 = (bf16[768,128]{1,0:T(8,128)(2,1)}, bf16[768,128]{1,0:T(8,128)(2,1)S(1)}, u32[]{:S(2)}, u32[]{:S(2)}) collective-permute-start(bf16[768,128]{1,0:T(8,128)(2,1)} %shard_map.133), channel_id=1, source_target_pairs={{0,0},{1,8},{2,2},{3,10},{4,4},{5,12},{6,6},{7,14},{8,1},{9,9},{10... | collective-permute-start | bytes 589832 | tf_op jit(solution)/shard_map/ppermute | solution.py:355
  104.2 13.0 %collective-permute-start.15 = (bf16[768,128]{1,0:T(8,128)(2,1)S(1)}, bf16[768,128]{1,0:T(8,128)(2,1)S(1)}, u32[]{:S(2)}, u32[]{:S(2)}) collective-permute-start(bf16[768,128]{1,0:T(8,128)(2,1)S(1)} %collective-permute-done.9.refs_0_), channel_id=1, source_target_pairs={{0,1},{1,0},{2,3},{3,2},{4,5},{5,4},{6,7},{7,6},{8,9},{9,8},{10,11... | collective-permute-start | bytes 589832 | tf_op jit(solution)/shard_map/ppermute | solution.py:356
  113.6 9.8 %collective-permute-start.19 = (bf16[768,128]{1,0:T(8,128)(2,1)}, bf16[768,128]{1,0:T(8,128)(2,1)S(1)}, u32[]{:S(2)}, u32[]{:S(2)}) collective-permute-start(bf16[768,128]{1,0:T(8,128)(2,1)} %shard_map.133), channel_id=1, source_target_pairs={{0,1},{1,9},{2,3},{3,11},{4,5},{5,13},{6,7},{7,15},{8,0},{9,8},{10... | collective-permute-start | bytes 589832 | tf_op jit(solution)/shard_map/ppermute | solution.py:357
  130.1 15.2 %collective-permute-start.24 = (bf16[96,2560]{1,0:T(8,128)(2,1)}, bf16[96,2560]{1,0:T(8,128)(2,1)S(1)}, u32[]{:S(2)}, u32[]{:S(2)}) collective-permute-start(bf16[96,2560]{1,0:T(8,128)(2,1)} %get-tuple-element.87), channel_id=1, source_target_pairs={{0,6},{1,7},{2,0},{3,1},{4,2},{5,3},{6,4},{7,5},{8,14},{9,15},{10,... | collective-permute-start | bytes 1474568 | tf_op jit(solution)/shard_map/ppermute | solution.py:364
  132.8 16.0 %collective-permute-start.20 = (bf16[96,2560]{1,0:T(8,128)(2,1)}, bf16[96,2560]{1,0:T(8,128)(2,1)S(1)}, u32[]{:S(2)}, u32[]{:S(2)}) collective-permute-start(bf16[96,2560]{1,0:T(8,128)(2,1)} %get-tuple-element.86), channel_id=1, source_target_pairs={{0,2},{1,3},{2,4},{3,5},{4,6},{5,7},{6,0},{7,1},{8,10},{9,11},{10,... | collective-permute-start | bytes 1474568 | tf_op jit(solution)/shard_map/ppermute | solution.py:363
  141.9 15.7 %collective-permute-start.22 = (bf16[96,2560]{1,0:T(8,128)(2,1)}, bf16[96,2560]{1,0:T(8,128)(2,1)S(1)}, u32[]{:S(2)}, u32[]{:S(2)}) collective-permute-start(bf16[96,2560]{1,0:T(8,128)(2,1)} %get-tuple-element.101), channel_id=1, source_target_pairs={{0,2},{1,3},{2,4},{3,5},{4,6},{5,7},{6,0},{7,1},{8,10},{9,11},{10,... | collective-permute-start | bytes 1474568 | tf_op jit(solution)/shard_map/ppermute | solution.py:370
  142.7 14.8 %collective-permute-start.23 = (bf16[96,2560]{1,0:T(8,128)(2,1)}, bf16[96,2560]{1,0:T(8,128)(2,1)S(1)}, u32[]{:S(2)}, u32[]{:S(2)}) collective-permute-start(bf16[96,2560]{1,0:T(8,128)(2,1)} %get-tuple-element.102), channel_id=1, source_target_pairs={{0,6},{1,7},{2,0},{3,1},{4,2},{5,3},{6,4},{7,5},{8,14},{9,15},{10,... | collective-permute-start | bytes 1474568 | tf_op jit(solution)/shard_map/ppermute | solution.py:371
  146.5 16.1 %collective-permute-start.25 = (bf16[96,2560]{1,0:T(8,128)(2,1)S(1)}, bf16[96,2560]{1,0:T(8,128)(2,1)S(1)}, u32[]{:S(2)}, u32[]{:S(2)}) collective-permute-start(bf16[96,2560]{1,0:T(8,128)(2,1)S(1)} %add_convert_fusion), channel_id=1, source_target_pairs={{0,6},{1,7},{2,0},{3,1},{4,2},{5,3},{6,4},{7,5},{8,14},{9,15},{10,... | collective-permute-start | bytes 1474568 | tf_op jit(solution)/shard_map/ppermute | solution.py:375
  150.8 13.8 %collective-permute-start.21 = (bf16[96,2560]{1,0:T(8,128)(2,1)}, bf16[96,2560]{1,0:T(8,128)(2,1)S(1)}, u32[]{:S(2)}, u32[]{:S(2)}) collective-permute-start(bf16[96,2560]{1,0:T(8,128)(2,1)} %add_convert_fusion.1), channel_id=1, source_target_pairs={{0,2},{1,3},{2,4},{3,5},{4,6},{5,7},{6,0},{7,1},{8,10},{9,11},{10,... | collective-permute-start | bytes 1474568 | tf_op jit(solution)/shard_map/ppermute | solution.py:374
  178.5 5.5 %collective-permute-start.30 = (f32[32,192]{1,0:T(8,128)S(1)}, f32[32,192]{1,0:T(8,128)S(1)}, u32[]{:S(2)}, u32[]{:S(2)}) collective-permute-start(f32[32,192]{1,0:T(8,128)S(1)} %fusion.10), channel_id=1, source_target_pairs={{0,4},{1,5},{2,6},{3,7},{4,0},{5,1},{6,2},{7,3},{8,12},{9,13},{10,... | collective-permute-start | bytes 73736 | tf_op jit(solution)/shard_map/ppermute | solution.py:401
  178.7 5.5 %collective-permute-start.31 = (f32[32,192]{1,0:T(8,128)S(1)}, f32[32,192]{1,0:T(8,128)S(1)}, u32[]{:S(2)}, u32[]{:S(2)}) collective-permute-start(f32[32,192]{1,0:T(8,128)S(1)} %fusion.10), channel_id=1, source_target_pairs={{0,2},{1,3},{2,4},{3,5},{4,6},{5,7},{6,0},{7,1},{8,10},{9,11},{10,... | collective-permute-start | bytes 73736 | tf_op jit(solution)/shard_map/ppermute | solution.py:401
  (40 other events, 322.5 us)
Sparse Core Ops, SparseCore 0:
  59.6 28.5 all-gather.1

commit v4 on v3

--- a/solution.py
+++ b/solution.py
@@ -25,12 +25,9 @@
 both_swap = [(n, n ^ (HEAD + 1)) for n in range(2 * HEAD)]
 
 
-def traded(step, flip=0):
+def traded(step):
     return [
-        (
-            (z * YH + y) * HEAD + x * CORE + c,
-            ((z + step) % Z * YH + c) * HEAD + x * CORE + (y + flip) % CORE,
-        )
+        ((z * YH + y) * HEAD + x * CORE + c, ((z + step) % Z * YH + c) * HEAD + x * CORE + y)
         for z in range(Z)
         for y in range(YH)
         for x in range(X)
@@ -47,41 +44,32 @@
     return flow_shift / (1.0 + (flow_shift - 1.0) * moment) ** 2
 
 
-def pack_body(place, *refs, heads):
+def pack_body(place, *refs):
     sources, outs = refs[:3], refs[3:]
-    number = 0
-    for out, count in zip(outs, heads):
-        for head in range(count):
-
-            @pl.when(pl.program_id(0) == number)
-            def _(out=out, head=head):
-                for kind, source in enumerate(sources):
-                    out[3 * head + kind] = source[...]
-
-            number += 1
-
-
-def pack(place, sources, steps, heads):
+    for number, out in enumerate(outs):
+
+        @pl.when(pl.program_id(0) == number)
+        def _(out=out):
+            for kind, source in enumerate(sources):
+                out[kind] = source[...]
+
+
+def pack(place, sources, steps):
     tokens = sources[0].shape[0]
 
     def column(i, place):
         step = sum(jnp.where(i == n, step, 0) for n, step in enumerate(steps))
-        return 0, jnp.where(i < len(steps), (place[3] + step) % Z, Z)
+        return 0, (place[3] + step) % Z
 
     return pl.pallas_call(
-        functools.partial(pack_body, heads=heads),
+        pack_body,
         grid_spec=pltpu.PrefetchScalarGridSpec(
             num_scalar_prefetch=1,
-            grid=(sum(heads),),
+            grid=(len(steps),),
             in_specs=[pl.BlockSpec((tokens, HSIZE), column)] * len(sources),
-            out_specs=[
-                pl.BlockSpec((3 * count, tokens, HSIZE), lambda i, place: (0, 0, 0))
-                for count in heads
-            ],
+            out_specs=[pl.BlockSpec((3, tokens, HSIZE), lambda i, place: (0, 0, 0))] * len(steps),
         ),
-        out_shape=[
-            jax.ShapeDtypeStruct((3 * count, tokens, HSIZE), jnp.bfloat16) for count in heads
-        ],
+        out_shape=[jax.ShapeDtypeStruct((3, tokens, HSIZE), jnp.bfloat16)] * len(steps),
         compiler_params=pltpu.CompilerParams(vmem_limit_bytes=56 * 2**20),
     )(place, *sources)
 
@@ -141,16 +129,19 @@
 
 
 def attend(queries, keys, values, chunk=3072):
-    rows = queries[0][0].shape[1]
+    rows = queries[0][0].shape[-2]
     tokens = sum(part.shape[1] for part, _ in keys)
     operands = (*queries, *keys, *values)
+
+    def block(array, index):
+        if array.ndim == 2:
+            return pl.BlockSpec((array.shape[0], HSIZE), lambda i: (0, index))
+        return pl.BlockSpec((pl.squeezed, array.shape[1], HSIZE), lambda i: (index, 0, 0))
+
     return pl.pallas_call(
         functools.partial(attend_body, heads=len(queries), parts=len(keys), chunk=chunk),
         grid=(len(queries),),
-        in_specs=[
-            pl.BlockSpec((pl.squeezed, array.shape[1], HSIZE), lambda i, index=index: (index, 0, 0))
-            for array, index in operands
-        ],
+        in_specs=[block(*operand) for operand in operands],
         out_specs=[pl.BlockSpec((rows, HSIZE), lambda i: (0, 0))] * len(queries),
         out_shape=[jax.ShapeDtypeStruct((rows, HSIZE), jnp.bfloat16)] * len(queries),
         scratch_shapes=[
@@ -164,20 +155,19 @@
 
 
 def project_body(place, *refs, steps):
-    operands, own_weight, other_weight, outs = refs[: 2 * Z + 2], *refs[2 * Z + 2 :][:2], refs[2 * Z + 4 : -2]
+    count = (2 * Z + 2) * len(steps)
+    operands, own_weight, other_weight, outs = refs[:count], *refs[count:][:2], refs[count + 2 : -2]
     rows, weight = refs[-2:]
     share = rows.shape[0] // len(steps)
     depth = own_weight.shape[0]
 
     @pl.when(pl.program_id(0) == 0)
     def _():
-        for index, step in enumerate(steps):
-            start = pl.multiple_of((place[0] + step) % X * share, share)
-            span = slice(index * share, (index + 1) * share)
-            for number, ref in enumerate(operands):
-                side, head = divmod(number, Z + 1)
-                at = side * depth + (spread(place, head) if head < Z else Z * HSIZE)
-                rows[span, pl.ds(at, HSIZE)] = ref[pl.ds(start, share), :]
+        for number, ref in enumerate(operands):
+            index, number = divmod(number, 2 * Z + 2)
+            side, head = divmod(number, Z + 1)
+            at = side * depth + (spread(place, head) if head < Z else Z * HSIZE)
+            rows[index * share : (index + 1) * share, pl.ds(at, HSIZE)] = ref[...]
 
     weight[:depth] = own_weight[...]
     weight[depth:] = other_weight[...]
@@ -193,15 +183,17 @@
 
 def project(place, attended, own_weight, other_weight, steps, kinds, height, tile=1280):
     depth, half = other_weight.shape
-    rows = attended[0].shape[0] // X * len(steps)
-    tiles = half // tile
+    share = attended[0].shape[0] // X
+    rows, tiles = share * len(steps), half // tile
     return pl.pallas_call(
         functools.partial(project_body, steps=steps),
         grid_spec=pltpu.PrefetchScalarGridSpec(
             num_scalar_prefetch=1,
             grid=(tiles,),
             in_specs=[
-                pl.BlockSpec(operand.shape, lambda i, place: (0, 0)) for operand in attended
+                pl.BlockSpec((share, HSIZE), lambda i, place, step=step: ((place[0] + step) % X, 0))
+                for step in steps
+                for _ in attended
             ]
             + [
                 pl.BlockSpec((depth, tile), lambda i, place: (0, place[1] * tiles + i)),
@@ -216,7 +208,7 @@
         out_shape=[jax.ShapeDtypeStruct((height, half), kind) for kind in kinds],
         compiler_params=pltpu.CompilerParams(vmem_limit_bytes=56 * 2**20),
         cost_estimate=pl.CostEstimate(flops=1000, bytes_accessed=1000, transcendentals=0),
-    )(place, *attended, own_weight, other_weight)
+    )(place, *(attended * len(steps)), own_weight, other_weight)
 
 
 def finish_body(place, *refs):
@@ -319,8 +311,10 @@
     place = jnp.stack([column, core, branch, z]).astype(jnp.int32)
     pair = "seq", "head"
 
+    fifth = jnp.stack([keys[:, Z * HSIZE :], values[:, Z * HSIZE :]])
+    fifth = lax.all_gather(fifth, "seq", axis=1, tiled=True)
     order = (1, 3, 2, 0)
-    messages = pack(place, (queries, keys, values), order, (1, 1, 1, 2))
+    messages = pack(place, (queries, keys, values), order)
     messages, weight = lax.optimization_barrier((messages, out_weight))
     near = {
         step: lax.ppermute(message, pair, traded(step)) for step, message in zip(order, messages)
@@ -328,33 +322,23 @@
     other_weight = lax.ppermute(
         lax.dynamic_slice_in_dim(weight, (1 - core) * half, half, 1), "head", core_swap
     )
-    far = {step: lax.ppermute(near[step][:3], "head", core_swap) for step in order}
+    far = {step: lax.ppermute(near[step], "head", core_swap) for step in order}
     near, far, other_weight = lax.optimization_barrier((near, far, other_weight))
-    fifth_near = lax.all_gather(
-        near[0][4:], "seq", axis=1, tiled=True, axis_index_groups=z_groups
-    )
     dealt = attend(
         [(near[step], 0) for step in order],
         [(side[step], 1) for side in (near, far) for step in order],
         [(side[step], 2) for side in (near, far) for step in order],
     )
-    fifth_near, dealt = lax.optimization_barrier((fifth_near, dealt))
-    fifth_far = lax.ppermute(fifth_near, "head", core_swap)
+    fifth_queries, dealt = lax.optimization_barrier((queries, dealt))
     back = {
         step: lax.ppermute(result, pair, traded(-step)) for step, result in zip(order, dealt)
     }
-    (fifth_out,) = attend(
-        [(near[0], 3)],
-        [(fifth_near, 0), (fifth_far, 0)],
-        [(fifth_near, 1), (fifth_far, 1)],
-    )
+    (fifth_out,) = attend([(fifth_queries, Z)], [(fifth, 0)], [(fifth, 1)])
     back, fifth_out = lax.optimization_barrier((back, fifth_out))
-    own_attended = [back[step] for step in range(Z)]
+    own_attended = [back[step] for step in range(Z)] + [fifth_out]
     attended = (
         *own_attended,
-        lax.ppermute(fifth_out, pair, traded(0)),
         *(lax.ppermute(part, "head", core_swap) for part in own_attended),
-        lax.ppermute(fifth_out, pair, traded(0, 1)),
     )
 
     wire, middle = jnp.bfloat16, share // 2

time: 194 us -> 180 us (0.928); the launches traced: 192 us -> 180 us
  starting transfers between devices: 67.9 us -> 49.1 us
  waiting for transfers between devices: 36 us -> 42.4 us
    ppermute x7 -> x4, starting transfers between devices: 32.3 us -> 20.5 us  [per_device(): far = {step: lax.ppermute(near[step], 'head', core_swap) for step in order}]
    ppermute x4 -> x5, starting transfers between devices: 9.47 us -> 1.32 us  [per_device(): lax.ppermute(part, 'head', core_swap)]
    ppermute x4, waiting for transfers between devices: 5.39 us -> 12.1 us  [per_device(): lax.ppermute(message, pair, traded(step))]
    ppermute x7 -> x4, waiting for transfers between devices: 8.72 us -> 2.31 us  [per_device(): far = {step: lax.ppermute(near[step], 'head', core_swap) for step in order}]
    ppermute x1, waiting for transfers between devices: 5.12 us -> 7.65 us  [per_device(): ahead_lower = lax.ppermute(backward, 'head', x_shift(3))]
  transfers between devices with their start and end apart: 33 -> 31, of which waited for: 12 -> 15; matrix products, arithmetic and copies ran while one was open for 3% -> 5% of each run, Pallas kernels for 22% -> 27%
where the time goes in v4:
time: 180 us
  Pallas kernels  59 us (33%)
  starting transfers between devices  49.1 us (27%)
  waiting for transfers between devices  42.4 us (24%)
  between operations  15.2 us (8%)
  local copies, waits for them, and re-layouts  7.38 us (4%)
  other arithmetic  6.44 us (4%)
    pallas_call x2, Pallas kernels, attend(): pl.pallas_call(functools.partial(attend_body, heads=len(queries), parts=l...  34.5 us
    ppermute x4, starting transfers between devices, per_device(): far = {step: lax.ppermute(near[step], 'head', core_swap) for step in order}  20.5 us
    pallas_call x2, Pallas kernels, project(): pl.pallas_call(functools.partial(project_body, steps=steps), grid_spec=pl...  14.7 us
    ppermute x4, waiting for transfers between devices, per_device(): lax.ppermute(message, pair, traded(step))  12.1 us
    ppermute x1, waiting for transfers between devices, per_device(): ahead_lower = lax.ppermute(backward, 'head', x_shift(3))  7.65 us
    ppermute x4, starting transfers between devices, per_device(): lax.ppermute(message, pair, traded(step))  7.36 us
    all_gather x1, waiting for transfers between devices, per_device(): fifth = lax.all_gather(fifth, 'seq', axis=1, tiled=True)  5.56 us
    ppermute x1, waiting for transfers between devices, per_device(): behind_lower = lax.ppermute(forward_lower, 'head', x_shift(1))  5.54 us
  transfers between devices with their start and end apart: 31, of which 15 were waited for; matrix products, arithmetic and copies ran while one was open for 5% of the time, Pallas kernels for 27%

profile of v4, /device:TPU:0, one launch (start us, length us, event | category | flops | bytes accessed | tf_op | source)
XLA Modules:
  0.0 180.1 jit_solution(17444843543070375711)
XLA Ops:
  9.7 4.7 %shard_map.131 = (bf16[3,768,128]{2,1,0:T(8,128)(2,1)}, bf16[3,768,128]{2,1,0:T(8,128)(2,1)}, bf16[3,768,128]{2,1,0:T(8,128)(2,1)}, bf16[3,768,128]{2,1,0:T(8,128)(2,1)}) custom-call(s32[4]{0:T(128)} %pad_add_fusion.place, bf16[768,640]{1,0:T(8,128)(2,1)} %bitcast.49, bf16[768,640]{1,0:T(8,128)(2,1)} %bitcast.52, bf16[768,640]{1,0:T(8,128)(2,1)} %bitcast.54), custom_call_target="tpu_custom_call" | custom-call | tf_op jit(solution)/shard_map/pallas_call | solution.py:64
  14.4 2.3 %constant_dynamic-slice_fusion = bf16[640,2560]{1,0:T(8,128)(2,1)S(1)} fusion(bf16[640,5120]{1,0:T(8,128)(2,1)} %refs_30_.1, s32[]{:T(128)S(6)} %select_n.43), kind=kLoop, calls=%fused_computation.35 | loop fusion | bytes 6553604 | tf_op jit(solution)/shard_map/dynamic_slice | solution.py:323
  17.6 2.1 %collective-permute-start.1 = (bf16[3,768,128]{2,1,0:T(8,128)(2,1)S(1)}, bf16[3,768,128]{2,1,0:T(8,128)(2,1)S(1)}, u32[]{:S(2)}, u32[]{:S(2)}) collective-permute-start(bf16[3,768,128]{2,1,0:T(8,128)(2,1)S(1)} %copy-done.29), channel_id=1, source_target_pairs={{0,16},{1,24},{2,18},{3,26},{4,20},{5,28},{6,22},{7,30},{8,17},{9,... | collective-permute-start | bytes 1769480 | tf_op jit(solution)/shard_map/ppermute | solution.py:320
  19.6 3.6 %collective-permute-start.2 = (bf16[3,768,128]{2,1,0:T(8,128)(2,1)S(1)}, bf16[3,768,128]{2,1,0:T(8,128)(2,1)S(1)}, u32[]{:S(2)}, u32[]{:S(2)}) collective-permute-start(bf16[3,768,128]{2,1,0:T(8,128)(2,1)S(1)} %copy-done.28), channel_id=1, source_target_pairs={{0,32},{1,40},{2,34},{3,42},{4,36},{5,44},{6,38},{7,46},{8,33},{9,... | collective-permute-start | bytes 1769480 | tf_op jit(solution)/shard_map/ppermute | solution.py:320
  24.2 10.3 %collective-permute-start.4 = (bf16[3,768,128]{2,1,0:T(8,128)(2,1)S(1)}, bf16[3,768,128]{2,1,0:T(8,128)(2,1)S(1)}, u32[]{:S(2)}, u32[]{:S(2)}) collective-permute-start(bf16[3,768,128]{2,1,0:T(8,128)(2,1)S(1)} %collective-permute-done.refs_3_.refs_7_.refs_15_), channel_id=1, source_target_pairs={{0,1},{1,0},{2,3},{3,2},{4,5},{5,4},{6,7},{7,6},{8,9},{9,8},{10,11... | collective-permute-start | bytes 1769480 | tf_op jit(solution)/shard_map/ppermute | solution.py:325
  34.5 9.7 %collective-permute-start.5 = (bf16[3,768,128]{2,1,0:T(8,128)(2,1)S(1)}, bf16[3,768,128]{2,1,0:T(8,128)(2,1)S(1)}, u32[]{:S(2)}, u32[]{:S(2)}) collective-permute-start(bf16[3,768,128]{2,1,0:T(8,128)(2,1)S(1)} %collective-permute-done.1.refs_0_.refs_4_.refs_12_), channel_id=1, source_target_pairs={{0,1},{1,0},{2,3},{3,2},{4,5},{5,4},{6,7},{7,6},{8,9},{9,8},{10,11... | collective-permute-start | bytes 1769480 | tf_op jit(solution)/shard_map/ppermute | solution.py:325
  44.3 12.1 %collective-permute-done.2.refs_2_.refs_6_.refs_14_ = bf16[3,768,128]{2,1,0:T(8,128)(2,1)S(1)} collective-permute-done((bf16[3,768,128]{2,1,0:T(8,128)(2,1)S(1)}, bf16[3,768,128]{2,1,0:T(8,128)(2,1)S(1)}, u32[]{:S(2)}, u32[]{:S(2)}) %collective-permute-start.2) | collective-permute-done | bytes 589856 | tf_op jit(solution)/shard_map/ppermute | solution.py:320
  60.1 26.1 %shard_map.132 = (bf16[768,128]{1,0:T(8,128)(2,1)}, bf16[768,128]{1,0:T(8,128)(2,1)}, bf16[768,128]{1,0:T(8,128)(2,1)}, bf16[768,128]{1,0:T(8,128)(2,1)}) custom-call(bf16[3,768,128]{2,1,0:T(8,128)(2,1)} %copy-done.2, bf16[3,768,128]{2,1,0:T(8,128)(2,1)} %copy-done.4, bf16[3,768,128]{2,1,0:T(8,128)(2,1)} %copy-done.3, bf16[3,768,128]{2,1,0:T(8,128)(2,1)} %copy-done.1, ...), custom_call_target="tpu_custom_call" | custom-call | flops 1000 | bytes 1000 | tf_op jit(solution)/shard_map/pallas_call | solution.py:141
  90.0 5.6 %all-gather.2.cloned.1.call-done.refs_1_.refs_2_ = bf16[2,6144,128]{2,1,0:T(8,128)(2,1)} async-done(((bf16[2,768,128]{2,1,0:T(8,128)(2,1)}), bf16[2,6144,128]{2,1,0:T(8,128)(2,1)}) %all-gather.2.cloned.1.call-update) | async-done | bytes 3145744 | tf_op jit(solution)/shard_map/all_gather | solution.py:315
  95.6 8.4 %shard_map.133.refs_4_.refs_14_.refs_24_ = bf16[768,128]{1,0:T(8,128)(2,1)} custom-call(bf16[768,640]{1,0:T(8,128)(2,1)} %bitcast.50, bf16[2,6144,128]{2,1,0:T(8,128)(2,1)} %all-gather.2.cloned.1.call-done.refs_1_.refs_2_, bf16[2,6144,128]{2,1,0:T(8,128)(2,1)} %all-gather.2.cloned.1.call-done.refs_1_.refs_2_), custom_call_target="tpu_custom_call" | custom-call | flops 1000 | bytes 1000 | tf_op jit(solution)/shard_map/pallas_call | solution.py:141
  107.8 5.4 %shard_map.134 = (bf16[96,2560]{1,0:T(8,128)(2,1)}, bf16[96,2560]{1,0:T(8,128)(2,1)}) custom-call(s32[4]{0:T(128)} %pad_add_fusion.place, bf16[768,128]{1,0:T(8,128)(2,1)} %copy-done.8, bf16[768,128]{1,0:T(8,128)(2,1)} %copy-done.5, bf16[768,128]{1,0:T(8,128)(2,1)} %copy-done.6, bf16[768,128]{1,0:T(8,128)(2,1)} %copy-done.7, ...), custom_call_target="tpu_custom_call" | custom-call | flops 1000 | bytes 1000 | tf_op jit(solution)/shard_map/pallas_call | solution.py:188
  113.2 4.5 %collective-permute-start.22 = (bf16[96,2560]{1,0:T(8,128)(2,1)}, bf16[96,2560]{1,0:T(8,128)(2,1)S(1)}, u32[]{:S(2)}, u32[]{:S(2)}) collective-permute-start(bf16[96,2560]{1,0:T(8,128)(2,1)} %get-tuple-element.87), channel_id=1, source_target_pairs={{0,6},{1,7},{2,0},{3,1},{4,2},{5,3},{6,4},{7,5},{8,14},{9,15},{10,... | collective-permute-start | bytes 1474568 | tf_op jit(solution)/shard_map/ppermute | solution.py:348
  117.7 9.3 %shard_map.135 = (f32[96,2560]{1,0:T(8,128)}, bf16[96,2560]{1,0:T(8,128)(2,1)}, bf16[96,2560]{1,0:T(8,128)(2,1)}, f32[96,2560]{1,0:T(8,128)}, f32[96,2560]{1,0:T(8,128)}, /*index=5*/f32[96,2560]{1,0:T(8,128)}) custom-call(s32[4]{0:T(128)} %pad_add_fusion.place, bf16[768,128]{1,0:T(8,128)(2,1)} %copy-done.8, bf16[768,128]{1,0:T(8,128)(2,1)} %copy-done.5, ...), custom_call_target="tpu_custom_call" | custom-call | flops 1000 | bytes 1000 | tf_op jit(solution)/shard_map/pallas_call | solution.py:188
  127.5 2.9 %collective-permute-start.21 = (bf16[96,2560]{1,0:T(8,128)(2,1)}, bf16[96,2560]{1,0:T(8,128)(2,1)S(1)}, u32[]{:S(2)}, u32[]{:S(2)}) collective-permute-start(bf16[96,2560]{1,0:T(8,128)(2,1)} %get-tuple-element.102), channel_id=1, source_target_pairs={{0,6},{1,7},{2,0},{3,1},{4,2},{5,3},{6,4},{7,5},{8,14},{9,15},{10,... | collective-permute-start | bytes 1474568 | tf_op jit(solution)/shard_map/ppermute | solution.py:355
  131.7 2.4 %collective-permute-start.23 = (bf16[96,2560]{1,0:T(8,128)(2,1)S(1)}, bf16[96,2560]{1,0:T(8,128)(2,1)S(1)}, u32[]{:S(2)}, u32[]{:S(2)}) collective-permute-start(bf16[96,2560]{1,0:T(8,128)(2,1)S(1)} %add_convert_fusion), channel_id=1, source_target_pairs={{0,6},{1,7},{2,0},{3,1},{4,2},{5,3},{6,4},{7,5},{8,14},{9,15},{10,... | collective-permute-start | bytes 1474568 | tf_op jit(solution)/shard_map/ppermute | solution.py:359
  134.1 2.1 %add_convert_fusion.1 = bf16[96,2560]{1,0:T(8,128)(2,1)} fusion(f32[96,2560]{1,0:T(8,128)} %get-tuple-element.100, bf16[96,2560]{1,0:T(8,128)(2,1)S(1)} %collective-permute-done.18), kind=kLoop, calls=%fused_computation.1 | loop fusion | flops 737280 | bytes 1966080 | tf_op jit(solution)/shard_map/convert_element_type | solution.py:356
  138.3 5.5 %collective-permute-done.20.refs_3_ = bf16[96,2560]{1,0:T(8,128)(2,1)S(1)} collective-permute-done((bf16[96,2560]{1,0:T(8,128)(2,1)}, bf16[96,2560]{1,0:T(8,128)(2,1)S(1)}, u32[]{:S(2)}, u32[]{:S(2)}) %collective-permute-start.20) | collective-permute-done | bytes 491552 | tf_op jit(solution)/shard_map/ppermute | solution.py:354
  143.8 7.7 %collective-permute-done.23.refs_5_ = bf16[96,2560]{1,0:T(8,128)(2,1)S(1)} collective-permute-done((bf16[96,2560]{1,0:T(8,128)(2,1)S(1)}, bf16[96,2560]{1,0:T(8,128)(2,1)S(1)}, u32[]{:S(2)}, u32[]{:S(2)}) %collective-permute-start.23) | collective-permute-done | bytes 491552 | tf_op jit(solution)/shard_map/ppermute | solution.py:359
  151.5 1.8 %collective-permute-done.19.refs_2_ = bf16[96,2560]{1,0:T(8,128)(2,1)S(1)} collective-permute-done((bf16[96,2560]{1,0:T(8,128)(2,1)}, bf16[96,2560]{1,0:T(8,128)(2,1)S(1)}, u32[]{:S(2)}, u32[]{:S(2)}) %collective-permute-start.19) | collective-permute-done | bytes 491552 | tf_op jit(solution)/shard_map/ppermute | solution.py:358
  154.1 5.0 %shard_map.136 = (f32[40,192]{1,0:T(8,128)}, f32[40,192]{1,0:T(8,128)}) custom-call(s32[4]{0:T(128)} %pad_add_fusion.place, f32[96,2560]{1,0:T(8,128)} %get-tuple-element.98.refs_0_, f32[96,2560]{1,0:T(8,128)} %get-tuple-element.99.refs_1_, bf16[96,2560]{1,0:T(8,128)(2,1)} %copy-done.22, bf16[96,2560]{1,0:T(8,128)(2,1)} %copy-done.19, ...), custom_call_target="tpu_custom_call" | custom-call | flops 377487360 | bytes 5898240 | tf_op jit(solution)/shard_map/pallas_call | solution.py:260
  159.6 1.7 collective-permute-start.26
  161.4 2.3 %collective-permute-done.24 = f32[40,192]{1,0:T(8,128)S(1)} collective-permute-done((f32[40,192]{1,0:T(8,128)}, f32[40,192]{1,0:T(8,128)S(1)}, u32[]{:S(2)}, u32[]{:S(2)}) %collective-permute-start.24) | collective-permute-done | bytes 30752 | tf_op jit(solution)/shard_map/ppermute | solution.py:366
  164.6 2.1 %collective-permute-start.27 = (f32[32,192]{1,0:T(8,128)S(1)}, f32[32,192]{1,0:T(8,128)S(1)}, u32[]{:S(2)}, u32[]{:S(2)}) collective-permute-start(f32[32,192]{1,0:T(8,128)S(1)} %fusion.10), channel_id=1, source_target_pairs={{0,6},{1,7},{2,0},{3,1},{4,2},{5,3},{6,4},{7,5},{8,14},{9,15},{10,... | collective-permute-start | bytes 73736 | tf_op jit(solution)/shard_map/ppermute | solution.py:385
  168.8 3.3 %collective-permute-done.28 = f32[32,192]{1,0:T(8,128)S(1)} collective-permute-done((f32[32,192]{1,0:T(8,128)S(1)}, f32[32,192]{1,0:T(8,128)S(1)}, u32[]{:S(2)}, u32[]{:S(2)}) %collective-permute-start.28) | collective-permute-done | bytes 24608 | tf_op jit(solution)/shard_map/ppermute | solution.py:385
  (123 shorter events, 23.9 us)
Async XLA Ops:
  7.2 88.4 %all-gather.2.cloned.1.call-start = ((), (), s32[]{:S(2)}) async-start(), calls=%async_computation | async-start | bytes 3538944 | tf_op jit(solution)/shard_map/all_gather | solution.py:315
  16.7 42.5 %collective-permute-start.8 = (bf16[640,2560]{1,0:T(8,128)(2,1)S(1)}, bf16[640,2560]{1,0:T(8,128)(2,1)S(1)}, u32[]{:S(2)}, u32[]{:S(2)}) collective-permute-start(bf16[640,2560]{1,0:T(8,128)(2,1)S(1)} %constant_dynamic-slice_fusion), channel_id=1, source_target_pairs={{0,1},{1,0},{2,3},{3,2},{4,5},{5,4},{6,7},{7,6},{8,9},{9,8},{10,11... | collective-permute-start | bytes 9830408 | tf_op jit(solution)/shard_map/ppermute | solution.py:322
  16.8 7.4 %collective-permute-start = (bf16[3,768,128]{2,1,0:T(8,128)(2,1)S(1)}, bf16[3,768,128]{2,1,0:T(8,128)(2,1)S(1)}, u32[]{:S(2)}, u32[]{:S(2)}) collective-permute-start(bf16[3,768,128]{2,1,0:T(8,128)(2,1)S(1)} %copy-done.30), channel_id=1, source_target_pairs={{0,0},{1,8},{2,2},{3,10},{4,4},{5,12},{6,6},{7,14},{8,1},{9,9},{10... | collective-permute-start | bytes 1769480 | tf_op jit(solution)/shard_map/ppermute | solution.py:320
  17.6 17.0 %collective-permute-start.1 = (bf16[3,768,128]{2,1,0:T(8,128)(2,1)S(1)}, bf16[3,768,128]{2,1,0:T(8,128)(2,1)S(1)}, u32[]{:S(2)}, u32[]{:S(2)}) collective-permute-start(bf16[3,768,128]{2,1,0:T(8,128)(2,1)S(1)} %copy-done.29), channel_id=1, source_target_pairs={{0,16},{1,24},{2,18},{3,26},{4,20},{5,28},{6,22},{7,30},{8,17},{9,... | collective-permute-start | bytes 1769480 | tf_op jit(solution)/shard_map/ppermute | solution.py:320
  19.6 36.8 %collective-permute-start.2 = (bf16[3,768,128]{2,1,0:T(8,128)(2,1)S(1)}, bf16[3,768,128]{2,1,0:T(8,128)(2,1)S(1)}, u32[]{:S(2)}, u32[]{:S(2)}) collective-permute-start(bf16[3,768,128]{2,1,0:T(8,128)(2,1)S(1)} %copy-done.28), channel_id=1, source_target_pairs={{0,32},{1,40},{2,34},{3,42},{4,36},{5,44},{6,38},{7,46},{8,33},{9,... | collective-permute-start | bytes 1769480 | tf_op jit(solution)/shard_map/ppermute | solution.py:320
  23.2 33.2 %collective-permute-start.3 = (bf16[3,768,128]{2,1,0:T(8,128)(2,1)S(1)}, bf16[3,768,128]{2,1,0:T(8,128)(2,1)S(1)}, u32[]{:S(2)}, u32[]{:S(2)}) collective-permute-start(bf16[3,768,128]{2,1,0:T(8,128)(2,1)S(1)} %copy-done.27), channel_id=1, source_target_pairs={{0,48},{1,56},{2,50},{3,58},{4,52},{5,60},{6,54},{7,62},{8,49},{9,... | collective-permute-start | bytes 1769480 | tf_op jit(solution)/shard_map/ppermute | solution.py:320
  24.2 32.7 %collective-permute-start.4 = (bf16[3,768,128]{2,1,0:T(8,128)(2,1)S(1)}, bf16[3,768,128]{2,1,0:T(8,128)(2,1)S(1)}, u32[]{:S(2)}, u32[]{:S(2)}) collective-permute-start(bf16[3,768,128]{2,1,0:T(8,128)(2,1)S(1)} %collective-permute-done.refs_3_.refs_7_.refs_15_), channel_id=1, source_target_pairs={{0,1},{1,0},{2,3},{3,2},{4,5},{5,4},{6,7},{7,6},{8,9},{9,8},{10,11... | collective-permute-start | bytes 1769480 | tf_op jit(solution)/shard_map/ppermute | solution.py:325
  34.5 22.4 %collective-permute-start.5 = (bf16[3,768,128]{2,1,0:T(8,128)(2,1)S(1)}, bf16[3,768,128]{2,1,0:T(8,128)(2,1)S(1)}, u32[]{:S(2)}, u32[]{:S(2)}) collective-permute-start(bf16[3,768,128]{2,1,0:T(8,128)(2,1)S(1)} %collective-permute-done.1.refs_0_.refs_4_.refs_12_), channel_id=1, source_target_pairs={{0,1},{1,0},{2,3},{3,2},{4,5},{5,4},{6,7},{7,6},{8,9},{9,8},{10,11... | collective-permute-start | bytes 1769480 | tf_op jit(solution)/shard_map/ppermute | solution.py:325
  86.2 17.8 %collective-permute-start.10 = (bf16[768,128]{1,0:T(8,128)(2,1)}, bf16[768,128]{1,0:T(8,128)(2,1)S(1)}, u32[]{:S(2)}, u32[]{:S(2)}) collective-permute-start(bf16[768,128]{1,0:T(8,128)(2,1)} %get-tuple-element.76), channel_id=1, source_target_pairs={{0,48},{1,56},{2,50},{3,58},{4,52},{5,60},{6,54},{7,62},{8,49},{9,... | collective-permute-start | bytes 589832 | tf_op jit(solution)/shard_map/ppermute | solution.py:334
  87.5 16.5 %collective-permute-start.11 = (bf16[768,128]{1,0:T(8,128)(2,1)}, bf16[768,128]{1,0:T(8,128)(2,1)S(1)}, u32[]{:S(2)}, u32[]{:S(2)}) collective-permute-start(bf16[768,128]{1,0:T(8,128)(2,1)} %get-tuple-element.77), channel_id=1, source_target_pairs={{0,32},{1,40},{2,34},{3,42},{4,36},{5,44},{6,38},{7,46},{8,33},{9,... | collective-permute-start | bytes 589832 | tf_op jit(solution)/shard_map/ppermute | solution.py:334
  88.4 15.6 %collective-permute-start.12 = (bf16[768,128]{1,0:T(8,128)(2,1)}, bf16[768,128]{1,0:T(8,128)(2,1)S(1)}, u32[]{:S(2)}, u32[]{:S(2)}) collective-permute-start(bf16[768,128]{1,0:T(8,128)(2,1)} %get-tuple-element.78), channel_id=1, source_target_pairs={{0,16},{1,24},{2,18},{3,26},{4,20},{5,28},{6,22},{7,30},{8,17},{9,... | collective-permute-start | bytes 589832 | tf_op jit(solution)/shard_map/ppermute | solution.py:334
  88.5 15.6 %collective-permute-start.9 = (bf16[768,128]{1,0:T(8,128)(2,1)}, bf16[768,128]{1,0:T(8,128)(2,1)S(1)}, u32[]{:S(2)}, u32[]{:S(2)}) collective-permute-start(bf16[768,128]{1,0:T(8,128)(2,1)} %get-tuple-element.75), channel_id=1, source_target_pairs={{0,0},{1,8},{2,2},{3,10},{4,4},{5,12},{6,6},{7,14},{8,1},{9,9},{10... | collective-permute-start | bytes 589832 | tf_op jit(solution)/shard_map/ppermute | solution.py:334
  113.2 17.2 %collective-permute-start.22 = (bf16[96,2560]{1,0:T(8,128)(2,1)}, bf16[96,2560]{1,0:T(8,128)(2,1)S(1)}, u32[]{:S(2)}, u32[]{:S(2)}) collective-permute-start(bf16[96,2560]{1,0:T(8,128)(2,1)} %get-tuple-element.87), channel_id=1, source_target_pairs={{0,6},{1,7},{2,0},{3,1},{4,2},{5,3},{6,4},{7,5},{8,14},{9,15},{10,... | collective-permute-start | bytes 1474568 | tf_op jit(solution)/shard_map/ppermute | solution.py:348
  117.7 16.4 %collective-permute-start.18 = (bf16[96,2560]{1,0:T(8,128)(2,1)}, bf16[96,2560]{1,0:T(8,128)(2,1)S(1)}, u32[]{:S(2)}, u32[]{:S(2)}) collective-permute-start(bf16[96,2560]{1,0:T(8,128)(2,1)} %get-tuple-element.86), channel_id=1, source_target_pairs={{0,2},{1,3},{2,4},{3,5},{4,6},{5,7},{6,0},{7,1},{8,10},{9,11},{10,... | collective-permute-start | bytes 1474568 | tf_op jit(solution)/shard_map/ppermute | solution.py:347
  127.1 16.7 %collective-permute-start.20 = (bf16[96,2560]{1,0:T(8,128)(2,1)}, bf16[96,2560]{1,0:T(8,128)(2,1)S(1)}, u32[]{:S(2)}, u32[]{:S(2)}) collective-permute-start(bf16[96,2560]{1,0:T(8,128)(2,1)} %get-tuple-element.101), channel_id=1, source_target_pairs={{0,2},{1,3},{2,4},{3,5},{4,6},{5,7},{6,0},{7,1},{8,10},{9,11},{10,... | collective-permute-start | bytes 1474568 | tf_op jit(solution)/shard_map/ppermute | solution.py:354
  127.5 16.3 %collective-permute-start.21 = (bf16[96,2560]{1,0:T(8,128)(2,1)}, bf16[96,2560]{1,0:T(8,128)(2,1)S(1)}, u32[]{:S(2)}, u32[]{:S(2)}) collective-permute-start(bf16[96,2560]{1,0:T(8,128)(2,1)} %get-tuple-element.102), channel_id=1, source_target_pairs={{0,6},{1,7},{2,0},{3,1},{4,2},{5,3},{6,4},{7,5},{8,14},{9,15},{10,... | collective-permute-start | bytes 1474568 | tf_op jit(solution)/shard_map/ppermute | solution.py:355
  131.7 19.8 %collective-permute-start.23 = (bf16[96,2560]{1,0:T(8,128)(2,1)S(1)}, bf16[96,2560]{1,0:T(8,128)(2,1)S(1)}, u32[]{:S(2)}, u32[]{:S(2)}) collective-permute-start(bf16[96,2560]{1,0:T(8,128)(2,1)S(1)} %add_convert_fusion), channel_id=1, source_target_pairs={{0,6},{1,7},{2,0},{3,1},{4,2},{5,3},{6,4},{7,5},{8,14},{9,15},{10,... | collective-permute-start | bytes 1474568 | tf_op jit(solution)/shard_map/ppermute | solution.py:359
  136.2 17.1 %collective-permute-start.19 = (bf16[96,2560]{1,0:T(8,128)(2,1)}, bf16[96,2560]{1,0:T(8,128)(2,1)S(1)}, u32[]{:S(2)}, u32[]{:S(2)}) collective-permute-start(bf16[96,2560]{1,0:T(8,128)(2,1)} %add_convert_fusion.1), channel_id=1, source_target_pairs={{0,2},{1,3},{2,4},{3,5},{4,6},{5,7},{6,0},{7,1},{8,10},{9,11},{10,... | collective-permute-start | bytes 1474568 | tf_op jit(solution)/shard_map/ppermute | solution.py:358
  159.1 4.5 %collective-permute-start.24 = (f32[40,192]{1,0:T(8,128)}, f32[40,192]{1,0:T(8,128)S(1)}, u32[]{:S(2)}, u32[]{:S(2)}) collective-permute-start(f32[40,192]{1,0:T(8,128)} %get-tuple-element.104), channel_id=1, source_target_pairs={{0,64},{64,0},{1,65},{65,1},{2,66},{66,2},{3,67},{67,3},{4,68},{68... | collective-permute-start | bytes 92168 | tf_op jit(solution)/shard_map/ppermute | solution.py:366
  159.6 4.1 %collective-permute-start.25 = (f32[40,192]{1,0:T(8,128)}, f32[40,192]{1,0:T(8,128)S(1)}, u32[]{:S(2)}, u32[]{:S(2)}) collective-permute-start(f32[40,192]{1,0:T(8,128)} %get-tuple-element.104), channel_id=1, source_target_pairs={{0,65},{1,64},{2,67},{3,66},{4,69},{5,68},{6,71},{7,70},{64,1},{65... | collective-permute-start | bytes 92168 | tf_op jit(solution)/shard_map/ppermute | solution.py:366
  159.6 4.0 %collective-permute-start.26 = (f32[40,192]{1,0:T(8,128)}, f32[40,192]{1,0:T(8,128)S(1)}, u32[]{:S(2)}, u32[]{:S(2)}) collective-permute-start(f32[40,192]{1,0:T(8,128)} %get-tuple-element.105), channel_id=1, source_target_pairs={{0,1},{1,0},{2,3},{3,2},{4,5},{5,4},{6,7},{7,6},{8,9},{9,8},{10,11... | collective-permute-start | bytes 92168 | tf_op jit(solution)/shard_map/ppermute | solution.py:365
  164.6 4.3 %collective-permute-start.27 = (f32[32,192]{1,0:T(8,128)S(1)}, f32[32,192]{1,0:T(8,128)S(1)}, u32[]{:S(2)}, u32[]{:S(2)}) collective-permute-start(f32[32,192]{1,0:T(8,128)S(1)} %fusion.10), channel_id=1, source_target_pairs={{0,6},{1,7},{2,0},{3,1},{4,2},{5,3},{6,4},{7,5},{8,14},{9,15},{10,... | collective-permute-start | bytes 73736 | tf_op jit(solution)/shard_map/ppermute | solution.py:385
  166.7 5.5 %collective-permute-start.28 = (f32[32,192]{1,0:T(8,128)S(1)}, f32[32,192]{1,0:T(8,128)S(1)}, u32[]{:S(2)}, u32[]{:S(2)}) collective-permute-start(f32[32,192]{1,0:T(8,128)S(1)} %fusion.10), channel_id=1, source_target_pairs={{0,4},{1,5},{2,6},{3,7},{4,0},{5,1},{6,2},{7,3},{8,12},{9,13},{10,... | collective-permute-start | bytes 73736 | tf_op jit(solution)/shard_map/ppermute | solution.py:385
  166.8 5.5 %collective-permute-start.29 = (f32[32,192]{1,0:T(8,128)S(1)}, f32[32,192]{1,0:T(8,128)S(1)}, u32[]{:S(2)}, u32[]{:S(2)}) collective-permute-start(f32[32,192]{1,0:T(8,128)S(1)} %fusion.10), channel_id=1, source_target_pairs={{0,2},{1,3},{2,4},{3,5},{4,6},{5,7},{6,0},{7,1},{8,10},{9,11},{10,... | collective-permute-start | bytes 73736 | tf_op jit(solution)/shard_map/ppermute | solution.py:385
  (38 other events, 234.9 us)
Sparse Core Ops, SparseCore 0:
  10.3 85.2 all-gather.1

commit v5 on v4

--- a/solution.py
+++ b/solution.py
@@ -154,11 +154,11 @@
     )(*(array for array, _ in operands))
 
 
-def project_body(place, *refs, steps):
-    count = (2 * Z + 2) * len(steps)
+def project_body(place, *refs, pieces):
+    count = (2 * Z + 2) * pieces
     operands, own_weight, other_weight, outs = refs[:count], *refs[count:][:2], refs[count + 2 : -2]
     rows, weight = refs[-2:]
-    share = rows.shape[0] // len(steps)
+    share = rows.shape[0] // pieces
     depth = own_weight.shape[0]
 
     @pl.when(pl.program_id(0) == 0)
@@ -181,18 +181,21 @@
     return pl.multiple_of((place[3] + step) % Z * HSIZE, HSIZE)
 
 
-def project(place, attended, own_weight, other_weight, steps, kinds, height, tile=1280):
+def project(place, attended, own_weight, other_weight, pieces, kinds, tile=1280):
     depth, half = other_weight.shape
-    share = attended[0].shape[0] // X
-    rows, tiles = share * len(steps), half // tile
+    height = attended[0].shape[0] // X // 2
+    rows, tiles = height * len(pieces), half // tile
     return pl.pallas_call(
-        functools.partial(project_body, steps=steps),
+        functools.partial(project_body, pieces=len(pieces)),
         grid_spec=pltpu.PrefetchScalarGridSpec(
             num_scalar_prefetch=1,
             grid=(tiles,),
             in_specs=[
-                pl.BlockSpec((share, HSIZE), lambda i, place, step=step: ((place[0] + step) % X, 0))
-                for step in steps
+                pl.BlockSpec(
+                    (height, HSIZE),
+                    lambda i, place, step=step, n=n: ((place[0] + step) % X * 2 + n, 0),
+                )
+                for step, n in pieces
                 for _ in attended
             ]
             + [
@@ -208,7 +211,7 @@
         out_shape=[jax.ShapeDtypeStruct((height, half), kind) for kind in kinds],
         compiler_params=pltpu.CompilerParams(vmem_limit_bytes=56 * 2**20),
         cost_estimate=pl.CostEstimate(flops=1000, bytes_accessed=1000, transcendentals=0),
-    )(place, *(attended * len(steps)), own_weight, other_weight)
+    )(place, *(attended * len(pieces)), own_weight, other_weight)
 
 
 def finish_body(place, *refs):
@@ -341,18 +344,21 @@
         *(lax.ppermute(part, "head", core_swap) for part in own_attended),
     )
 
-    wire, middle = jnp.bfloat16, share // 2
+    wire = jnp.bfloat16
     weights = out_weight, other_weight
-    opposite = project(place, attended, *weights, (2,), (wire,) * 2, middle)
+    opposite = project(place, attended, *weights, ((2, 0), (2, 1)), (wire,) * 2)
     behind_far = lax.ppermute(opposite[0], "head", x_shift(1))
     ahead_far = lax.ppermute(opposite[1], "head", x_shift(3))
     attended, opposite = lax.optimization_barrier((attended, opposite))
-    *rest, own_upper, own_lower = project(
-        place, attended, *weights, (1, 3, 0), (jnp.float32, wire, wire) + (jnp.float32,) * 3, middle
-    )
-    forward, forward_lower, backward_upper, backward = rest
+    forward_lower, backward_upper = project(
+        place, attended, *weights, ((1, 1), (3, 0)), (wire,) * 2
+    )
     behind_lower = lax.ppermute(forward_lower, "head", x_shift(1))
     ahead_upper = lax.ppermute(backward_upper, "head", x_shift(3))
+    attended, forward_lower = lax.optimization_barrier((attended, forward_lower))
+    forward, backward, own_upper, own_lower = project(
+        place, attended, *weights, ((1, 0), (3, 1), (0, 0), (0, 1)), (jnp.float32,) * 4
+    )
     forward = (forward + behind_far.astype(jnp.float32)).astype(wire)
     backward = (backward + ahead_far.astype(jnp.float32)).astype(wire)
     behind_upper = lax.ppermute(forward, "head", x_shift(1))

time: 180 us -> 179 us (level)
  Pallas kernels: 59 us -> 63.1 us
  starting transfers between devices: 49.1 us -> 46.3 us
  waiting for transfers between devices: 42.4 us -> 39.6 us
    ppermute x1, waiting for transfers between devices: 5.54 us -> 0.4 us  [per_device(): behind_lower = lax.ppermute(forward_lower, 'head', x_shift(1))]
    pallas_call x2 -> x3, Pallas kernels: 14.7 us -> 18.9 us  [project(): pl.pallas_call(functools.partial(project_body, pieces=len(pieces)), grid_...]
  transfers between devices with their start and end apart: 31 -> 31, of which waited for: 15 -> 17; matrix products, arithmetic and copies ran while one was open for 5% -> 5% of each run, Pallas kernels for 27% -> 29%
where the time goes in v5:
time: 179 us
  Pallas kernels  63.1 us (35%)
  starting transfers between devices  46.3 us (26%)
  waiting for transfers between devices  39.6 us (22%)
  between operations  15.2 us (8%)
  local copies, waits for them, and re-layouts  7.35 us (4%)
  other arithmetic  6.47 us (4%)
    pallas_call x2, Pallas kernels, attend(): pl.pallas_call(functools.partial(attend_body, heads=len(queries), parts=l...  34.5 us
    ppermute x4, starting transfers between devices, per_device(): far = {step: lax.ppermute(near[step], 'head', core_swap) for step in order}  20.5 us
    pallas_call x3, Pallas kernels, project(): pl.pallas_call(functools.partial(project_body, pieces=len(pieces)), grid_...  18.9 us
    ppermute x4, waiting for transfers between devices, per_device(): lax.ppermute(message, pair, traded(step))  12.1 us
    ppermute x4, starting transfers between devices, per_device(): lax.ppermute(message, pair, traded(step))  7.36 us
    ppermute x1, waiting for transfers between devices, per_device(): ahead_lower = lax.ppermute(backward, 'head', x_shift(3))  7.11 us
    all_gather x1, waiting for transfers between devices, per_device(): fifth = lax.all_gather(fifth, 'seq', axis=1, tiled=True)  5.52 us
    pallas_call x1, Pallas kernels, finish(): pl.pallas_call(finish_body, grid_spec=pltpu.PrefetchScalarGridSpec(num_sc...  5.04 us
  transfers between devices with their start and end apart: 31, of which 17 were waited for; matrix products, arithmetic and copies ran while one was open for 5% of the time, Pallas kernels for 29%

profile of v5, /device:TPU:0, one launch (start us, length us, event | category | flops | bytes accessed | tf_op | source)
XLA Modules:
  0.0 178.7 jit_solution(13495105001134428041)
XLA Ops:
  9.7 4.7 %shard_map.131 = (bf16[3,768,128]{2,1,0:T(8,128)(2,1)}, bf16[3,768,128]{2,1,0:T(8,128)(2,1)}, bf16[3,768,128]{2,1,0:T(8,128)(2,1)}, bf16[3,768,128]{2,1,0:T(8,128)(2,1)}) custom-call(s32[4]{0:T(128)} %pad_add_fusion.place, bf16[768,640]{1,0:T(8,128)(2,1)} %bitcast.49, bf16[768,640]{1,0:T(8,128)(2,1)} %bitcast.52, bf16[768,640]{1,0:T(8,128)(2,1)} %bitcast.54), custom_call_target="tpu_custom_call" | custom-call | tf_op jit(solution)/shard_map/pallas_call | solution.py:64
  14.4 2.3 %constant_dynamic-slice_fusion = bf16[640,2560]{1,0:T(8,128)(2,1)S(1)} fusion(bf16[640,5120]{1,0:T(8,128)(2,1)} %refs_40_.1, s32[]{:T(128)S(6)} %select_n.43), kind=kLoop, calls=%fused_computation.35 | loop fusion | bytes 6553604 | tf_op jit(solution)/shard_map/dynamic_slice | solution.py:326
  17.5 2.1 %collective-permute-start.1 = (bf16[3,768,128]{2,1,0:T(8,128)(2,1)S(1)}, bf16[3,768,128]{2,1,0:T(8,128)(2,1)S(1)}, u32[]{:S(2)}, u32[]{:S(2)}) collective-permute-start(bf16[3,768,128]{2,1,0:T(8,128)(2,1)S(1)} %copy-done.29), channel_id=1, source_target_pairs={{0,16},{1,24},{2,18},{3,26},{4,20},{5,28},{6,22},{7,30},{8,17},{9,... | collective-permute-start | bytes 1769480 | tf_op jit(solution)/shard_map/ppermute | solution.py:323
  19.6 3.6 %collective-permute-start.2 = (bf16[3,768,128]{2,1,0:T(8,128)(2,1)S(1)}, bf16[3,768,128]{2,1,0:T(8,128)(2,1)S(1)}, u32[]{:S(2)}, u32[]{:S(2)}) collective-permute-start(bf16[3,768,128]{2,1,0:T(8,128)(2,1)S(1)} %copy-done.28), channel_id=1, source_target_pairs={{0,32},{1,40},{2,34},{3,42},{4,36},{5,44},{6,38},{7,46},{8,33},{9,... | collective-permute-start | bytes 1769480 | tf_op jit(solution)/shard_map/ppermute | solution.py:323
  24.2 10.3 %collective-permute-start.4 = (bf16[3,768,128]{2,1,0:T(8,128)(2,1)S(1)}, bf16[3,768,128]{2,1,0:T(8,128)(2,1)S(1)}, u32[]{:S(2)}, u32[]{:S(2)}) collective-permute-start(bf16[3,768,128]{2,1,0:T(8,128)(2,1)S(1)} %collective-permute-done.refs_3_.refs_7_.refs_15_), channel_id=1, source_target_pairs={{0,1},{1,0},{2,3},{3,2},{4,5},{5,4},{6,7},{7,6},{8,9},{9,8},{10,11... | collective-permute-start | bytes 1769480 | tf_op jit(solution)/shard_map/ppermute | solution.py:328
  34.5 9.7 %collective-permute-start.5 = (bf16[3,768,128]{2,1,0:T(8,128)(2,1)S(1)}, bf16[3,768,128]{2,1,0:T(8,128)(2,1)S(1)}, u32[]{:S(2)}, u32[]{:S(2)}) collective-permute-start(bf16[3,768,128]{2,1,0:T(8,128)(2,1)S(1)} %collective-permute-done.1.refs_0_.refs_4_.refs_12_), channel_id=1, source_target_pairs={{0,1},{1,0},{2,3},{3,2},{4,5},{5,4},{6,7},{7,6},{8,9},{9,8},{10,11... | collective-permute-start | bytes 1769480 | tf_op jit(solution)/shard_map/ppermute | solution.py:328
  44.3 12.1 %collective-permute-done.2.refs_2_.refs_6_.refs_14_ = bf16[3,768,128]{2,1,0:T(8,128)(2,1)S(1)} collective-permute-done((bf16[3,768,128]{2,1,0:T(8,128)(2,1)S(1)}, bf16[3,768,128]{2,1,0:T(8,128)(2,1)S(1)}, u32[]{:S(2)}, u32[]{:S(2)}) %collective-permute-start.2) | collective-permute-done | bytes 589856 | tf_op jit(solution)/shard_map/ppermute | solution.py:323
  60.1 26.1 %shard_map.132 = (bf16[768,128]{1,0:T(8,128)(2,1)}, bf16[768,128]{1,0:T(8,128)(2,1)}, bf16[768,128]{1,0:T(8,128)(2,1)}, bf16[768,128]{1,0:T(8,128)(2,1)}) custom-call(bf16[3,768,128]{2,1,0:T(8,128)(2,1)} %copy-done.11, bf16[3,768,128]{2,1,0:T(8,128)(2,1)} %copy-done.13, bf16[3,768,128]{2,1,0:T(8,128)(2,1)} %copy-done.12, bf16[3,768,128]{2,1,0:T(8,128)(2,1)} %copy-done.10, ...), custom_call_target="tpu_custom_call" | custom-call | flops 1000 | bytes 1000 | tf_op jit(solution)/shard_map/pallas_call | solution.py:141
  88.4 1.6 collective-permute-start.9
  90.0 5.5 %all-gather.2.cloned.1.call-done.refs_1_.refs_2_ = bf16[2,6144,128]{2,1,0:T(8,128)(2,1)} async-done(((bf16[2,768,128]{2,1,0:T(8,128)(2,1)}), bf16[2,6144,128]{2,1,0:T(8,128)(2,1)}) %all-gather.2.cloned.1.call-update) | async-done | bytes 3145744 | tf_op jit(solution)/shard_map/all_gather | solution.py:318
  95.5 8.4 %shard_map.133.refs_4_.refs_14_.refs_24_.refs_34_ = bf16[768,128]{1,0:T(8,128)(2,1)} custom-call(bf16[768,640]{1,0:T(8,128)(2,1)} %bitcast.50, bf16[2,6144,128]{2,1,0:T(8,128)(2,1)} %all-gather.2.cloned.1.call-done.refs_1_.refs_2_, bf16[2,6144,128]{2,1,0:T(8,128)(2,1)} %all-gather.2.cloned.1.call-done.refs_1_.refs_2_), custom_call_target="tpu_custom_call" | custom-call | flops 1000 | bytes 1000 | tf_op jit(solution)/shard_map/pallas_call | solution.py:141
  107.7 5.6 %shard_map.134 = (bf16[96,2560]{1,0:T(8,128)(2,1)}, bf16[96,2560]{1,0:T(8,128)(2,1)}) custom-call(s32[4]{0:T(128)} %pad_add_fusion.place, bf16[768,128]{1,0:T(8,128)(2,1)} %copy-done.4, bf16[768,128]{1,0:T(8,128)(2,1)} %copy-done.1, bf16[768,128]{1,0:T(8,128)(2,1)} %copy-done.2, bf16[768,128]{1,0:T(8,128)(2,1)} %copy-done.3, ...), custom_call_target="tpu_custom_call" | custom-call | flops 1000 | bytes 1000 | tf_op jit(solution)/shard_map/pallas_call | solution.py:188
  113.3 2.9 %collective-permute-start.22 = (bf16[96,2560]{1,0:T(8,128)(2,1)}, bf16[96,2560]{1,0:T(8,128)(2,1)S(1)}, u32[]{:S(2)}, u32[]{:S(2)}) collective-permute-start(bf16[96,2560]{1,0:T(8,128)(2,1)} %get-tuple-element.97), channel_id=1, source_target_pairs={{0,6},{1,7},{2,0},{3,1},{4,2},{5,3},{6,4},{7,5},{8,14},{9,15},{10,... | collective-permute-start | bytes 1474568 | tf_op jit(solution)/shard_map/ppermute | solution.py:351
  116.2 5.6 %shard_map.135 = (bf16[96,2560]{1,0:T(8,128)(2,1)}, bf16[96,2560]{1,0:T(8,128)(2,1)}) custom-call(s32[4]{0:T(128)} %pad_add_fusion.place, bf16[768,128]{1,0:T(8,128)(2,1)} %copy-done.4, bf16[768,128]{1,0:T(8,128)(2,1)} %copy-done.1, bf16[768,128]{1,0:T(8,128)(2,1)} %copy-done.2, bf16[768,128]{1,0:T(8,128)(2,1)} %copy-done.3, ...), custom_call_target="tpu_custom_call" | custom-call | flops 1000 | bytes 1000 | tf_op jit(solution)/shard_map/pallas_call | solution.py:188
  122.5 2.9 %collective-permute-start.21 = (bf16[96,2560]{1,0:T(8,128)(2,1)}, bf16[96,2560]{1,0:T(8,128)(2,1)S(1)}, u32[]{:S(2)}, u32[]{:S(2)}) collective-permute-start(bf16[96,2560]{1,0:T(8,128)(2,1)} %get-tuple-element.122), channel_id=1, source_target_pairs={{0,6},{1,7},{2,0},{3,1},{4,2},{5,3},{6,4},{7,5},{8,14},{9,15},{10,... | collective-permute-start | bytes 1474568 | tf_op jit(solution)/shard_map/ppermute | solution.py:357
  125.3 7.8 %shard_map.136 = (f32[96,2560]{1,0:T(8,128)}, f32[96,2560]{1,0:T(8,128)}, f32[96,2560]{1,0:T(8,128)}, f32[96,2560]{1,0:T(8,128)}) custom-call(s32[4]{0:T(128)} %pad_add_fusion.place, bf16[768,128]{1,0:T(8,128)(2,1)} %copy-done.4, bf16[768,128]{1,0:T(8,128)(2,1)} %copy-done.1, bf16[768,128]{1,0:T(8,128)(2,1)} %copy-done.2, bf16[768,128]{1,0:T(8,128)(2,1)} %copy-done.3, ...), custom_call_target="tpu_custom_call" | custom-call | flops 1000 | bytes 1000 | tf_op jit(solution)/shard_map/pallas_call | solution.py:188
  134.5 1.8 collective-permute-start.23
  136.3 2.1 %add_convert_fusion.1 = bf16[96,2560]{1,0:T(8,128)(2,1)} fusion(f32[96,2560]{1,0:T(8,128)} %get-tuple-element.121, bf16[96,2560]{1,0:T(8,128)(2,1)S(1)} %collective-permute-done.18), kind=kLoop, calls=%fused_computation.1 | loop fusion | flops 737280 | bytes 1966080 | tf_op jit(solution)/shard_map/convert_element_type | solution.py:362
  141.2 7.1 %collective-permute-done.23.refs_5_ = bf16[96,2560]{1,0:T(8,128)(2,1)S(1)} collective-permute-done((bf16[96,2560]{1,0:T(8,128)(2,1)S(1)}, bf16[96,2560]{1,0:T(8,128)(2,1)S(1)}, u32[]{:S(2)}, u32[]{:S(2)}) %collective-permute-start.23) | collective-permute-done | bytes 491552 | tf_op jit(solution)/shard_map/ppermute | solution.py:365
  148.3 3.5 %collective-permute-done.19.refs_2_ = bf16[96,2560]{1,0:T(8,128)(2,1)S(1)} collective-permute-done((bf16[96,2560]{1,0:T(8,128)(2,1)}, bf16[96,2560]{1,0:T(8,128)(2,1)S(1)}, u32[]{:S(2)}, u32[]{:S(2)}) %collective-permute-start.19) | collective-permute-done | bytes 491552 | tf_op jit(solution)/shard_map/ppermute | solution.py:364
  152.6 5.0 %shard_map.137 = (f32[40,192]{1,0:T(8,128)}, f32[40,192]{1,0:T(8,128)}) custom-call(s32[4]{0:T(128)} %pad_add_fusion.place, f32[96,2560]{1,0:T(8,128)} %get-tuple-element.119.refs_0_, f32[96,2560]{1,0:T(8,128)} %get-tuple-element.120.refs_1_, bf16[96,2560]{1,0:T(8,128)(2,1)} %copy-done.22, bf16[96,2560]{1,0:T(8,128)(2,1)} %copy-done.19, ...), custom_call_target="tpu_custom_call" | custom-call | flops 377487360 | bytes 5898240 | tf_op jit(solution)/shard_map/pallas_call | solution.py:263
  157.6 2.1 %collective-permute-start.24 = (f32[40,192]{1,0:T(8,128)}, f32[40,192]{1,0:T(8,128)S(1)}, u32[]{:S(2)}, u32[]{:S(2)}) collective-permute-start(f32[40,192]{1,0:T(8,128)} %get-tuple-element.124), channel_id=1, source_target_pairs={{0,64},{64,0},{1,65},{65,1},{2,66},{66,2},{3,67},{67,3},{4,68},{68... | collective-permute-start | bytes 92168 | tf_op jit(solution)/shard_map/ppermute | solution.py:372
  159.9 2.0 %collective-permute-done.24 = f32[40,192]{1,0:T(8,128)S(1)} collective-permute-done((f32[40,192]{1,0:T(8,128)}, f32[40,192]{1,0:T(8,128)S(1)}, u32[]{:S(2)}, u32[]{:S(2)}) %collective-permute-start.24) | collective-permute-done | bytes 30752 | tf_op jit(solution)/shard_map/ppermute | solution.py:372
  168.3 1.9 %collective-permute-done.28 = f32[32,192]{1,0:T(8,128)S(1)} collective-permute-done((f32[32,192]{1,0:T(8,128)S(1)}, f32[32,192]{1,0:T(8,128)S(1)}, u32[]{:S(2)}, u32[]{:S(2)}) %collective-permute-start.28) | collective-permute-done | bytes 24608 | tf_op jit(solution)/shard_map/ppermute | solution.py:391
  (124 shorter events, 26.9 us)
Async XLA Ops:
  7.2 88.4 %all-gather.2.cloned.1.call-start = ((), (), s32[]{:S(2)}) async-start(), calls=%async_computation | async-start | bytes 3538944 | tf_op jit(solution)/shard_map/all_gather | solution.py:318
  16.7 42.5 %collective-permute-start.8 = (bf16[640,2560]{1,0:T(8,128)(2,1)S(1)}, bf16[640,2560]{1,0:T(8,128)(2,1)S(1)}, u32[]{:S(2)}, u32[]{:S(2)}) collective-permute-start(bf16[640,2560]{1,0:T(8,128)(2,1)S(1)} %constant_dynamic-slice_fusion), channel_id=1, source_target_pairs={{0,1},{1,0},{2,3},{3,2},{4,5},{5,4},{6,7},{7,6},{8,9},{9,8},{10,11... | collective-permute-start | bytes 9830408 | tf_op jit(solution)/shard_map/ppermute | solution.py:325
  16.8 7.4 %collective-permute-start = (bf16[3,768,128]{2,1,0:T(8,128)(2,1)S(1)}, bf16[3,768,128]{2,1,0:T(8,128)(2,1)S(1)}, u32[]{:S(2)}, u32[]{:S(2)}) collective-permute-start(bf16[3,768,128]{2,1,0:T(8,128)(2,1)S(1)} %copy-done.30), channel_id=1, source_target_pairs={{0,0},{1,8},{2,2},{3,10},{4,4},{5,12},{6,6},{7,14},{8,1},{9,9},{10... | collective-permute-start | bytes 1769480 | tf_op jit(solution)/shard_map/ppermute | solution.py:323
  17.5 17.0 %collective-permute-start.1 = (bf16[3,768,128]{2,1,0:T(8,128)(2,1)S(1)}, bf16[3,768,128]{2,1,0:T(8,128)(2,1)S(1)}, u32[]{:S(2)}, u32[]{:S(2)}) collective-permute-start(bf16[3,768,128]{2,1,0:T(8,128)(2,1)S(1)} %copy-done.29), channel_id=1, source_target_pairs={{0,16},{1,24},{2,18},{3,26},{4,20},{5,28},{6,22},{7,30},{8,17},{9,... | collective-permute-start | bytes 1769480 | tf_op jit(solution)/shard_map/ppermute | solution.py:323
  19.6 36.8 %collective-permute-start.2 = (bf16[3,768,128]{2,1,0:T(8,128)(2,1)S(1)}, bf16[3,768,128]{2,1,0:T(8,128)(2,1)S(1)}, u32[]{:S(2)}, u32[]{:S(2)}) collective-permute-start(bf16[3,768,128]{2,1,0:T(8,128)(2,1)S(1)} %copy-done.28), channel_id=1, source_target_pairs={{0,32},{1,40},{2,34},{3,42},{4,36},{5,44},{6,38},{7,46},{8,33},{9,... | collective-permute-start | bytes 1769480 | tf_op jit(solution)/shard_map/ppermute | solution.py:323
  23.2 33.2 %collective-permute-start.3 = (bf16[3,768,128]{2,1,0:T(8,128)(2,1)S(1)}, bf16[3,768,128]{2,1,0:T(8,128)(2,1)S(1)}, u32[]{:S(2)}, u32[]{:S(2)}) collective-permute-start(bf16[3,768,128]{2,1,0:T(8,128)(2,1)S(1)} %copy-done.27), channel_id=1, source_target_pairs={{0,48},{1,56},{2,50},{3,58},{4,52},{5,60},{6,54},{7,62},{8,49},{9,... | collective-permute-start | bytes 1769480 | tf_op jit(solution)/shard_map/ppermute | solution.py:323
  24.2 32.7 %collective-permute-start.4 = (bf16[3,768,128]{2,1,0:T(8,128)(2,1)S(1)}, bf16[3,768,128]{2,1,0:T(8,128)(2,1)S(1)}, u32[]{:S(2)}, u32[]{:S(2)}) collective-permute-start(bf16[3,768,128]{2,1,0:T(8,128)(2,1)S(1)} %collective-permute-done.refs_3_.refs_7_.refs_15_), channel_id=1, source_target_pairs={{0,1},{1,0},{2,3},{3,2},{4,5},{5,4},{6,7},{7,6},{8,9},{9,8},{10,11... | collective-permute-start | bytes 1769480 | tf_op jit(solution)/shard_map/ppermute | solution.py:328
  34.5 22.4 %collective-permute-start.5 = (bf16[3,768,128]{2,1,0:T(8,128)(2,1)S(1)}, bf16[3,768,128]{2,1,0:T(8,128)(2,1)S(1)}, u32[]{:S(2)}, u32[]{:S(2)}) collective-permute-start(bf16[3,768,128]{2,1,0:T(8,128)(2,1)S(1)} %collective-permute-done.1.refs_0_.refs_4_.refs_12_), channel_id=1, source_target_pairs={{0,1},{1,0},{2,3},{3,2},{4,5},{5,4},{6,7},{7,6},{8,9},{9,8},{10,11... | collective-permute-start | bytes 1769480 | tf_op jit(solution)/shard_map/ppermute | solution.py:328
  86.1 17.8 %collective-permute-start.10 = (bf16[768,128]{1,0:T(8,128)(2,1)}, bf16[768,128]{1,0:T(8,128)(2,1)S(1)}, u32[]{:S(2)}, u32[]{:S(2)}) collective-permute-start(bf16[768,128]{1,0:T(8,128)(2,1)} %get-tuple-element.86), channel_id=1, source_target_pairs={{0,48},{1,56},{2,50},{3,58},{4,52},{5,60},{6,54},{7,62},{8,49},{9,... | collective-permute-start | bytes 589832 | tf_op jit(solution)/shard_map/ppermute | solution.py:337
  87.5 16.5 %collective-permute-start.11 = (bf16[768,128]{1,0:T(8,128)(2,1)}, bf16[768,128]{1,0:T(8,128)(2,1)S(1)}, u32[]{:S(2)}, u32[]{:S(2)}) collective-permute-start(bf16[768,128]{1,0:T(8,128)(2,1)} %get-tuple-element.87), channel_id=1, source_target_pairs={{0,32},{1,40},{2,34},{3,42},{4,36},{5,44},{6,38},{7,46},{8,33},{9,... | collective-permute-start | bytes 589832 | tf_op jit(solution)/shard_map/ppermute | solution.py:337
  88.4 15.6 %collective-permute-start.12 = (bf16[768,128]{1,0:T(8,128)(2,1)}, bf16[768,128]{1,0:T(8,128)(2,1)S(1)}, u32[]{:S(2)}, u32[]{:S(2)}) collective-permute-start(bf16[768,128]{1,0:T(8,128)(2,1)} %get-tuple-element.88), channel_id=1, source_target_pairs={{0,16},{1,24},{2,18},{3,26},{4,20},{5,28},{6,22},{7,30},{8,17},{9,... | collective-permute-start | bytes 589832 | tf_op jit(solution)/shard_map/ppermute | solution.py:337
  88.4 15.5 %collective-permute-start.9 = (bf16[768,128]{1,0:T(8,128)(2,1)}, bf16[768,128]{1,0:T(8,128)(2,1)S(1)}, u32[]{:S(2)}, u32[]{:S(2)}) collective-permute-start(bf16[768,128]{1,0:T(8,128)(2,1)} %get-tuple-element.85), channel_id=1, source_target_pairs={{0,0},{1,8},{2,2},{3,10},{4,4},{5,12},{6,6},{7,14},{8,1},{9,9},{10... | collective-permute-start | bytes 589832 | tf_op jit(solution)/shard_map/ppermute | solution.py:337
  113.3 19.9 %collective-permute-start.22 = (bf16[96,2560]{1,0:T(8,128)(2,1)}, bf16[96,2560]{1,0:T(8,128)(2,1)S(1)}, u32[]{:S(2)}, u32[]{:S(2)}) collective-permute-start(bf16[96,2560]{1,0:T(8,128)(2,1)} %get-tuple-element.97), channel_id=1, source_target_pairs={{0,6},{1,7},{2,0},{3,1},{4,2},{5,3},{6,4},{7,5},{8,14},{9,15},{10,... | collective-permute-start | bytes 1474568 | tf_op jit(solution)/shard_map/ppermute | solution.py:351
  116.2 20.2 %collective-permute-start.18 = (bf16[96,2560]{1,0:T(8,128)(2,1)}, bf16[96,2560]{1,0:T(8,128)(2,1)S(1)}, u32[]{:S(2)}, u32[]{:S(2)}) collective-permute-start(bf16[96,2560]{1,0:T(8,128)(2,1)} %get-tuple-element.96), channel_id=1, source_target_pairs={{0,2},{1,3},{2,4},{3,5},{4,6},{5,7},{6,0},{7,1},{8,10},{9,11},{10,... | collective-permute-start | bytes 1474568 | tf_op jit(solution)/shard_map/ppermute | solution.py:350
  121.7 19.5 %collective-permute-start.20 = (bf16[96,2560]{1,0:T(8,128)(2,1)}, bf16[96,2560]{1,0:T(8,128)(2,1)S(1)}, u32[]{:S(2)}, u32[]{:S(2)}) collective-permute-start(bf16[96,2560]{1,0:T(8,128)(2,1)} %get-tuple-element.108), channel_id=1, source_target_pairs={{0,2},{1,3},{2,4},{3,5},{4,6},{5,7},{6,0},{7,1},{8,10},{9,11},{10,... | collective-permute-start | bytes 1474568 | tf_op jit(solution)/shard_map/ppermute | solution.py:356
  122.5 18.7 %collective-permute-start.21 = (bf16[96,2560]{1,0:T(8,128)(2,1)}, bf16[96,2560]{1,0:T(8,128)(2,1)S(1)}, u32[]{:S(2)}, u32[]{:S(2)}) collective-permute-start(bf16[96,2560]{1,0:T(8,128)(2,1)} %get-tuple-element.122), channel_id=1, source_target_pairs={{0,6},{1,7},{2,0},{3,1},{4,2},{5,3},{6,4},{7,5},{8,14},{9,15},{10,... | collective-permute-start | bytes 1474568 | tf_op jit(solution)/shard_map/ppermute | solution.py:357
  134.5 13.8 %collective-permute-start.23 = (bf16[96,2560]{1,0:T(8,128)(2,1)S(1)}, bf16[96,2560]{1,0:T(8,128)(2,1)S(1)}, u32[]{:S(2)}, u32[]{:S(2)}) collective-permute-start(bf16[96,2560]{1,0:T(8,128)(2,1)S(1)} %add_convert_fusion), channel_id=1, source_target_pairs={{0,6},{1,7},{2,0},{3,1},{4,2},{5,3},{6,4},{7,5},{8,14},{9,15},{10,... | collective-permute-start | bytes 1474568 | tf_op jit(solution)/shard_map/ppermute | solution.py:365
  138.4 13.4 %collective-permute-start.19 = (bf16[96,2560]{1,0:T(8,128)(2,1)}, bf16[96,2560]{1,0:T(8,128)(2,1)S(1)}, u32[]{:S(2)}, u32[]{:S(2)}) collective-permute-start(bf16[96,2560]{1,0:T(8,128)(2,1)} %add_convert_fusion.1), channel_id=1, source_target_pairs={{0,2},{1,3},{2,4},{3,5},{4,6},{5,7},{6,0},{7,1},{8,10},{9,11},{10,... | collective-permute-start | bytes 1474568 | tf_op jit(solution)/shard_map/ppermute | solution.py:364
  157.6 4.3 %collective-permute-start.24 = (f32[40,192]{1,0:T(8,128)}, f32[40,192]{1,0:T(8,128)S(1)}, u32[]{:S(2)}, u32[]{:S(2)}) collective-permute-start(f32[40,192]{1,0:T(8,128)} %get-tuple-element.124), channel_id=1, source_target_pairs={{0,64},{64,0},{1,65},{65,1},{2,66},{66,2},{3,67},{67,3},{4,68},{68... | collective-permute-start | bytes 92168 | tf_op jit(solution)/shard_map/ppermute | solution.py:372
  159.7 3.6 %collective-permute-start.25 = (f32[40,192]{1,0:T(8,128)}, f32[40,192]{1,0:T(8,128)S(1)}, u32[]{:S(2)}, u32[]{:S(2)}) collective-permute-start(f32[40,192]{1,0:T(8,128)} %get-tuple-element.124), channel_id=1, source_target_pairs={{0,65},{1,64},{2,67},{3,66},{4,69},{5,68},{6,71},{7,70},{64,1},{65... | collective-permute-start | bytes 92168 | tf_op jit(solution)/shard_map/ppermute | solution.py:372
  159.7 3.6 %collective-permute-start.26 = (f32[40,192]{1,0:T(8,128)}, f32[40,192]{1,0:T(8,128)S(1)}, u32[]{:S(2)}, u32[]{:S(2)}) collective-permute-start(f32[40,192]{1,0:T(8,128)} %get-tuple-element.125), channel_id=1, source_target_pairs={{0,1},{1,0},{2,3},{3,2},{4,5},{5,4},{6,7},{7,6},{8,9},{9,8},{10,11... | collective-permute-start | bytes 92168 | tf_op jit(solution)/shard_map/ppermute | solution.py:371
  164.3 4.0 %collective-permute-start.27 = (f32[32,192]{1,0:T(8,128)S(1)}, f32[32,192]{1,0:T(8,128)S(1)}, u32[]{:S(2)}, u32[]{:S(2)}) collective-permute-start(f32[32,192]{1,0:T(8,128)S(1)} %fusion.10), channel_id=1, source_target_pairs={{0,6},{1,7},{2,0},{3,1},{4,2},{5,3},{6,4},{7,5},{8,14},{9,15},{10,... | collective-permute-start | bytes 73736 | tf_op jit(solution)/shard_map/ppermute | solution.py:391
  164.8 5.4 %collective-permute-start.28 = (f32[32,192]{1,0:T(8,128)S(1)}, f32[32,192]{1,0:T(8,128)S(1)}, u32[]{:S(2)}, u32[]{:S(2)}) collective-permute-start(f32[32,192]{1,0:T(8,128)S(1)} %fusion.10), channel_id=1, source_target_pairs={{0,4},{1,5},{2,6},{3,7},{4,0},{5,1},{6,2},{7,3},{8,12},{9,13},{10,... | collective-permute-start | bytes 73736 | tf_op jit(solution)/shard_map/ppermute | solution.py:391
  165.8 5.2 %collective-permute-start.29 = (f32[32,192]{1,0:T(8,128)S(1)}, f32[32,192]{1,0:T(8,128)S(1)}, u32[]{:S(2)}, u32[]{:S(2)}) collective-permute-start(f32[32,192]{1,0:T(8,128)S(1)} %fusion.10), channel_id=1, source_target_pairs={{0,2},{1,3},{2,4},{3,5},{4,6},{5,7},{6,0},{7,1},{8,10},{9,11},{10,... | collective-permute-start | bytes 73736 | tf_op jit(solution)/shard_map/ppermute | solution.py:391
  (38 other events, 228.2 us)
Sparse Core Ops, SparseCore 0:
  10.3 85.1 all-gather.1

commit v6 on v5

--- a/solution.py
+++ b/solution.py
@@ -336,7 +336,7 @@
     back = {
         step: lax.ppermute(result, pair, traded(-step)) for step, result in zip(order, dealt)
     }
-    (fifth_out,) = attend([(fifth_queries, Z)], [(fifth, 0)], [(fifth, 1)])
+    (fifth_out,) = attend([(fifth_queries, Z)], [(fifth, 0)], [(fifth, 1)], chunk=1536)
     back, fifth_out = lax.optimization_barrier((back, fifth_out))
     own_attended = [back[step] for step in range(Z)] + [fifth_out]
     attended = (

time: 179 us -> 180 us (level)
  transfers between devices with their start and end apart: 31 -> 31, of which waited for: 17 -> 17; matrix products, arithmetic and copies ran while one was open for 5% -> 5% of each run, Pallas kernels for 29% -> 30%
where the time goes in v6:
time: 180 us; the launch traced here: 179 us
  Pallas kernels  63.6 us (35%)
  starting transfers between devices  46.3 us (26%)
  waiting for transfers between devices  39.6 us (22%)
  between operations  15.2 us (8%)
  local copies, waits for them, and re-layouts  7.35 us (4%)
  other arithmetic  6.47 us (4%)
    pallas_call x2, Pallas kernels, attend(): pl.pallas_call(functools.partial(attend_body, heads=len(queries), parts=l...  35 us
    ppermute x4, starting transfers between devices, per_device(): far = {step: lax.ppermute(near[step], 'head', core_swap) for step in order}  20.5 us
    pallas_call x3, Pallas kernels, project(): pl.pallas_call(functools.partial(project_body, pieces=len(pieces)), grid_...  18.9 us
    ppermute x4, waiting for transfers between devices, per_device(): lax.ppermute(message, pair, traded(step))  12.1 us
    ppermute x4, starting transfers between devices, per_device(): lax.ppermute(message, pair, traded(step))  7.36 us
    ppermute x1, waiting for transfers between devices, per_device(): ahead_lower = lax.ppermute(backward, 'head', x_shift(3))  7.11 us
    all_gather x1, waiting for transfers between devices, per_device(): fifth = lax.all_gather(fifth, 'seq', axis=1, tiled=True)  5.52 us
    pallas_call x1, Pallas kernels, finish(): pl.pallas_call(finish_body, grid_spec=pltpu.PrefetchScalarGridSpec(num_sc...  5.04 us
  transfers between devices with their start and end apart: 31, of which 17 were waited for; matrix products, arithmetic and copies ran while one was open for 5% of the time, Pallas kernels for 30%

profile of v6, /device:TPU:0, one launch (start us, length us, event | category | flops | bytes accessed | tf_op | source)
XLA Modules:
  0.0 179.2 jit_solution(5533819758697296890)
XLA Ops:
  9.7 4.7 %shard_map.131 = (bf16[3,768,128]{2,1,0:T(8,128)(2,1)}, bf16[3,768,128]{2,1,0:T(8,128)(2,1)}, bf16[3,768,128]{2,1,0:T(8,128)(2,1)}, bf16[3,768,128]{2,1,0:T(8,128)(2,1)}) custom-call(s32[4]{0:T(128)} %pad_add_fusion.place, bf16[768,640]{1,0:T(8,128)(2,1)} %bitcast.49, bf16[768,640]{1,0:T(8,128)(2,1)} %bitcast.52, bf16[768,640]{1,0:T(8,128)(2,1)} %bitcast.54), custom_call_target="tpu_custom_call" | custom-call | tf_op jit(solution)/shard_map/pallas_call | solution.py:64
  14.4 2.3 %constant_dynamic-slice_fusion = bf16[640,2560]{1,0:T(8,128)(2,1)S(1)} fusion(bf16[640,5120]{1,0:T(8,128)(2,1)} %refs_40_.1, s32[]{:T(128)S(6)} %select_n.43), kind=kLoop, calls=%fused_computation.35 | loop fusion | bytes 6553604 | tf_op jit(solution)/shard_map/dynamic_slice | solution.py:326
  17.5 2.1 %collective-permute-start.1 = (bf16[3,768,128]{2,1,0:T(8,128)(2,1)S(1)}, bf16[3,768,128]{2,1,0:T(8,128)(2,1)S(1)}, u32[]{:S(2)}, u32[]{:S(2)}) collective-permute-start(bf16[3,768,128]{2,1,0:T(8,128)(2,1)S(1)} %copy-done.29), channel_id=1, source_target_pairs={{0,16},{1,24},{2,18},{3,26},{4,20},{5,28},{6,22},{7,30},{8,17},{9,... | collective-permute-start | bytes 1769480 | tf_op jit(solution)/shard_map/ppermute | solution.py:323
  19.6 3.6 %collective-permute-start.2 = (bf16[3,768,128]{2,1,0:T(8,128)(2,1)S(1)}, bf16[3,768,128]{2,1,0:T(8,128)(2,1)S(1)}, u32[]{:S(2)}, u32[]{:S(2)}) collective-permute-start(bf16[3,768,128]{2,1,0:T(8,128)(2,1)S(1)} %copy-done.28), channel_id=1, source_target_pairs={{0,32},{1,40},{2,34},{3,42},{4,36},{5,44},{6,38},{7,46},{8,33},{9,... | collective-permute-start | bytes 1769480 | tf_op jit(solution)/shard_map/ppermute | solution.py:323
  24.2 10.3 %collective-permute-start.4 = (bf16[3,768,128]{2,1,0:T(8,128)(2,1)S(1)}, bf16[3,768,128]{2,1,0:T(8,128)(2,1)S(1)}, u32[]{:S(2)}, u32[]{:S(2)}) collective-permute-start(bf16[3,768,128]{2,1,0:T(8,128)(2,1)S(1)} %collective-permute-done.refs_3_.refs_7_.refs_15_), channel_id=1, source_target_pairs={{0,1},{1,0},{2,3},{3,2},{4,5},{5,4},{6,7},{7,6},{8,9},{9,8},{10,11... | collective-permute-start | bytes 1769480 | tf_op jit(solution)/shard_map/ppermute | solution.py:328
  34.5 9.7 %collective-permute-start.5 = (bf16[3,768,128]{2,1,0:T(8,128)(2,1)S(1)}, bf16[3,768,128]{2,1,0:T(8,128)(2,1)S(1)}, u32[]{:S(2)}, u32[]{:S(2)}) collective-permute-start(bf16[3,768,128]{2,1,0:T(8,128)(2,1)S(1)} %collective-permute-done.1.refs_0_.refs_4_.refs_12_), channel_id=1, source_target_pairs={{0,1},{1,0},{2,3},{3,2},{4,5},{5,4},{6,7},{7,6},{8,9},{9,8},{10,11... | collective-permute-start | bytes 1769480 | tf_op jit(solution)/shard_map/ppermute | solution.py:328
  44.3 12.1 %collective-permute-done.2.refs_2_.refs_6_.refs_14_ = bf16[3,768,128]{2,1,0:T(8,128)(2,1)S(1)} collective-permute-done((bf16[3,768,128]{2,1,0:T(8,128)(2,1)S(1)}, bf16[3,768,128]{2,1,0:T(8,128)(2,1)S(1)}, u32[]{:S(2)}, u32[]{:S(2)}) %collective-permute-start.2) | collective-permute-done | bytes 589856 | tf_op jit(solution)/shard_map/ppermute | solution.py:323
  60.1 26.1 %shard_map.132 = (bf16[768,128]{1,0:T(8,128)(2,1)}, bf16[768,128]{1,0:T(8,128)(2,1)}, bf16[768,128]{1,0:T(8,128)(2,1)}, bf16[768,128]{1,0:T(8,128)(2,1)}) custom-call(bf16[3,768,128]{2,1,0:T(8,128)(2,1)} %copy-done.11, bf16[3,768,128]{2,1,0:T(8,128)(2,1)} %copy-done.13, bf16[3,768,128]{2,1,0:T(8,128)(2,1)} %copy-done.12, bf16[3,768,128]{2,1,0:T(8,128)(2,1)} %copy-done.10, ...), custom_call_target="tpu_custom_call" | custom-call | flops 1000 | bytes 1000 | tf_op jit(solution)/shard_map/pallas_call | solution.py:141
  88.4 1.6 collective-permute-start.9
  90.0 5.5 %all-gather.2.cloned.1.call-done.refs_1_.refs_2_ = bf16[2,6144,128]{2,1,0:T(8,128)(2,1)} async-done(((bf16[2,768,128]{2,1,0:T(8,128)(2,1)}), bf16[2,6144,128]{2,1,0:T(8,128)(2,1)}) %all-gather.2.cloned.1.call-update) | async-done | bytes 3145744 | tf_op jit(solution)/shard_map/all_gather | solution.py:318
  95.5 8.9 %shard_map.133.refs_4_.refs_14_.refs_24_.refs_34_ = bf16[768,128]{1,0:T(8,128)(2,1)} custom-call(bf16[768,640]{1,0:T(8,128)(2,1)} %bitcast.50, bf16[2,6144,128]{2,1,0:T(8,128)(2,1)} %all-gather.2.cloned.1.call-done.refs_1_.refs_2_, bf16[2,6144,128]{2,1,0:T(8,128)(2,1)} %all-gather.2.cloned.1.call-done.refs_1_.refs_2_), custom_call_target="tpu_custom_call" | custom-call | flops 1000 | bytes 1000 | tf_op jit(solution)/shard_map/pallas_call | solution.py:141
  108.2 5.6 %shard_map.134 = (bf16[96,2560]{1,0:T(8,128)(2,1)}, bf16[96,2560]{1,0:T(8,128)(2,1)}) custom-call(s32[4]{0:T(128)} %pad_add_fusion.place, bf16[768,128]{1,0:T(8,128)(2,1)} %copy-done.4, bf16[768,128]{1,0:T(8,128)(2,1)} %copy-done.1, bf16[768,128]{1,0:T(8,128)(2,1)} %copy-done.2, bf16[768,128]{1,0:T(8,128)(2,1)} %copy-done.3, ...), custom_call_target="tpu_custom_call" | custom-call | flops 1000 | bytes 1000 | tf_op jit(solution)/shard_map/pallas_call | solution.py:188
  113.7 2.9 %collective-permute-start.22 = (bf16[96,2560]{1,0:T(8,128)(2,1)}, bf16[96,2560]{1,0:T(8,128)(2,1)S(1)}, u32[]{:S(2)}, u32[]{:S(2)}) collective-permute-start(bf16[96,2560]{1,0:T(8,128)(2,1)} %get-tuple-element.97), channel_id=1, source_target_pairs={{0,6},{1,7},{2,0},{3,1},{4,2},{5,3},{6,4},{7,5},{8,14},{9,15},{10,... | collective-permute-start | bytes 1474568 | tf_op jit(solution)/shard_map/ppermute | solution.py:351
  116.6 5.6 %shard_map.135 = (bf16[96,2560]{1,0:T(8,128)(2,1)}, bf16[96,2560]{1,0:T(8,128)(2,1)}) custom-call(s32[4]{0:T(128)} %pad_add_fusion.place, bf16[768,128]{1,0:T(8,128)(2,1)} %copy-done.4, bf16[768,128]{1,0:T(8,128)(2,1)} %copy-done.1, bf16[768,128]{1,0:T(8,128)(2,1)} %copy-done.2, bf16[768,128]{1,0:T(8,128)(2,1)} %copy-done.3, ...), custom_call_target="tpu_custom_call" | custom-call | flops 1000 | bytes 1000 | tf_op jit(solution)/shard_map/pallas_call | solution.py:188
  122.9 2.9 %collective-permute-start.21 = (bf16[96,2560]{1,0:T(8,128)(2,1)}, bf16[96,2560]{1,0:T(8,128)(2,1)S(1)}, u32[]{:S(2)}, u32[]{:S(2)}) collective-permute-start(bf16[96,2560]{1,0:T(8,128)(2,1)} %get-tuple-element.122), channel_id=1, source_target_pairs={{0,6},{1,7},{2,0},{3,1},{4,2},{5,3},{6,4},{7,5},{8,14},{9,15},{10,... | collective-permute-start | bytes 1474568 | tf_op jit(solution)/shard_map/ppermute | solution.py:357
  125.8 7.8 %shard_map.136 = (f32[96,2560]{1,0:T(8,128)}, f32[96,2560]{1,0:T(8,128)}, f32[96,2560]{1,0:T(8,128)}, f32[96,2560]{1,0:T(8,128)}) custom-call(s32[4]{0:T(128)} %pad_add_fusion.place, bf16[768,128]{1,0:T(8,128)(2,1)} %copy-done.4, bf16[768,128]{1,0:T(8,128)(2,1)} %copy-done.1, bf16[768,128]{1,0:T(8,128)(2,1)} %copy-done.2, bf16[768,128]{1,0:T(8,128)(2,1)} %copy-done.3, ...), custom_call_target="tpu_custom_call" | custom-call | flops 1000 | bytes 1000 | tf_op jit(solution)/shard_map/pallas_call | solution.py:188
  135.0 1.8 %collective-permute-start.23 = (bf16[96,2560]{1,0:T(8,128)(2,1)S(1)}, bf16[96,2560]{1,0:T(8,128)(2,1)S(1)}, u32[]{:S(2)}, u32[]{:S(2)}) collective-permute-start(bf16[96,2560]{1,0:T(8,128)(2,1)S(1)} %add_convert_fusion), channel_id=1, source_target_pairs={{0,6},{1,7},{2,0},{3,1},{4,2},{5,3},{6,4},{7,5},{8,14},{9,15},{10,... | collective-permute-start | bytes 1474568 | tf_op jit(solution)/shard_map/ppermute | solution.py:365
  136.8 2.1 %add_convert_fusion.1 = bf16[96,2560]{1,0:T(8,128)(2,1)} fusion(f32[96,2560]{1,0:T(8,128)} %get-tuple-element.121, bf16[96,2560]{1,0:T(8,128)(2,1)S(1)} %collective-permute-done.18), kind=kLoop, calls=%fused_computation.1 | loop fusion | flops 737280 | bytes 1966080 | tf_op jit(solution)/shard_map/convert_element_type | solution.py:362
  141.7 7.1 %collective-permute-done.23.refs_5_ = bf16[96,2560]{1,0:T(8,128)(2,1)S(1)} collective-permute-done((bf16[96,2560]{1,0:T(8,128)(2,1)S(1)}, bf16[96,2560]{1,0:T(8,128)(2,1)S(1)}, u32[]{:S(2)}, u32[]{:S(2)}) %collective-permute-start.23) | collective-permute-done | bytes 491552 | tf_op jit(solution)/shard_map/ppermute | solution.py:365
  148.8 3.5 %collective-permute-done.19.refs_2_ = bf16[96,2560]{1,0:T(8,128)(2,1)S(1)} collective-permute-done((bf16[96,2560]{1,0:T(8,128)(2,1)}, bf16[96,2560]{1,0:T(8,128)(2,1)S(1)}, u32[]{:S(2)}, u32[]{:S(2)}) %collective-permute-start.19) | collective-permute-done | bytes 491552 | tf_op jit(solution)/shard_map/ppermute | solution.py:364
  153.0 5.0 %shard_map.137 = (f32[40,192]{1,0:T(8,128)}, f32[40,192]{1,0:T(8,128)}) custom-call(s32[4]{0:T(128)} %pad_add_fusion.place, f32[96,2560]{1,0:T(8,128)} %get-tuple-element.119.refs_0_, f32[96,2560]{1,0:T(8,128)} %get-tuple-element.120.refs_1_, bf16[96,2560]{1,0:T(8,128)(2,1)} %copy-done.22, bf16[96,2560]{1,0:T(8,128)(2,1)} %copy-done.19, ...), custom_call_target="tpu_custom_call" | custom-call | flops 377487360 | bytes 5898240 | tf_op jit(solution)/shard_map/pallas_call | solution.py:263
  158.1 2.1 %collective-permute-start.24 = (f32[40,192]{1,0:T(8,128)}, f32[40,192]{1,0:T(8,128)S(1)}, u32[]{:S(2)}, u32[]{:S(2)}) collective-permute-start(f32[40,192]{1,0:T(8,128)} %get-tuple-element.124), channel_id=1, source_target_pairs={{0,64},{64,0},{1,65},{65,1},{2,66},{66,2},{3,67},{67,3},{4,68},{68... | collective-permute-start | bytes 92168 | tf_op jit(solution)/shard_map/ppermute | solution.py:372
  160.4 2.0 %collective-permute-done.24 = f32[40,192]{1,0:T(8,128)S(1)} collective-permute-done((f32[40,192]{1,0:T(8,128)}, f32[40,192]{1,0:T(8,128)S(1)}, u32[]{:S(2)}, u32[]{:S(2)}) %collective-permute-start.24) | collective-permute-done | bytes 30752 | tf_op jit(solution)/shard_map/ppermute | solution.py:372
  168.8 1.9 %collective-permute-done.28 = f32[32,192]{1,0:T(8,128)S(1)} collective-permute-done((f32[32,192]{1,0:T(8,128)S(1)}, f32[32,192]{1,0:T(8,128)S(1)}, u32[]{:S(2)}, u32[]{:S(2)}) %collective-permute-start.28) | collective-permute-done | bytes 24608 | tf_op jit(solution)/shard_map/ppermute | solution.py:391
  (124 shorter events, 26.9 us)
Async XLA Ops:
  7.2 88.4 %all-gather.2.cloned.1.call-start = ((), (), s32[]{:S(2)}) async-start(), calls=%async_computation | async-start | bytes 3538944 | tf_op jit(solution)/shard_map/all_gather | solution.py:318
  16.7 42.5 %collective-permute-start.8 = (bf16[640,2560]{1,0:T(8,128)(2,1)S(1)}, bf16[640,2560]{1,0:T(8,128)(2,1)S(1)}, u32[]{:S(2)}, u32[]{:S(2)}) collective-permute-start(bf16[640,2560]{1,0:T(8,128)(2,1)S(1)} %constant_dynamic-slice_fusion), channel_id=1, source_target_pairs={{0,1},{1,0},{2,3},{3,2},{4,5},{5,4},{6,7},{7,6},{8,9},{9,8},{10,11... | collective-permute-start | bytes 9830408 | tf_op jit(solution)/shard_map/ppermute | solution.py:325
  16.8 7.4 %collective-permute-start = (bf16[3,768,128]{2,1,0:T(8,128)(2,1)S(1)}, bf16[3,768,128]{2,1,0:T(8,128)(2,1)S(1)}, u32[]{:S(2)}, u32[]{:S(2)}) collective-permute-start(bf16[3,768,128]{2,1,0:T(8,128)(2,1)S(1)} %copy-done.30), channel_id=1, source_target_pairs={{0,0},{1,8},{2,2},{3,10},{4,4},{5,12},{6,6},{7,14},{8,1},{9,9},{10... | collective-permute-start | bytes 1769480 | tf_op jit(solution)/shard_map/ppermute | solution.py:323
  17.5 17.0 %collective-permute-start.1 = (bf16[3,768,128]{2,1,0:T(8,128)(2,1)S(1)}, bf16[3,768,128]{2,1,0:T(8,128)(2,1)S(1)}, u32[]{:S(2)}, u32[]{:S(2)}) collective-permute-start(bf16[3,768,128]{2,1,0:T(8,128)(2,1)S(1)} %copy-done.29), channel_id=1, source_target_pairs={{0,16},{1,24},{2,18},{3,26},{4,20},{5,28},{6,22},{7,30},{8,17},{9,... | collective-permute-start | bytes 1769480 | tf_op jit(solution)/shard_map/ppermute | solution.py:323
  19.6 36.8 %collective-permute-start.2 = (bf16[3,768,128]{2,1,0:T(8,128)(2,1)S(1)}, bf16[3,768,128]{2,1,0:T(8,128)(2,1)S(1)}, u32[]{:S(2)}, u32[]{:S(2)}) collective-permute-start(bf16[3,768,128]{2,1,0:T(8,128)(2,1)S(1)} %copy-done.28), channel_id=1, source_target_pairs={{0,32},{1,40},{2,34},{3,42},{4,36},{5,44},{6,38},{7,46},{8,33},{9,... | collective-permute-start | bytes 1769480 | tf_op jit(solution)/shard_map/ppermute | solution.py:323
  23.2 33.2 %collective-permute-start.3 = (bf16[3,768,128]{2,1,0:T(8,128)(2,1)S(1)}, bf16[3,768,128]{2,1,0:T(8,128)(2,1)S(1)}, u32[]{:S(2)}, u32[]{:S(2)}) collective-permute-start(bf16[3,768,128]{2,1,0:T(8,128)(2,1)S(1)} %copy-done.27), channel_id=1, source_target_pairs={{0,48},{1,56},{2,50},{3,58},{4,52},{5,60},{6,54},{7,62},{8,49},{9,... | collective-permute-start | bytes 1769480 | tf_op jit(solution)/shard_map/ppermute | solution.py:323
  24.2 32.7 %collective-permute-start.4 = (bf16[3,768,128]{2,1,0:T(8,128)(2,1)S(1)}, bf16[3,768,128]{2,1,0:T(8,128)(2,1)S(1)}, u32[]{:S(2)}, u32[]{:S(2)}) collective-permute-start(bf16[3,768,128]{2,1,0:T(8,128)(2,1)S(1)} %collective-permute-done.refs_3_.refs_7_.refs_15_), channel_id=1, source_target_pairs={{0,1},{1,0},{2,3},{3,2},{4,5},{5,4},{6,7},{7,6},{8,9},{9,8},{10,11... | collective-permute-start | bytes 1769480 | tf_op jit(solution)/shard_map/ppermute | solution.py:328
  34.5 22.4 %collective-permute-start.5 = (bf16[3,768,128]{2,1,0:T(8,128)(2,1)S(1)}, bf16[3,768,128]{2,1,0:T(8,128)(2,1)S(1)}, u32[]{:S(2)}, u32[]{:S(2)}) collective-permute-start(bf16[3,768,128]{2,1,0:T(8,128)(2,1)S(1)} %collective-permute-done.1.refs_0_.refs_4_.refs_12_), channel_id=1, source_target_pairs={{0,1},{1,0},{2,3},{3,2},{4,5},{5,4},{6,7},{7,6},{8,9},{9,8},{10,11... | collective-permute-start | bytes 1769480 | tf_op jit(solution)/shard_map/ppermute | solution.py:328
  86.1 18.3 %collective-permute-start.10 = (bf16[768,128]{1,0:T(8,128)(2,1)}, bf16[768,128]{1,0:T(8,128)(2,1)S(1)}, u32[]{:S(2)}, u32[]{:S(2)}) collective-permute-start(bf16[768,128]{1,0:T(8,128)(2,1)} %get-tuple-element.86), channel_id=1, source_target_pairs={{0,48},{1,56},{2,50},{3,58},{4,52},{5,60},{6,54},{7,62},{8,49},{9,... | collective-permute-start | bytes 589832 | tf_op jit(solution)/shard_map/ppermute | solution.py:337
  87.5 16.9 %collective-permute-start.11 = (bf16[768,128]{1,0:T(8,128)(2,1)}, bf16[768,128]{1,0:T(8,128)(2,1)S(1)}, u32[]{:S(2)}, u32[]{:S(2)}) collective-permute-start(bf16[768,128]{1,0:T(8,128)(2,1)} %get-tuple-element.87), channel_id=1, source_target_pairs={{0,32},{1,40},{2,34},{3,42},{4,36},{5,44},{6,38},{7,46},{8,33},{9,... | collective-permute-start | bytes 589832 | tf_op jit(solution)/shard_map/ppermute | solution.py:337
  88.4 16.1 %collective-permute-start.12 = (bf16[768,128]{1,0:T(8,128)(2,1)}, bf16[768,128]{1,0:T(8,128)(2,1)S(1)}, u32[]{:S(2)}, u32[]{:S(2)}) collective-permute-start(bf16[768,128]{1,0:T(8,128)(2,1)} %get-tuple-element.88), channel_id=1, source_target_pairs={{0,16},{1,24},{2,18},{3,26},{4,20},{5,28},{6,22},{7,30},{8,17},{9,... | collective-permute-start | bytes 589832 | tf_op jit(solution)/shard_map/ppermute | solution.py:337
  88.4 16.0 %collective-permute-start.9 = (bf16[768,128]{1,0:T(8,128)(2,1)}, bf16[768,128]{1,0:T(8,128)(2,1)S(1)}, u32[]{:S(2)}, u32[]{:S(2)}) collective-permute-start(bf16[768,128]{1,0:T(8,128)(2,1)} %get-tuple-element.85), channel_id=1, source_target_pairs={{0,0},{1,8},{2,2},{3,10},{4,4},{5,12},{6,6},{7,14},{8,1},{9,9},{10... | collective-permute-start | bytes 589832 | tf_op jit(solution)/shard_map/ppermute | solution.py:337
  113.7 19.9 %collective-permute-start.22 = (bf16[96,2560]{1,0:T(8,128)(2,1)}, bf16[96,2560]{1,0:T(8,128)(2,1)S(1)}, u32[]{:S(2)}, u32[]{:S(2)}) collective-permute-start(bf16[96,2560]{1,0:T(8,128)(2,1)} %get-tuple-element.97), channel_id=1, source_target_pairs={{0,6},{1,7},{2,0},{3,1},{4,2},{5,3},{6,4},{7,5},{8,14},{9,15},{10,... | collective-permute-start | bytes 1474568 | tf_op jit(solution)/shard_map/ppermute | solution.py:351
  116.6 20.2 %collective-permute-start.18 = (bf16[96,2560]{1,0:T(8,128)(2,1)}, bf16[96,2560]{1,0:T(8,128)(2,1)S(1)}, u32[]{:S(2)}, u32[]{:S(2)}) collective-permute-start(bf16[96,2560]{1,0:T(8,128)(2,1)} %get-tuple-element.96), channel_id=1, source_target_pairs={{0,2},{1,3},{2,4},{3,5},{4,6},{5,7},{6,0},{7,1},{8,10},{9,11},{10,... | collective-permute-start | bytes 1474568 | tf_op jit(solution)/shard_map/ppermute | solution.py:350
  122.2 19.4 %collective-permute-start.20 = (bf16[96,2560]{1,0:T(8,128)(2,1)}, bf16[96,2560]{1,0:T(8,128)(2,1)S(1)}, u32[]{:S(2)}, u32[]{:S(2)}) collective-permute-start(bf16[96,2560]{1,0:T(8,128)(2,1)} %get-tuple-element.108), channel_id=1, source_target_pairs={{0,2},{1,3},{2,4},{3,5},{4,6},{5,7},{6,0},{7,1},{8,10},{9,11},{10,... | collective-permute-start | bytes 1474568 | tf_op jit(solution)/shard_map/ppermute | solution.py:356
  122.9 18.7 %collective-permute-start.21 = (bf16[96,2560]{1,0:T(8,128)(2,1)}, bf16[96,2560]{1,0:T(8,128)(2,1)S(1)}, u32[]{:S(2)}, u32[]{:S(2)}) collective-permute-start(bf16[96,2560]{1,0:T(8,128)(2,1)} %get-tuple-element.122), channel_id=1, source_target_pairs={{0,6},{1,7},{2,0},{3,1},{4,2},{5,3},{6,4},{7,5},{8,14},{9,15},{10,... | collective-permute-start | bytes 1474568 | tf_op jit(solution)/shard_map/ppermute | solution.py:357
  135.0 13.8 %collective-permute-start.23 = (bf16[96,2560]{1,0:T(8,128)(2,1)S(1)}, bf16[96,2560]{1,0:T(8,128)(2,1)S(1)}, u32[]{:S(2)}, u32[]{:S(2)}) collective-permute-start(bf16[96,2560]{1,0:T(8,128)(2,1)S(1)} %add_convert_fusion), channel_id=1, source_target_pairs={{0,6},{1,7},{2,0},{3,1},{4,2},{5,3},{6,4},{7,5},{8,14},{9,15},{10,... | collective-permute-start | bytes 1474568 | tf_op jit(solution)/shard_map/ppermute | solution.py:365
  138.9 13.4 %collective-permute-start.19 = (bf16[96,2560]{1,0:T(8,128)(2,1)}, bf16[96,2560]{1,0:T(8,128)(2,1)S(1)}, u32[]{:S(2)}, u32[]{:S(2)}) collective-permute-start(bf16[96,2560]{1,0:T(8,128)(2,1)} %add_convert_fusion.1), channel_id=1, source_target_pairs={{0,2},{1,3},{2,4},{3,5},{4,6},{5,7},{6,0},{7,1},{8,10},{9,11},{10,... | collective-permute-start | bytes 1474568 | tf_op jit(solution)/shard_map/ppermute | solution.py:364
  158.1 4.3 %collective-permute-start.24 = (f32[40,192]{1,0:T(8,128)}, f32[40,192]{1,0:T(8,128)S(1)}, u32[]{:S(2)}, u32[]{:S(2)}) collective-permute-start(f32[40,192]{1,0:T(8,128)} %get-tuple-element.124), channel_id=1, source_target_pairs={{0,64},{64,0},{1,65},{65,1},{2,66},{66,2},{3,67},{67,3},{4,68},{68... | collective-permute-start | bytes 92168 | tf_op jit(solution)/shard_map/ppermute | solution.py:372
  160.2 3.6 %collective-permute-start.25 = (f32[40,192]{1,0:T(8,128)}, f32[40,192]{1,0:T(8,128)S(1)}, u32[]{:S(2)}, u32[]{:S(2)}) collective-permute-start(f32[40,192]{1,0:T(8,128)} %get-tuple-element.124), channel_id=1, source_target_pairs={{0,65},{1,64},{2,67},{3,66},{4,69},{5,68},{6,71},{7,70},{64,1},{65... | collective-permute-start | bytes 92168 | tf_op jit(solution)/shard_map/ppermute | solution.py:372
  160.2 3.6 %collective-permute-start.26 = (f32[40,192]{1,0:T(8,128)}, f32[40,192]{1,0:T(8,128)S(1)}, u32[]{:S(2)}, u32[]{:S(2)}) collective-permute-start(f32[40,192]{1,0:T(8,128)} %get-tuple-element.125), channel_id=1, source_target_pairs={{0,1},{1,0},{2,3},{3,2},{4,5},{5,4},{6,7},{7,6},{8,9},{9,8},{10,11... | collective-permute-start | bytes 92168 | tf_op jit(solution)/shard_map/ppermute | solution.py:371
  164.8 4.0 %collective-permute-start.27 = (f32[32,192]{1,0:T(8,128)S(1)}, f32[32,192]{1,0:T(8,128)S(1)}, u32[]{:S(2)}, u32[]{:S(2)}) collective-permute-start(f32[32,192]{1,0:T(8,128)S(1)} %fusion.10), channel_id=1, source_target_pairs={{0,6},{1,7},{2,0},{3,1},{4,2},{5,3},{6,4},{7,5},{8,14},{9,15},{10,... | collective-permute-start | bytes 73736 | tf_op jit(solution)/shard_map/ppermute | solution.py:391
  165.2 5.4 %collective-permute-start.28 = (f32[32,192]{1,0:T(8,128)S(1)}, f32[32,192]{1,0:T(8,128)S(1)}, u32[]{:S(2)}, u32[]{:S(2)}) collective-permute-start(f32[32,192]{1,0:T(8,128)S(1)} %fusion.10), channel_id=1, source_target_pairs={{0,4},{1,5},{2,6},{3,7},{4,0},{5,1},{6,2},{7,3},{8,12},{9,13},{10,... | collective-permute-start | bytes 73736 | tf_op jit(solution)/shard_map/ppermute | solution.py:391
  166.3 5.2 %collective-permute-start.29 = (f32[32,192]{1,0:T(8,128)S(1)}, f32[32,192]{1,0:T(8,128)S(1)}, u32[]{:S(2)}, u32[]{:S(2)}) collective-permute-start(f32[32,192]{1,0:T(8,128)S(1)} %fusion.10), channel_id=1, source_target_pairs={{0,2},{1,3},{2,4},{3,5},{4,6},{5,7},{6,0},{7,1},{8,10},{9,11},{10,... | collective-permute-start | bytes 73736 | tf_op jit(solution)/shard_map/ppermute | solution.py:391
  (38 other events, 228.2 us)
Sparse Core Ops, SparseCore 0:
  10.3 85.1 all-gather.1
